TPU v7x, 256 devices: a whole 4x4x8 slice. The times are simulated.
256 devices in a mesh: seq: 256 (over y, x, z, core).
Axes of the slice: x: 4, y: 4, z: 8, core: 2. Of those that a mesh axis runs over, the one named last changes fastest.
Arguments:
- query_rows: bfloat16 [65536, 1024], P('seq'), may hold values from -16 to 16
- key_rows: bfloat16 [65536, 1024], P('seq'), may hold values from -16 to 16
- value_rows: bfloat16 [65536, 1024], P('seq'), may hold values from -6 to 6
Outputs:
- attended: bfloat16 [65536, 1024], P('seq')
All inputs are finite; a program needn't handle non-finite values.
Results may differ from a plain program's by a relative error of at most 0.012.
The roundings to bfloat16 on the way count: a program that leaves them out, or rounds other values in their place, can miss the bound.
Values may be sent and summed in bfloat16 or wider, within the bound.
No kernel may reach another device: no remote copies, remote signals or barrier semaphores. Data moves between devices by JAX's collectives and lax.ppermute only.
A program may use at most 64 MiB of HBM per device.

v0:
```python
import functools
import math

import jax
import jax.numpy as jnp
from jax import lax
from jax.experimental import pallas as pl
from jax.experimental.pallas import tpu as pltpu
from jax.sharding import PartitionSpec as P

HEADS = 4
DH = 128
COLS = HEADS * DH
B = 256
PACK = COLS + 128
ABSENT = -1e30
SCALE = math.log2(math.e) / math.sqrt(DH)
F32 = jnp.float32
BF16 = jnp.bfloat16

CHIPS = 128
RING = 8
ROWS4, ROWS3 = 32, 64
SEND = 3 * ROWS4 + 2 * ROWS3
BACK = ROWS4 + ROWS3


def shaped(*shape):
    return jax.ShapeDtypeStruct(shape, BF16)


def call(body, outs, scalars, arrays, flops=0, size=0):
    return pl.pallas_call(
        body,
        out_shape=outs,
        in_specs=[pl.BlockSpec(memory_space=pltpu.SMEM)]
        + [pl.BlockSpec(memory_space=pltpu.VMEM)] * len(arrays),
        out_specs=jax.tree.map(lambda _: pl.BlockSpec(memory_space=pltpu.VMEM), outs),
        compiler_params=pltpu.CompilerParams(vmem_limit_bytes=56 * 2**20),
        cost_estimate=pl.CostEstimate(flops=flops, bytes_accessed=size, transcendentals=0),
    )(scalars, *arrays)


def pool_matrix(rows, width, level, scale):
    row = lax.broadcasted_iota(jnp.int32, (rows, width), 0)
    col = lax.broadcasted_iota(jnp.int32, (rows, width), 1)
    return jnp.where((col >> level) == row, scale, 0.0).astype(BF16)


def spread_matrix(rows, width, level):
    row = lax.broadcasted_iota(jnp.int32, (rows, width), 0)
    col = lax.broadcasted_iota(jnp.int32, (rows, width), 1)
    return jnp.where((row >> level) == col, 1.0, 0.0).astype(BF16)


def pooled(x, level, mean):
    scale = 1.0 / 2**level if mean else 1.0
    matrix = pool_matrix(B >> level, B, level, scale)
    return jnp.dot(matrix, x, preferred_element_type=F32).astype(BF16)


def attend(q, parts, factor):
    scores = []
    for k, _, bias in parts:
        s = lax.dot_general(q, k, (((1,), (1,)), ((), ())), preferred_element_type=F32) * SCALE
        scores.append(s if bias is None else s + bias)
    m = functools.reduce(jnp.maximum, [jnp.max(s, axis=1, keepdims=True) for s in scores])
    total, out = None, None
    for s, (_, v, _) in zip(scores, parts):
        w = jnp.exp2(s - m)
        t = jnp.sum(w, axis=1, keepdims=True)
        o = jnp.dot(w.astype(BF16), v, preferred_element_type=F32)
        total = t if total is None else total + t
        out = o if out is None else out + o
    total = total * factor
    return (out / total).astype(BF16), m + jnp.log2(total)


def tile_of(values):
    rows = values[0].shape[0]
    lane = lax.broadcasted_iota(jnp.int32, (rows, 128), 1)
    full = jnp.zeros((rows, 128), F32)
    for h, value in enumerate(values):
        full = jnp.where((lane & 3) == h, value, full)
    high = full.astype(BF16)
    rest = full - high.astype(F32)
    middle = rest.astype(BF16)
    low = (rest - middle.astype(F32)).astype(BF16)
    zero = jnp.zeros((rows, 128), BF16)
    part = lane >> 2
    return jnp.where(part == 0, high, jnp.where(part == 1, middle, jnp.where(part == 2, low, zero)))


def attend_to(out_ref, row, q_of, parts_of, rows, factor):
    values = []
    for h in range(HEADS):
        cols = slice(h * DH, (h + 1) * DH)
        o, value = attend(q_of(cols), parts_of(cols), factor)
        out_ref[row : row + rows, cols] = o
        values.append(value)
    out_ref[row : row + rows, COLS:] = tile_of(values)


def pool_body(s, q, k, v, got, fine, rpay, lpay, q1, ppay, apay):
    core, half = s[0], s[1]
    levels = {}
    for n, ref in enumerate((q, k, v)):
        own = ref[...]
        other = got[n]
        for at in (0, 1):
            x = jnp.where(core == at, own, other)
            fine[n, at * B : (at + 1) * B] = x
            for level in (1, 2, 3, 4):
                levels[n, at, level] = pooled(x, level, n < 2)
            if n:
                to = rpay if at else lpay
                to[(n - 1) * B : n * B] = x
                to = lpay if at else rpay
                to[2 * B + (n - 1) * 128 : 2 * B + n * 128] = levels[n, at, 1]
    for at in (0, 1):
        q1[at * 128 : (at + 1) * 128] = levels[0, at, 1]
        for n in range(3):
            ppay[n * 128 + at * 64 : n * 128 + (at + 1) * 64] = levels[n, at, 2]
        for j in range(RING):
            cols = slice((j % HEADS) * DH, (j % HEADS + 1) * DH)
            for n in range(3):
                apay[j, n * ROWS4 + at * 16 : n * ROWS4 + (at + 1) * 16] = levels[n, at, 4][:, cols]
            first = jnp.where(
                half == j // HEADS, levels[0, at, 3][:, cols], levels[1, at, 3][:, cols]
            )
            base = 3 * ROWS4
            apay[j, base + at * 32 : base + (at + 1) * 32] = first
            base += ROWS3
            apay[j, base + at * 32 : base + (at + 1) * 32] = levels[2, at, 3][:, cols]


def near_body(s, fine, out):
    for at in (0, 1):
        rows = slice(at * B, (at + 1) * B)
        attend_to(
            out,
            at * B,
            lambda cols: fine[0, rows, cols],
            lambda cols: [(fine[1, :, cols], fine[2, :, cols], None)],
            B,
            1.0,
        )


def far_body(s, fine, q1, rin, lin, out0, out1):
    has_left, has_right = s[2], s[3]
    bias_left = jnp.where(has_left == 1, 0.0, ABSENT).astype(F32)
    bias_right = jnp.where(has_right == 1, 0.0, ABSENT).astype(F32)
    for at, ref, bias in ((0, rin, bias_left), (1, lin, bias_right)):
        attend_to(
            out0,
            at * B,
            lambda cols: fine[0, at * B : (at + 1) * B, cols],
            lambda cols: [(ref[:B, cols], ref[B : 2 * B, cols], bias)],
            B,
            1.0,
        )

    def coarse(cols):
        parts = []
        for ref, bias in ((rin, bias_left), (lin, bias_right)):
            keys = pooled(ref[:B, cols], 1, True)
            values = pooled(ref[B : 2 * B, cols], 1, False)
            parts.append((keys, values, bias))
            parts.append((ref[2 * B : 2 * B + 128, cols], ref[2 * B + 128 :, cols], bias))
        return parts

    attend_to(out1, 0, lambda cols: q1[:, cols], coarse, B, 2.0)


def pair_body(s, ppay, pin, bin_, out):
    bias = jnp.where(s[4] == 1, 0.0, ABSENT).astype(F32)
    for row, ref in ((0, ppay), (128, pin)):
        attend_to(
            out,
            row,
            lambda cols: ref[:128, cols],
            lambda cols: [
                (bin_[:128, cols], bin_[128:256, cols], bias),
                (bin_[256:384, cols], bin_[384:, cols], bias),
            ],
            128,
            4.0,
        )


def row_pay_body(s, ain, xpay):
    other = (1 - s[1]) * HEADS
    for j in range(RING):
        xpay[j * ROWS4 : (j + 1) * ROWS4] = ain[j, ROWS4 : 2 * ROWS4]
        xpay[B + j * ROWS4 : B + (j + 1) * ROWS4] = ain[j, 2 * ROWS4 : 3 * ROWS4]
    for j in range(HEADS):
        for n in (0, 1):
            base = 3 * ROWS4 + n * ROWS3
            to = (2 + n) * B + j * ROWS3
            xpay[to : to + ROWS3] = ain[other + j, base : base + ROWS3]


def row_body(s, ain, xin, back):
    half, head = s[1], s[5]
    bias = jnp.where(s[6] == 1, 0.0, ABSENT).astype(F32)
    mine, other = half * HEADS, (1 - half) * HEADS
    base = 3 * ROWS4
    rows3 = lambda at, low: jnp.concatenate(
        [ain[at + j, low : low + ROWS3] for j in range(HEADS)], axis=0
    )
    lane = lax.broadcasted_iota(jnp.int32, (B, 128), 1)

    def tile(value):
        high = value.astype(BF16)
        rest = value - high.astype(F32)
        middle = rest.astype(BF16)
        low = (rest - middle.astype(F32)).astype(BF16)
        zero = jnp.zeros((B, 128), F32)
        picked = jnp.where(
            lane == head,
            high.astype(F32),
            jnp.where(
                lane == head + 4,
                middle.astype(F32),
                jnp.where(lane == head + 8, low.astype(F32), zero),
            ),
        )
        return picked.astype(BF16)

    q4 = jnp.concatenate([ain[j, :ROWS4] for j in range(RING)], axis=0)
    o4, value4 = attend(q4, [(xin[:B], xin[B : 2 * B], bias)], 16.0)
    t4 = tile(value4)
    for j in range(RING):
        rows = slice(j * ROWS4, (j + 1) * ROWS4)
        back[j, :ROWS4, :DH] = o4[rows]
        back[j, :ROWS4, DH:] = t4[rows]
    o3, value3 = attend(
        rows3(mine, base),
        [
            (rows3(other, base), rows3(other, base + ROWS3), None),
            (xin[2 * B : 3 * B], xin[3 * B :], bias),
        ],
        8.0,
    )
    t3 = tile(value3)
    for j in range(RING):
        rows = slice((j % HEADS) * ROWS3, (j % HEADS + 1) * ROWS3)
        back[j, ROWS4:, :DH] = o3[rows]
        back[j, ROWS4:, DH:] = t3[rows]


def merge_body(s, near, far, one, two, two_back, row_back, mine, send):
    core, half = s[0], s[1]
    low = half * HEADS
    four = []
    for side in (0, 1):
        o = [row_back[side * HEADS + g, :ROWS4, :DH] for g in range(HEADS)]
        t = [row_back[side * HEADS + g, :ROWS4, DH:].astype(F32) for g in range(HEADS)]
        four.append(jnp.concatenate(o + [(t[0] + t[1] + t[2] + t[3]).astype(BF16)], axis=1))
    o = [row_back[low + g, ROWS4:, :DH] for g in range(HEADS)]
    t = [row_back[low + g, ROWS4:, DH:].astype(F32) for g in range(HEADS)]
    three = jnp.concatenate(o + [(t[0] + t[1] + t[2] + t[3]).astype(BF16)], axis=1)
    for at in (0, 1):
        terms = [near[at * B : (at + 1) * B].astype(F32), far[at * B : (at + 1) * B].astype(F32)]
        for level, values in (
            (1, one[at * 128 : (at + 1) * 128]),
            (2, two[at * 64 : (at + 1) * 64]),
            (2, two_back[at * 64 : (at + 1) * 64]),
            (3, three[at * 32 : (at + 1) * 32]),
            (4, four[0][at * 16 : (at + 1) * 16]),
            (4, four[1][at * 16 : (at + 1) * 16]),
        ):
            spread = spread_matrix(B, B >> level, level)
            terms.append(jnp.dot(spread, values, preferred_element_type=F32))
        weights = []
        for term in terms:
            t = term[:, COLS:]
            weights.append(t + pltpu.roll(t, 128 - 4, 1) + pltpu.roll(t, 128 - 8, 1))
        top = functools.reduce(jnp.maximum, weights)
        weights = [jnp.exp2(t - top) for t in weights]
        inverse = 1.0 / functools.reduce(jnp.add, weights)
        weights = [t * inverse for t in weights]
        for h in range(HEADS):
            cols = slice(h * DH, (h + 1) * DH)
            total = None
            for term, t in zip(terms, weights):
                part = term[:, cols] * t[:, h : h + 1]
                total = part if total is None else total + part
            total = total.astype(BF16)

            @pl.when(core == at)
            def _():
                mine[:, cols] = total

            @pl.when(core != at)
            def _():
                send[:, cols] = total


def pairs_of(target):
    pairs = []
    for chip in range(CHIPS):
        to = target(chip)
        if 0 <= to < CHIPS:
            pairs += [(2 * chip + core, 2 * to + core) for core in (0, 1)]
    return pairs


SWAP = [(i, i ^ 1) for i in range(2 * CHIPS)]
RIGHT = pairs_of(lambda chip: chip + 1)
LEFT = pairs_of(lambda chip: chip - 1)
PAIR = pairs_of(lambda chip: chip ^ 1)
BOUND = pairs_of(lambda chip: chip + 1 if chip % 2 else chip - 1)
ROW = pairs_of(lambda chip: chip + RING if chip % RING < RING // 2 else chip - RING)
LINES = [
    [2 * (row * RING + z) + core for z in range(RING)]
    for row in range(CHIPS // RING)
    for core in (0, 1)
]


def send_to(x, pairs):
    return lax.ppermute(x, "seq", pairs)


def line_swap(x):
    return lax.all_to_all(x, "seq", 0, 0, axis_index_groups=LINES)


def local(query_rows, key_rows, value_rows):
    position = lax.axis_index("seq")
    core = position % 2
    chip = position // 2
    z = chip % RING
    row = chip // RING
    half = z // HEADS
    odd = chip % 2
    has_left = chip >= 1
    has_right = chip <= CHIPS - 2
    has_pair = jnp.where(odd == 1, chip <= CHIPS - 3, chip >= 2)
    has_row = jnp.where(half == 0, row >= 1, row <= CHIPS // RING - 2)
    s = jnp.stack(
        [core, half, has_left, has_right, has_pair, z % HEADS, has_row, odd]
    ).astype(jnp.int32)

    arrays = (query_rows, key_rows, value_rows)
    outgoing = jnp.stack([lax.dynamic_slice(x, (0, (1 - core) * COLS), (B, COLS)) for x in arrays])
    own = [lax.dynamic_slice(x, (0, core * COLS), (B, COLS)) for x in arrays]
    got = send_to(outgoing, SWAP)
    fine, rpay, lpay, q1, ppay, apay = call(
        pool_body,
        (
            shaped(3, 2 * B, COLS),
            shaped(3 * B, COLS),
            shaped(3 * B, COLS),
            shaped(B, COLS),
            shaped(384, COLS),
            shaped(RING, SEND, DH),
        ),
        s,
        (*own, got),
    )
    pin = send_to(ppay, PAIR)
    ain = line_swap(apay)
    rin = send_to(rpay, RIGHT)
    lin = send_to(lpay, LEFT)
    near = call(near_body, shaped(2 * B, PACK), s, (fine,), 2**28, 2**21)
    bin_ = send_to(jnp.concatenate([ppay[128:], pin[128:]]), BOUND)
    xin = send_to(call(row_pay_body, shaped(4 * B, DH), s, (ain,)), ROW)
    two = call(pair_body, shaped(B, PACK), s, (ppay, pin, bin_), 2**26, 2**20)
    two_back = send_to(two[128:], PAIR)
    row_back = line_swap(call(row_body, shaped(RING, BACK, 2 * DH), s, (ain, xin), 2**26, 2**20))
    far, one = call(
        far_body, (shaped(2 * B, PACK), shaped(B, PACK)), s, (fine, q1, rin, lin), 2**28, 2**21
    )
    mine, send = call(
        merge_body,
        (shaped(B, COLS), shaped(B, COLS)),
        s,
        (near, far, one, two[:128], two_back, row_back),
        2**26,
        2**21,
    )
    theirs = send_to(send, SWAP)
    return jnp.where(
        core == 0,
        jnp.concatenate([mine, theirs], axis=1),
        jnp.concatenate([theirs, mine], axis=1),
    )


def solution(mesh):
    spec = P("seq", None)
    return jax.shard_map(
        local, mesh=mesh, in_specs=(spec, spec, spec), out_specs=spec, check_vma=False
    )
```

profile of v0, /device:TPU:29, one launch (start us, length us, event | category | flops | bytes accessed | tf_op | source)
XLA Modules:
  0.0 120.1 jit_solution(13482904524109103126)
XLA Ops:
  0.0 1.8 %dynamic-slice_bitcast_fusion.2 = (bf16[1,256,512]{2,1,0:T(8,128)(2,1)S(1)}, bf16[256,512]{1,0:T(8,128)(2,1)}) fusion(bf16[256,1024]{1,0:T(8,128)(2,1)} %param.3, s32[]{:T(128)S(6)} %select_n.65, s32[]{:T(128)S(6)} %select_n.64), kind=kLoop, calls=%fused_computation.5 | loop fusion | bytes 1048584 | tf_op jit(solution)/shard_map/stack | solution.py:348
  1.8 2.1 %dynamic-slice_bitcast_fusion = (bf16[1,256,512]{2,1,0:T(8,128)(2,1)S(1)}, bf16[256,512]{1,0:T(8,128)(2,1)}, bf16[256,512]{1,0:T(8,128)(2,1)}, bf16[1,256,512]{2,1,0:T(8,128)(2,1)S(1)}) fusion(bf16[256,1024]{1,0:T(8,128)(2,1)} %param.5, s32[]{:T(128)S(6)} %select_n.65, s32[]{:T(128)S(6)} %select_n.64, bf16[256,1024]{1,0:T(8,128)(2,1)} %param.4), kind=kLoop, calls=%fused_computation.3 | loop fusion | bytes 2097160 | tf_op jit(solution)/shard_map/stack | solution.py:348
  3.8 0.1 pad_maximum_fusion
  3.9 0.8 collective-permute-start
  4.7 0.6 stack.63.s
  5.3 1.3 %collective-permute-done.got = bf16[3,256,512]{2,1,0:T(8,128)(2,1)S(1)} collective-permute-done((bf16[3,256,512]{2,1,0:T(8,128)(2,1)S(1)}, bf16[3,256,512]{2,1,0:T(8,128)(2,1)S(1)}, u32[]{:S(2)}, u32[]{:S(2)}) %collective-permute-start) | collective-permute-done | bytes 786464 | tf_op jit(solution)/shard_map/ppermute | solution.py:324
  6.6 0.0 copy-start.3
  6.6 0.9 copy-done.3
  7.5 4.2 %shard_map.37 = (bf16[3,512,512]{2,1,0:T(8,128)(2,1)}, bf16[768,512]{1,0:T(8,128)(2,1)}, bf16[768,512]{1,0:T(8,128)(2,1)}, bf16[256,512]{1,0:T(8,128)(2,1)}, bf1...) custom-call(s32[8]{0:T(128)} %stack.63.s, bf16[256,512]{1,0:T(8,128)(2,1)} %get-tuple-element.26.q, ...), custom_call_target="tpu_custom_call" | custom-call | tf_op jit(solution)/shard_map/pallas_call | solution.py:33
  11.7 8.2 %all-to-all-start = ((bf16[8,224,128]{2,1,0:T(8,128)(2,1)}), bf16[8,224,128]{2,1,0:T(8,128)(2,1)S(1)}, u32[]{:S(2)}, u32[]{:S(2)}) async-start(bf16[8,224,128]{2,1,0:T(8,128)(2,1)} %get-tuple-element.22), calls=%async_computation | async-start | bytes 917504 | tf_op jit(solution)/shard_map/all_to_all | solution.py:328
  19.8 1.5 %collective-permute-start.3 = (bf16[384,512]{1,0:T(8,128)(2,1)}, bf16[384,512]{1,0:T(8,128)(2,1)S(1)}, u32[]{:S(2)}, u32[]{:S(2)}) collective-permute-start(bf16[384,512]{1,0:T(8,128)(2,1)} %get-tuple-element.21.ppay), channel_id=1, source_target_pairs={{0,2},{1,3},{2,0},{3,1},{4,6},{5,7},{6,4},{7,5},{8,10},{9,11},{10,... | collective-permute-start | bytes 1179656 | tf_op jit(solution)/shard_map/ppermute | solution.py:324
  21.3 1.0 slice.12
  22.3 17.6 %collective-permute-done.3.pin = bf16[384,512]{1,0:T(8,128)(2,1)S(1)} collective-permute-done((bf16[384,512]{1,0:T(8,128)(2,1)}, bf16[384,512]{1,0:T(8,128)(2,1)S(1)}, u32[]{:S(2)}, u32[]{:S(2)}) %collective-permute-start.3) | collective-permute-done | bytes 393248 | tf_op jit(solution)/shard_map/ppermute | solution.py:324
  39.9 0.0 copy-start.2
  39.9 0.0 all-to-all-done.ain
  39.9 0.0 copy-start
  39.9 0.8 copy-done
  40.7 1.8 %shard_map.41 = bf16[1024,128]{1,0:T(8,128)(2,1)} custom-call(s32[8]{0:T(128)} %stack.63.s, bf16[8,224,128]{2,1,0:T(8,128)(2,1)} %copy-done), custom_call_target="tpu_custom_call" | custom-call | tf_op jit(solution)/shard_map/pallas_call | solution.py:33
  42.5 2.8 %collective-permute-start.6 = (bf16[1024,128]{1,0:T(8,128)(2,1)}, bf16[1024,128]{1,0:T(8,128)(2,1)S(1)}, u32[]{:S(2)}, u32[]{:S(2)}) collective-permute-start(bf16[1024,128]{1,0:T(8,128)(2,1)} %shard_map.41), channel_id=1, source_target_pairs={{0,16},{1,17},{2,18},{3,19},{4,20},{5,21},{6,22},{7,23},{16,32},{1... | collective-permute-start | bytes 786440 | tf_op jit(solution)/shard_map/ppermute | solution.py:324
  45.4 3.8 %collective-permute-start.4 = (bf16[512,512]{1,0:T(8,128)(2,1)S(1)}, bf16[512,512]{1,0:T(8,128)(2,1)S(1)}, u32[]{:S(2)}, u32[]{:S(2)}) collective-permute-start(bf16[512,512]{1,0:T(8,128)(2,1)S(1)} %pad_maximum_fusion.1), channel_id=1, source_target_pairs={{2,4},{3,5},{4,2},{5,3},{6,8},{7,9},{8,6},{9,7},{10,12},{11,13},{1... | collective-permute-start | bytes 1572872 | tf_op jit(solution)/shard_map/ppermute | solution.py:324
  49.1 2.4 %collective-permute-start.1 = (bf16[768,512]{1,0:T(8,128)(2,1)}, bf16[768,512]{1,0:T(8,128)(2,1)S(1)}, u32[]{:S(2)}, u32[]{:S(2)}) collective-permute-start(bf16[768,512]{1,0:T(8,128)(2,1)} %get-tuple-element.17), channel_id=1, source_target_pairs={{0,2},{1,3},{2,4},{3,5},{4,6},{5,7},{6,8},{7,9},{8,10},{9,11},{10,... | collective-permute-start | bytes 2359304 | tf_op jit(solution)/shard_map/ppermute | solution.py:324
  51.6 5.0 %collective-permute-start.2 = (bf16[768,512]{1,0:T(8,128)(2,1)}, bf16[768,512]{1,0:T(8,128)(2,1)S(1)}, u32[]{:S(2)}, u32[]{:S(2)}) collective-permute-start(bf16[768,512]{1,0:T(8,128)(2,1)} %get-tuple-element.18), channel_id=1, source_target_pairs={{2,0},{3,1},{4,2},{5,3},{6,4},{7,5},{8,6},{9,7},{10,8},{11,9},{12,... | collective-permute-start | bytes 2359304 | tf_op jit(solution)/shard_map/ppermute | solution.py:324
  56.5 0.0 collective-permute-done.6.xin
  56.6 0.0 copy-start.7
  56.6 0.7 copy-done.7
  57.3 2.7 %shard_map.42 = bf16[8,96,256]{2,1,0:T(8,128)(2,1)} custom-call(s32[8]{0:T(128)} %stack.63.s, bf16[8,224,128]{2,1,0:T(8,128)(2,1)} %copy-done, bf16[1024,128]{1,0:T(8,128)(2,1)} %copy-done.7), custom_call_target="tpu_custom_call" | custom-call | flops 67108864 | bytes 1048576 | tf_op jit(solution)/shard_map/pallas_call | solution.py:33
  59.9 0.0 copy-done.2
  59.9 3.5 %all-to-all-start.1 = ((bf16[8,96,256]{2,1,0:T(8,128)(2,1)}), bf16[8,96,256]{2,1,0:T(8,128)(2,1)S(1)}, u32[]{:S(2)}, u32[]{:S(2)}) async-start(bf16[8,96,256]{2,1,0:T(8,128)(2,1)} %shard_map.42), calls=%async_computation.1 | async-start | bytes 786432 | tf_op jit(solution)/shard_map/all_to_all | solution.py:328
  63.4 0.0 collective-permute-done.4.bin_
  63.4 0.0 copy-start.6
  63.4 0.8 copy-done.6
  64.2 4.2 %shard_map.40 = bf16[256,640]{1,0:T(8,128)(2,1)} custom-call(s32[8]{0:T(128)} %stack.63.s, bf16[384,512]{1,0:T(8,128)(2,1)} %get-tuple-element.21.ppay, bf16[384,512]{1,0:T(8,128)(2,1)} %copy-done.2, bf16[512,512]{1,0:T(8,128)(2,1)} %copy-done.6), custom_call_target="tpu_custom_call" | custom-call | flops 67108864 | bytes 1048576 | tf_op jit(solution)/shard_map/pallas_call | solution.py:33
  68.4 1.7 %fusion = (bf16[128,640]{1,0:T(8,128)(2,1)S(1)}, bf16[128,640]{1,0:T(8,128)(2,1)}) fusion(bf16[256,640]{1,0:T(8,128)(2,1)} %shard_map.40), kind=kLoop, calls=%fused_computation.9 | loop fusion | bytes 655360 | tf_op jit(solution)/shard_map/slice | solution.py:372
  70.1 1.4 %collective-permute-start.5 = (bf16[128,640]{1,0:T(8,128)(2,1)S(1)}, bf16[128,640]{1,0:T(8,128)(2,1)S(1)}, u32[]{:S(2)}, u32[]{:S(2)}) collective-permute-start(bf16[128,640]{1,0:T(8,128)(2,1)S(1)} %get-tuple-element.31), channel_id=1, source_target_pairs={{0,2},{1,3},{2,0},{3,1},{4,6},{5,7},{6,4},{7,5},{8,10},{9,11},{10,... | collective-permute-start | bytes 491528 | tf_op jit(solution)/shard_map/ppermute | solution.py:324
  71.5 4.9 %shard_map.38.near = bf16[512,640]{1,0:T(8,128)(2,1)} custom-call(s32[8]{0:T(128)} %stack.63.s, bf16[3,512,512]{2,1,0:T(8,128)(2,1)} %get-tuple-element.15.fine), custom_call_target="tpu_custom_call" | custom-call | flops 268435456 | bytes 2097152 | tf_op jit(solution)/shard_map/pallas_call | solution.py:33
  76.4 3.6 %collective-permute-done.1.rin = bf16[768,512]{1,0:T(8,128)(2,1)S(1)} collective-permute-done((bf16[768,512]{1,0:T(8,128)(2,1)}, bf16[768,512]{1,0:T(8,128)(2,1)S(1)}, u32[]{:S(2)}, u32[]{:S(2)}) %collective-permute-start.1) | collective-permute-done | bytes 786464 | tf_op jit(solution)/shard_map/ppermute | solution.py:324
  80.0 0.0 copy-start.4
  80.0 0.0 collective-permute-done.2.lin
  80.0 0.0 copy-start.5
  80.0 0.9 copy-done.4
  80.9 0.2 copy-done.5
  81.2 5.4 %shard_map.39 = (bf16[512,640]{1,0:T(8,128)(2,1)}, bf16[256,640]{1,0:T(8,128)(2,1)}) custom-call(s32[8]{0:T(128)} %stack.63.s, bf16[3,512,512]{2,1,0:T(8,128)(2,1)} %get-tuple-element.15.fine, bf16[256,512]{1,0:T(8,128)(2,1)} %get-tuple-element.16.q1, bf16[768,512]{1,0:T(8,128)(2,1)} %copy-done.4, bf16[768,512]{1,0:T(8,128)(2,1)} %copy-done.5), custom_call_target="tpu_custom_call" | custom-call | flops 268435456 | bytes 2097152 | tf_op jit(solution)/shard_map/pallas_call | solution.py:33
  86.6 0.0 collective-permute-done.5.two_back
  86.6 0.0 copy-start.8
  86.6 0.0 all-to-all-done.1.row_back
  86.6 0.0 copy-start.1
  86.6 0.7 copy-done.8
  87.3 0.1 copy-done.1
  87.4 6.9 %shard_map.43 = (bf16[256,512]{1,0:T(8,128)(2,1)}, bf16[256,512]{1,0:T(8,128)(2,1)}) custom-call(s32[8]{0:T(128)} %stack.63.s, bf16[512,640]{1,0:T(8,128)(2,1)} %shard_map.38.near, bf16[512,640]{1,0:T(8,128)(2,1)} %get-tuple-element.19.far, bf16[256,640]{1,0:T(8,128)(2,1)} %get-tuple-element.20.one, bf16[128,640]{1,0:T(8,128)(2,1)} %get-tuple-element.32.two, ...), custom_call_target="tpu_custom_call" | custom-call | flops 67108864 | bytes 2097152 | tf_op jit(solution)/shard_map/pallas_call | solution.py:33
  94.3 22.5 %collective-permute-start.7 = (bf16[256,512]{1,0:T(8,128)(2,1)}, bf16[256,512]{1,0:T(8,128)(2,1)S(1)}, u32[]{:S(2)}, u32[]{:S(2)}) collective-permute-start(bf16[256,512]{1,0:T(8,128)(2,1)} %get-tuple-element.24), channel_id=1, source_target_pairs={{0,1},{1,0},{2,3},{3,2},{4,5},{5,4},{6,7},{7,6},{8,9},{9,8},{10,11... | collective-permute-start | bytes 786440 | tf_op jit(solution)/shard_map/ppermute | solution.py:324
  116.8 1.4 %collective-permute-done.7 = bf16[256,512]{1,0:T(8,128)(2,1)S(1)} collective-permute-done((bf16[256,512]{1,0:T(8,128)(2,1)}, bf16[256,512]{1,0:T(8,128)(2,1)S(1)}, u32[]{:S(2)}, u32[]{:S(2)}) %collective-permute-start.7) | collective-permute-done | bytes 262176 | tf_op jit(solution)/shard_map/ppermute | solution.py:324
  118.2 2.0 %maximum_select_fusion = bf16[256,1024]{1,0:T(8,128)(2,1)} fusion(bf16[256,512]{1,0:T(8,128)(2,1)S(1)} %collective-permute-done.7, bf16[256,512]{1,0:T(8,128)(2,1)} %get-tuple-element.23, pred[]{:T(512)S(6)} %eq.14), kind=kLoop, calls=%fused_computation.2 | loop fusion | flops 2359296 | bytes 1048577 | tf_op jit(solution)/shard_map/jit(_where)/select_n | solution.py:386
  (2 shorter events, 0.1 us)
Async XLA Ops:
  3.9 2.7 %collective-permute-start = (bf16[3,256,512]{2,1,0:T(8,128)(2,1)S(1)}, bf16[3,256,512]{2,1,0:T(8,128)(2,1)S(1)}, u32[]{:S(2)}, u32[]{:S(2)}) collective-permute-start(bf16[3,256,512]{2,1,0:T(8,128)(2,1)S(1)} %pad_maximum_fusion), channel_id=1, source_target_pairs={{0,1},{1,0},{2,3},{3,2},{4,5},{5,4},{6,7},{7,6},{8,9},{9,8},{10,11... | collective-permute-start | bytes 2359304 | tf_op jit(solution)/shard_map/ppermute | solution.py:324
  6.6 0.9 copy-start.3
  11.7 28.3 %all-to-all-start = ((bf16[8,224,128]{2,1,0:T(8,128)(2,1)}), bf16[8,224,128]{2,1,0:T(8,128)(2,1)S(1)}, u32[]{:S(2)}, u32[]{:S(2)}) async-start(bf16[8,224,128]{2,1,0:T(8,128)(2,1)} %get-tuple-element.22), calls=%async_computation | async-start | bytes 917504 | tf_op jit(solution)/shard_map/all_to_all | solution.py:328
  19.8 20.0 %collective-permute-start.3 = (bf16[384,512]{1,0:T(8,128)(2,1)}, bf16[384,512]{1,0:T(8,128)(2,1)S(1)}, u32[]{:S(2)}, u32[]{:S(2)}) collective-permute-start(bf16[384,512]{1,0:T(8,128)(2,1)} %get-tuple-element.21.ppay), channel_id=1, source_target_pairs={{0,2},{1,3},{2,0},{3,1},{4,6},{5,7},{6,4},{7,5},{8,10},{9,11},{10,... | collective-permute-start | bytes 1179656 | tf_op jit(solution)/shard_map/ppermute | solution.py:324
  39.9 20.0 %copy-start.2 = (bf16[384,512]{1,0:T(8,128)(2,1)}, bf16[384,512]{1,0:T(8,128)(2,1)S(1)}, u32[]{:S(2)}) copy-start(bf16[384,512]{1,0:T(8,128)(2,1)S(1)} %collective-permute-done.3.pin) | copy-start | bytes 1179652
  39.9 0.8 copy-start
  42.5 14.0 %collective-permute-start.6 = (bf16[1024,128]{1,0:T(8,128)(2,1)}, bf16[1024,128]{1,0:T(8,128)(2,1)S(1)}, u32[]{:S(2)}, u32[]{:S(2)}) collective-permute-start(bf16[1024,128]{1,0:T(8,128)(2,1)} %shard_map.41), channel_id=1, source_target_pairs={{0,16},{1,17},{2,18},{3,19},{4,20},{5,21},{6,22},{7,23},{16,32},{1... | collective-permute-start | bytes 786440 | tf_op jit(solution)/shard_map/ppermute | solution.py:324
  45.4 18.0 %collective-permute-start.4 = (bf16[512,512]{1,0:T(8,128)(2,1)S(1)}, bf16[512,512]{1,0:T(8,128)(2,1)S(1)}, u32[]{:S(2)}, u32[]{:S(2)}) collective-permute-start(bf16[512,512]{1,0:T(8,128)(2,1)S(1)} %pad_maximum_fusion.1), channel_id=1, source_target_pairs={{2,4},{3,5},{4,2},{5,3},{6,8},{7,9},{8,6},{9,7},{10,12},{11,13},{1... | collective-permute-start | bytes 1572872 | tf_op jit(solution)/shard_map/ppermute | solution.py:324
  49.1 30.9 %collective-permute-start.1 = (bf16[768,512]{1,0:T(8,128)(2,1)}, bf16[768,512]{1,0:T(8,128)(2,1)S(1)}, u32[]{:S(2)}, u32[]{:S(2)}) collective-permute-start(bf16[768,512]{1,0:T(8,128)(2,1)} %get-tuple-element.17), channel_id=1, source_target_pairs={{0,2},{1,3},{2,4},{3,5},{4,6},{5,7},{6,8},{7,9},{8,10},{9,11},{10,... | collective-permute-start | bytes 2359304 | tf_op jit(solution)/shard_map/ppermute | solution.py:324
  51.6 28.5 %collective-permute-start.2 = (bf16[768,512]{1,0:T(8,128)(2,1)}, bf16[768,512]{1,0:T(8,128)(2,1)S(1)}, u32[]{:S(2)}, u32[]{:S(2)}) collective-permute-start(bf16[768,512]{1,0:T(8,128)(2,1)} %get-tuple-element.18), channel_id=1, source_target_pairs={{2,0},{3,1},{4,2},{5,3},{6,4},{7,5},{8,6},{9,7},{10,8},{11,9},{12,... | collective-permute-start | bytes 2359304 | tf_op jit(solution)/shard_map/ppermute | solution.py:324
  56.6 0.7 copy-start.7
  59.9 26.7 %all-to-all-start.1 = ((bf16[8,96,256]{2,1,0:T(8,128)(2,1)}), bf16[8,96,256]{2,1,0:T(8,128)(2,1)S(1)}, u32[]{:S(2)}, u32[]{:S(2)}) async-start(bf16[8,96,256]{2,1,0:T(8,128)(2,1)} %shard_map.42), calls=%async_computation.1 | async-start | bytes 786432 | tf_op jit(solution)/shard_map/all_to_all | solution.py:328
  63.4 0.8 copy-start.6
  70.1 16.5 %collective-permute-start.5 = (bf16[128,640]{1,0:T(8,128)(2,1)S(1)}, bf16[128,640]{1,0:T(8,128)(2,1)S(1)}, u32[]{:S(2)}, u32[]{:S(2)}) collective-permute-start(bf16[128,640]{1,0:T(8,128)(2,1)S(1)} %get-tuple-element.31), channel_id=1, source_target_pairs={{0,2},{1,3},{2,0},{3,1},{4,6},{5,7},{6,4},{7,5},{8,10},{9,11},{10,... | collective-permute-start | bytes 491528 | tf_op jit(solution)/shard_map/ppermute | solution.py:324
  80.0 0.9 copy-start.4
  80.0 1.1 copy-start.5
  86.6 0.7 copy-start.8
  86.6 0.8 copy-start.1
  94.3 23.9 %collective-permute-start.7 = (bf16[256,512]{1,0:T(8,128)(2,1)}, bf16[256,512]{1,0:T(8,128)(2,1)S(1)}, u32[]{:S(2)}, u32[]{:S(2)}) collective-permute-start(bf16[256,512]{1,0:T(8,128)(2,1)} %get-tuple-element.24), channel_id=1, source_target_pairs={{0,1},{1,0},{2,3},{3,2},{4,5},{5,4},{6,7},{7,6},{8,9},{9,8},{10,11... | collective-permute-start | bytes 786440 | tf_op jit(solution)/shard_map/ppermute | solution.py:324
where the time goes:
time: 121 us; the launch traced here: 120 us
  starting transfers between devices  51.7 us (43%)
  Pallas kernels  30 us (25%)
  waiting for transfers between devices  23.9 us (20%)
  local copies, waits for them, and re-layouts  12.2 us (10%)
  other arithmetic  2.1 us (2%)
    ppermute x8, starting transfers between devices, send_to(): return lax.ppermute(x, 'seq', pairs)  40.1 us
    pallas_call x7, Pallas kernels, call(): pl.pallas_call(body, out_shape=outs, in_specs=[pl.BlockSpec(memory_space=...  30 us
    ppermute x8, waiting for transfers between devices, send_to(): return lax.ppermute(x, 'seq', pairs)  23.9 us
    all_to_all x2, starting transfers between devices, line_swap(): return lax.all_to_all(x, 'seq', 0, 0, axis_index_groups=LINES)  11.6 us
    unnamed x18, local copies, waits for them, and re-layouts  5.11 us
    another operation x2, local copies, waits for them, and re-layouts, local(): jnp.stack([lax.dynamic_slice(x, (0, (1 - core) * COLS), (B, COLS)) for x...  3.82 us
  transfers between devices with their start and end apart: 10, of which 4 were waited for; matrix products, arithmetic and copies ran while one was open for 3% of the time, Pallas kernels for 14%

commit v1 on v0

v1 whole, which is shorter than its diff:
```python
import functools
import math

import jax
import jax.numpy as jnp
from jax import lax
from jax.experimental import pallas as pl
from jax.experimental.pallas import tpu as pltpu
from jax.sharding import PartitionSpec as P

HEADS = 4
DH = 128
COLS = HEADS * DH
B = 256
PACK = COLS + 128
ABSENT = -1e30
SCALE = math.log2(math.e) / math.sqrt(DH)
F32 = jnp.float32
BF16 = jnp.bfloat16

CHIPS = 128
RING = 8
ROWS4, ROWS3 = 32, 64
SEND = 3 * ROWS4 + 2 * ROWS3
BACK = ROWS4 + ROWS3 + 16
VMEM_LIMIT = 24 * 2**20


def shaped(*shape):
    return jax.ShapeDtypeStruct(shape, BF16)


def call(body, outs, scalars, arrays, halves=0, extra=()):
    def outer(s, *refs):
        whole, rest = refs[:halves], list(refs[halves:])
        if halves:
            *rest, held, sems = rest
            start = pl.multiple_of(s[0] * COLS, COLS)
            copies = [
                pltpu.make_async_copy(ref.at[:, pl.ds(start, COLS)], held.at[i], sems.at[i])
                for i, ref in enumerate(whole)
            ]
            for copy in copies:
                copy.start()
            for copy in copies:
                copy.wait()
            rest = [held.at[i] for i in range(halves)] + rest
        body(s, *rest)

    scratch = list(extra)
    if halves:
        scratch += [pltpu.VMEM((halves, B, COLS), BF16), pltpu.SemaphoreType.DMA((halves,))]
    return pl.pallas_call(
        outer,
        out_shape=outs,
        in_specs=[pl.BlockSpec(memory_space=pltpu.SMEM)]
        + [pl.BlockSpec(memory_space=pl.ANY)] * halves
        + [pl.BlockSpec(memory_space=pltpu.VMEM)] * (len(arrays) - halves),
        out_specs=[pl.BlockSpec(memory_space=pltpu.VMEM)] * len(outs),
        scratch_shapes=scratch,
        compiler_params=pltpu.CompilerParams(vmem_limit_bytes=VMEM_LIMIT),
        cost_estimate=pl.CostEstimate(flops=0, bytes_accessed=0, transcendentals=0),
    )(scalars, *arrays)


def pool_matrix(rows, width, level, scale):
    row = lax.broadcasted_iota(jnp.int32, (rows, width), 0)
    col = lax.broadcasted_iota(jnp.int32, (rows, width), 1)
    return jnp.where((col >> level) == row, scale, 0.0).astype(BF16)


def spread_matrix(rows, width, level):
    row = lax.broadcasted_iota(jnp.int32, (rows, width), 0)
    col = lax.broadcasted_iota(jnp.int32, (rows, width), 1)
    return jnp.where((row >> level) == col, 1.0, 0.0).astype(BF16)


def pooled(x, level, mean):
    rows = x.shape[0]
    scale = 1.0 / 2**level if mean else 1.0
    matrix = pool_matrix(rows >> level, rows, level, scale)
    return jnp.dot(matrix, x, preferred_element_type=F32).astype(BF16)


def attend(jobs, factor):
    results = []
    scores = []
    for q, parts in jobs:
        row = []
        for k, _, bias in parts:
            s = lax.dot_general(q, k, (((1,), (1,)), ((), ())), preferred_element_type=F32) * SCALE
            row.append(s if bias is None else s + bias)
        scores.append(row)
    tops = [
        functools.reduce(jnp.maximum, [jnp.max(s, axis=1, keepdims=True) for s in row])
        for row in scores
    ]
    weights = [[jnp.exp2(s - m) for s in row] for row, m in zip(scores, tops)]
    totals = [
        functools.reduce(jnp.add, [jnp.sum(w, axis=1, keepdims=True) for w in row]) * factor
        for row in weights
    ]
    for (_, parts), row, m, total in zip(jobs, weights, tops, totals):
        out = None
        for w, (_, v, _) in zip(row, parts):
            o = jnp.dot(w.astype(BF16), v, preferred_element_type=F32)
            out = o if out is None else out + o
        results.append(((out / total).astype(BF16), m + jnp.log2(total)))
    return results


def tile_of(values):
    rows = values[0].shape[0]
    lane = lax.broadcasted_iota(jnp.int32, (rows, 128), 1)
    full = jnp.zeros((rows, 128), F32)
    for h, value in enumerate(values):
        full = jnp.where((lane & 3) == h, value, full)
    high = full.astype(BF16)
    rest = full - high.astype(F32)
    middle = rest.astype(BF16)
    low = (rest - middle.astype(F32)).astype(BF16)
    zero = jnp.zeros((rows, 128), BF16)
    part = lane >> 2
    return jnp.where(part == 0, high, jnp.where(part == 1, middle, jnp.where(part == 2, low, zero)))


def merged(terms):
    top = functools.reduce(jnp.maximum, [t for _, t in terms])
    weights = [jnp.exp2(t - top) for _, t in terms]
    total = functools.reduce(jnp.add, weights)
    inverse = 1.0 / total
    weights = [t * inverse for t in weights]
    outs = []
    for h in range(HEADS):
        cols = slice(h * DH, (h + 1) * DH)
        parts = [o[:, cols] * t[:, h : h + 1] for (o, _), t in zip(terms, weights)]
        outs.append(functools.reduce(jnp.add, parts))
    return outs, top + jnp.log2(total)


def unpacked(values):
    values = values.astype(F32)
    t = values[:, COLS:]
    return values[:, :COLS], t + pltpu.roll(t, 128 - 4, 1) + pltpu.roll(t, 128 - 8, 1)


def packed_tile(full):
    lane = lax.broadcasted_iota(jnp.int32, full.shape, 1)
    full = jnp.where(lane < HEADS, full, 0.0)
    high = full.astype(BF16).astype(F32)
    middle = (full - high).astype(BF16).astype(F32)
    low = (full - high - middle).astype(BF16).astype(F32)
    return (high + pltpu.roll(middle, 4, 1) + pltpu.roll(low, 8, 1)).astype(BF16)


def spread(values, rows, level):
    matrix = spread_matrix(rows, rows >> level, level)
    return unpacked(jnp.dot(matrix, values, preferred_element_type=F32))


def attend_to(out_ref, row, q_of, parts_of, rows, factor, group=2):
    values = []
    for first in range(0, HEADS, group):
        spans = [slice(h * DH, (h + 1) * DH) for h in range(first, first + group)]
        for cols, (o, value) in zip(
            spans, attend([(q_of(cols), parts_of(cols)) for cols in spans], factor)
        ):
            out_ref[row : row + rows, cols] = o
            values.append(value)
    out_ref[row : row + rows, COLS:] = tile_of(values)


def edge_body(s, k0, v0, k1, v1, rpay, lpay):
    low_first = s[0] == 0
    for n, pair in enumerate(((k0, k1), (v0, v1))):
        low = jnp.where(low_first, pair[0][...], pair[1][...])
        high = jnp.where(low_first, pair[1][...], pair[0][...])
        rpay[n * B : (n + 1) * B] = high
        lpay[n * B : (n + 1) * B] = low
        rows = slice(2 * B + n * 128, 2 * B + (n + 1) * 128)
        rpay[rows] = pooled(low, 1, n == 0)
        lpay[rows] = pooled(high, 1, n == 0)


def pool_body(s, q0, k0, v0, q1, k1, v1, q_one, q_two, apay):
    half = s[1]
    for at, refs in enumerate(((q0, k0, v0), (q1, k1, v1))):
        q = refs[0][...]
        q_one[at * 128 : (at + 1) * 128] = pooled(q, 1, True)
        q_two[at * 64 : (at + 1) * 64] = pooled(q, 2, True)
        three = [pooled(ref[...], 3, n < 2) for n, ref in enumerate(refs)]
        four = [pooled(ref[...], 4, n < 2) for n, ref in enumerate(refs)]
        for j in range(RING):
            cols = slice((j % HEADS) * DH, (j % HEADS + 1) * DH)
            for n in range(3):
                apay[j, n * ROWS4 + at * 16 : n * ROWS4 + (at + 1) * 16] = four[n][:, cols]
            first = jnp.where(half == j // HEADS, three[0][:, cols], three[1][:, cols])
            base = 3 * ROWS4
            apay[j, base + at * 32 : base + (at + 1) * 32] = first
            base += ROWS3
            apay[j, base + at * 32 : base + (at + 1) * 32] = three[2][:, cols]


def near_body(s, q0, k0, v0, q1, k1, v1, out):
    for at, q in enumerate((q0, q1)):
        attend_to(
            out,
            at * B,
            lambda cols: q[:, cols],
            lambda cols: [(k0[:, cols], v0[:, cols], None), (k1[:, cols], v1[:, cols], None)],
            B,
            1.0,
        )


def derive_body(s, rin, lin, bpay, kept):
    odd = s[7] == 1
    for n in (0, 1):
        sides = []
        for ref in (rin, lin):
            near = pooled(ref[n * B : (n + 1) * B], 2, n == 0)
            far = pooled(ref[2 * B + n * 128 : 2 * B + (n + 1) * 128], 1, n == 0)
            sides.append((near, far))
        for i in (0, 1):
            rows = slice(n * 128 + i * 64, n * 128 + (i + 1) * 64)
            bpay[rows] = jnp.where(odd, sides[0][i], sides[1][i])
            kept[rows] = jnp.where(odd, sides[1][i], sides[0][i])


def far_body(s, q0, q1, q_one, near, rin, lin, out, tile, out0, out1):
    first = s[0] == 0
    bias_left = jnp.where(s[2] == 1, 0.0, ABSENT).astype(F32)
    bias_right = jnp.where(s[3] == 1, 0.0, ABSENT).astype(F32)
    for at, q in enumerate((q0, q1)):
        left = first if at == 0 else jnp.logical_not(first)
        bias = jnp.where(left, bias_left, bias_right)
        attend_to(
            out0,
            at * B,
            lambda cols: q[:, cols],
            lambda cols: [
                (
                    jnp.where(left, rin[:B, cols], lin[:B, cols]),
                    jnp.where(left, rin[B : 2 * B, cols], lin[B : 2 * B, cols]),
                    bias,
                )
            ],
            B,
            1.0,
        )

    def coarse(cols):
        parts = []
        for ref, bias in ((rin, bias_left), (lin, bias_right)):
            keys = pooled(ref[:B, cols], 1, True)
            values = pooled(ref[B : 2 * B, cols], 1, False)
            keys = jnp.concatenate([keys, ref[2 * B : 2 * B + 128, cols]], axis=0)
            values = jnp.concatenate([values, ref[2 * B + 128 :, cols]], axis=0)
            parts.append((keys, values, bias))
        return parts

    attend_to(out1, 0, lambda cols: q_one[:, cols], coarse, B, 2.0)
    for at in (0, 1):
        rows = slice(at * B, (at + 1) * B)
        one = spread(out1[at * 128 : (at + 1) * 128], B, 1)
        outs, weights = merged([unpacked(near[rows]), unpacked(out0[rows]), one])
        for h in range(HEADS):
            out[rows, h * DH : (h + 1) * DH] = outs[h]
        tile[rows] = weights


def pair_body(s, q_two, kept, pin, bin_, mine, theirs):
    bias = jnp.where(s[4] == 1, 0.0, ABSENT).astype(F32)
    for out, ref in ((mine, q_two), (theirs, pin)):
        attend_to(
            out,
            0,
            lambda cols: ref[:, cols],
            lambda cols: [
                (
                    jnp.concatenate([kept[:128, cols], bin_[:128, cols]], axis=0),
                    jnp.concatenate([kept[128:, cols], bin_[128:, cols]], axis=0),
                    bias,
                ),
            ],
            128,
            4.0,
            4,
        )


def row_pay_body(s, ain, xpay):
    other = (1 - s[1]) * HEADS
    for j in range(RING):
        xpay[j * ROWS4 : (j + 1) * ROWS4] = ain[j, ROWS4 : 2 * ROWS4]
        xpay[B + j * ROWS4 : B + (j + 1) * ROWS4] = ain[j, 2 * ROWS4 : 3 * ROWS4]
    for j in range(HEADS):
        for n in (0, 1):
            base = 3 * ROWS4 + n * ROWS3
            to = (2 + n) * B + j * ROWS3
            xpay[to : to + ROWS3] = ain[other + j, base : base + ROWS3]


def row_body(s, ain, xin, back):
    half, head = s[1], s[5]
    bias = jnp.where(s[6] == 1, 0.0, ABSENT).astype(F32)
    mine, other = half * HEADS, (1 - half) * HEADS
    base = 3 * ROWS4
    rows3 = lambda at, low: jnp.concatenate(
        [ain[at + j, low : low + ROWS3] for j in range(HEADS)], axis=0
    )
    q4 = jnp.concatenate([ain[j, :ROWS4] for j in range(RING)], axis=0)
    ((o4, value4),) = attend([(q4, [(xin[:B], xin[B : 2 * B], bias)])], 16.0)
    parts = [
        (rows3(other, base), rows3(other, base + ROWS3), None),
        (xin[2 * B : 3 * B], xin[3 * B :], bias),
    ]
    ((o3, value3),) = attend([(rows3(mine, base), parts)], 8.0)
    row = lax.broadcasted_iota(jnp.int32, (ROWS4 + ROWS3, 128), 0)
    col = lax.broadcasted_iota(jnp.int32, (ROWS4 + ROWS3, 128), 1)
    term = lax.broadcasted_iota(jnp.int32, (16, 128), 0)
    for j in range(RING):
        rows4 = slice(j * ROWS4, (j + 1) * ROWS4)
        rows3 = slice((j % HEADS) * ROWS3, (j % HEADS + 1) * ROWS3)
        back[j, :ROWS4] = o4[rows4]
        back[j, ROWS4 : ROWS4 + ROWS3] = o3[rows3]
        values = jnp.concatenate([value4[rows4], value3[rows3]], axis=0)
        line = jnp.sum(jnp.where(row == col, values, 0.0), axis=0, keepdims=True)
        high = line.astype(BF16).astype(F32)
        middle = (line - high).astype(BF16).astype(F32)
        low = line - high - middle
        three = jnp.where(
            term == 0, high, jnp.where(term == 1, middle, jnp.where(term == 2, low, 0.0))
        )
        back[j, ROWS4 + ROWS3 :] = three.astype(BF16)


def merge_body(s, fine, tile, two, two_back, row_back, mine, send):
    low = s[1] * HEADS
    row = lax.broadcasted_iota(jnp.int32, (ROWS4 + ROWS3, 128), 0)
    lane = lax.broadcasted_iota(jnp.int32, (ROWS4 + ROWS3, 128), 1)

    def joined(first, rows):
        tile = jnp.zeros((ROWS4 + ROWS3, 128), F32)
        for g in range(HEADS):
            three = row_back[first + g, ROWS4 + ROWS3 :].astype(F32)
            line = jnp.sum(three, axis=0, keepdims=True)
            column = jnp.sum(jnp.where(row == lane, line, 0.0), axis=1, keepdims=True)
            tile = jnp.where(lane == g, column, tile)
        o = [row_back[first + g, rows] for g in range(HEADS)]
        return jnp.concatenate(o + [packed_tile(tile[rows])], axis=1)

    four = [joined(side * HEADS, slice(0, ROWS4)) for side in (0, 1)]
    three = joined(low, slice(ROWS4, ROWS4 + ROWS3))
    terms = [
        unpacked(two[...]),
        unpacked(two_back[...]),
        spread(three, 128, 1),
        spread(four[0], 128, 2),
        spread(four[1], 128, 2),
    ]
    outs, weights = merged(terms)
    coarse = jnp.concatenate([o.astype(BF16) for o in outs] + [packed_tile(weights)], axis=1)
    for at, out in enumerate((mine, send)):
        rows = slice(at * B, (at + 1) * B)
        outs, _ = merged(
            [(fine[rows], tile[rows]), spread(coarse[at * 64 : (at + 1) * 64], B, 2)]
        )
        for h in range(HEADS):
            out[:, h * DH : (h + 1) * DH] = outs[h].astype(BF16)


def join_body(s, mine, theirs, out, sems):
    low = pl.multiple_of(s[0] * COLS, COLS)
    high = pl.multiple_of((1 - s[0]) * COLS, COLS)
    copies = [
        pltpu.make_async_copy(mine, out.at[:, pl.ds(low, COLS)], sems.at[0]),
        pltpu.make_async_copy(theirs, out.at[:, pl.ds(high, COLS)], sems.at[1]),
    ]
    for copy in copies:
        copy.start()
    for copy in copies:
        copy.wait()


def join(s, mine, theirs):
    return pl.pallas_call(
        join_body,
        out_shape=shaped(B, 2 * COLS),
        in_specs=[pl.BlockSpec(memory_space=pltpu.SMEM)]
        + [pl.BlockSpec(memory_space=pltpu.VMEM)] * 2,
        out_specs=pl.BlockSpec(memory_space=pl.ANY),
        scratch_shapes=[pltpu.SemaphoreType.DMA((2,))],
        compiler_params=pltpu.CompilerParams(vmem_limit_bytes=VMEM_LIMIT),
    )(s, mine, theirs)


def pairs_of(target):
    pairs = []
    for chip in range(CHIPS):
        to = target(chip)
        if 0 <= to < CHIPS:
            pairs += [(2 * chip + core, 2 * to + core) for core in (0, 1)]
    return pairs


SWAP = [(i, i ^ 1) for i in range(2 * CHIPS)]
RIGHT = pairs_of(lambda chip: chip + 1)
LEFT = pairs_of(lambda chip: chip - 1)
PAIR = pairs_of(lambda chip: chip ^ 1)
BOUND = pairs_of(lambda chip: chip + 1 if chip % 2 else chip - 1)
ROW = pairs_of(lambda chip: chip + RING if chip % RING < RING // 2 else chip - RING)
LINES = [
    [2 * (row * RING + z) + core for z in range(RING)]
    for row in range(CHIPS // RING)
    for core in (0, 1)
]


def send_to(x, pairs):
    return lax.ppermute(x, "seq", pairs)


def after(x, y):
    return lax.optimization_barrier((x, y))


def line_swap(x):
    return lax.all_to_all(x, "seq", 0, 0, axis_index_groups=LINES)


def local(query_rows, key_rows, value_rows):
    position = lax.axis_index("seq")
    core = position % 2
    chip = position // 2
    z = chip % RING
    row = chip // RING
    half = z // HEADS
    odd = chip % 2
    has_left = chip >= 1
    has_right = chip <= CHIPS - 2
    has_pair = jnp.where(odd == 1, chip <= CHIPS - 3, chip >= 2)
    has_row = jnp.where(half == 0, row >= 1, row <= CHIPS // RING - 2)
    s = jnp.stack(
        [core, half, has_left, has_right, has_pair, z % HEADS, has_row, odd]
    ).astype(jnp.int32)

    own = (query_rows, key_rows, value_rows)
    got = [None, send_to(key_rows, SWAP), send_to(value_rows, SWAP)]
    got[0] = send_to(query_rows, SWAP)
    fine = (*own, *got)
    rpay, lpay = call(
        edge_body, (shaped(3 * B, COLS), shaped(3 * B, COLS)), s, (*own[1:], *got[1:]), halves=4
    )
    rin = send_to(rpay, RIGHT)
    lin = send_to(lpay, LEFT)
    s, rpay = after(s, rpay)
    outs = (shaped(B, COLS), shaped(128, COLS), shaped(RING, SEND, DH))
    q_one, q_two, apay = call(pool_body, outs, s, fine, halves=6)
    ain = line_swap(apay)
    pin = send_to(q_two, PAIR)
    (near,) = call(near_body, (shaped(2 * B, PACK),), s, fine, halves=6)
    s, near = after(s, near)
    (xpay,) = call(row_pay_body, (shaped(4 * B, DH),), s, (ain,))
    xin = send_to(xpay, ROW)
    s, _ = after(s, xpay)
    bpay, kept = call(derive_body, (shaped(B, COLS), shaped(B, COLS)), s, (rin, lin))
    bin_ = send_to(bpay, BOUND)
    s, _ = after(s, bpay)
    far, far_tile = call(
        far_body,
        (jax.ShapeDtypeStruct((2 * B, COLS), F32), jax.ShapeDtypeStruct((2 * B, 128), F32)),
        s,
        (query_rows, got[0], q_one, near, rin, lin),
        halves=2,
        extra=[pltpu.VMEM((2 * B, PACK), BF16), pltpu.VMEM((B, PACK), BF16)],
    )
    s, far = after(s, far)
    two, theirs = call(
        pair_body, (shaped(128, PACK), shaped(128, PACK)), s, (q_two, kept, pin, bin_)
    )
    two_back = send_to(theirs, PAIR)
    s, two = after(s, two)
    (back,) = call(row_body, (shaped(RING, BACK, DH),), s, (ain, xin))
    row_back = line_swap(back)
    mine, send = call(
        merge_body,
        (shaped(B, COLS), shaped(B, COLS)),
        s,
        (far, far_tile, two, two_back, row_back),
    )
    return join(s, mine, send_to(send, SWAP))


def solution(mesh):
    spec = P("seq", None)
    return jax.shard_map(
        local, mesh=mesh, in_specs=(spec, spec, spec), out_specs=spec, check_vma=False
    )
```

time: 121 us -> 96.4 us (0.80)
  the two profiles are of different devices: /device:TPU:29 before, /device:TPU:25 now
where the time goes in v1:
time: 96.4 us; the launch traced here: 95.7 us
  waiting for transfers between devices  37.8 us (39%)
  starting transfers between devices  31.5 us (33%)
  Pallas kernels  21.4 us (22%)
  local copies, waits for them, and re-layouts  4.66 us (5%)
    ppermute x10, waiting for transfers between devices, send_to(): return lax.ppermute(x, 'seq', pairs)  33.6 us
    pallas_call x9, Pallas kernels, call(): pl.pallas_call(outer, out_shape=outs, in_specs=[pl.BlockSpec(memory_space...  20.1 us
    ppermute x10, starting transfers between devices, send_to(): return lax.ppermute(x, 'seq', pairs)  19.8 us
    all_to_all x2, starting transfers between devices, line_swap(): return lax.all_to_all(x, 'seq', 0, 0, axis_index_groups=LINES)  11.7 us
    unnamed x20, local copies, waits for them, and re-layouts  4.58 us
    all_to_all x2, waiting for transfers between devices, line_swap(): return lax.all_to_all(x, 'seq', 0, 0, axis_index_groups=LINES)  4.17 us
  transfers between devices with their start and end apart: 12, of which 9 were waited for; matrix products, arithmetic and copies ran while one was open for 0% of the time, Pallas kernels for 12%

profile of v1, /device:TPU:25, one launch (start us, length us, event | category | flops | bytes accessed | tf_op | source)
XLA Modules:
  0.0 95.7 jit_solution(4739479740764808431)
XLA Ops:
  0.0 0.7 collective-permute-start
  0.7 0.0 collective-permute-start.1
  0.7 0.5 collective-permute-start.2
  1.2 0.1 stack.51.s
  1.3 1.2 %collective-permute-done.refs_2_.refs_4_ = bf16[256,1024]{1,0:T(8,128)(2,1)S(1)} collective-permute-done((bf16[256,1024]{1,0:T(8,128)(2,1)}, bf16[256,1024]{1,0:T(8,128)(2,1)S(1)}, u32[]{:S(2)}, u32[]{:S(2)}) %collective-permute-start) | collective-permute-done | bytes 524320 | tf_op jit(solution)/shard_map/ppermute | solution.py:421
  2.4 0.7 collective-permute-done.1.refs_3_.refs_5_
  3.2 0.0 copy-start
  3.2 1.0 %copy-done = bf16[256,1024]{1,0:T(8,128)(2,1)S(1)} copy-done((bf16[256,1024]{1,0:T(8,128)(2,1)S(1)}, bf16[256,1024]{1,0:T(8,128)(2,1)}, u32[]{:S(2)}) %copy-start) | copy-done | bytes 524312
  4.2 0.0 copy-start.2
  4.2 1.0 %copy-done.2 = bf16[256,1024]{1,0:T(8,128)(2,1)S(1)} copy-done((bf16[256,1024]{1,0:T(8,128)(2,1)S(1)}, bf16[256,1024]{1,0:T(8,128)(2,1)}, u32[]{:S(2)}) %copy-start.2) | copy-done | bytes 524312
  5.3 0.0 copy-start.1
  5.3 0.0 copy-start.4
  5.3 1.1 %shard_map.37 = (bf16[768,512]{1,0:T(8,128)(2,1)S(1)}, bf16[768,512]{1,0:T(8,128)(2,1)S(1)}) custom-call(s32[8]{0:T(128)S(1)} %stack.51.s, bf16[256,1024]{1,0:T(8,128)(2,1)S(1)} %copy-done, bf16[256,1024]{1,0:T(8,128)(2,1)S(1)} %copy-done.2, bf16[256,1024]{1,0:T(8,128)(2,1)S(1)} %collective-permute-done.refs_2_.refs_4_, ...), custom_call_target="tpu_custom_call" | custom-call | tf_op jit(solution)/shard_map/pallas_call | solution.py:53
  6.3 0.0 copy-start.9
  6.3 0.9 copy-done.9
  7.2 0.0 copy-start.8
  7.2 0.0 collective-permute-done.2.refs_3_.refs_1_
  7.2 0.0 copy-done.1
  7.2 0.0 copy-done.4
  7.2 1.5 %shard_map.39 = (bf16[256,512]{1,0:T(8,128)(2,1)S(1)}, bf16[128,512]{1,0:T(8,128)(2,1)S(1)}, bf16[8,224,128]{2,1,0:T(8,128)(2,1)S(1)}) custom-call(s32[8]{0:T(128)S(1)} %stack.51.s, bf16[256,1024]{1,0:T(8,128)(2,1)S(1)} %copy-done.4, bf16[256,1024]{1,0:T(8,128)(2,1)S(1)} %copy-done.1, bf16[256,1024]{1,0:T(8,128)(2,1)S(1)} %copy-done.2, ...), custom_call_target="tpu_custom_call" | custom-call | tf_op jit(solution)/shard_map/pallas_call | solution.py:53
  8.7 0.0 copy-done.8
  8.7 0.0 copy-start.7
  8.8 0.8 copy-done.7
  9.5 0.0 copy-start.3
  9.5 8.3 %all-to-all-start = ((bf16[8,224,128]{2,1,0:T(8,128)(2,1)}), bf16[8,224,128]{2,1,0:T(8,128)(2,1)}, u32[]{:S(2)}, u32[]{:S(2)}) async-start(bf16[8,224,128]{2,1,0:T(8,128)(2,1)} %copy-done.7), calls=%async_computation | async-start | bytes 917504 | tf_op jit(solution)/shard_map/all_to_all | solution.py:429
  17.8 3.4 %collective-permute-start.3 = (bf16[768,512]{1,0:T(8,128)(2,1)}, bf16[768,512]{1,0:T(8,128)(2,1)}, u32[]{:S(2)}, u32[]{:S(2)}) collective-permute-start(bf16[768,512]{1,0:T(8,128)(2,1)} %copy-done.9), channel_id=1, source_target_pairs={{0,2},{1,3},{2,4},{3,5},{4,6},{5,7},{6,8},{7,9},{8,10},{9,11},{10,... | collective-permute-start | bytes 2359304 | tf_op jit(solution)/shard_map/ppermute | solution.py:421
  21.2 6.1 %collective-permute-start.4 = (bf16[768,512]{1,0:T(8,128)(2,1)}, bf16[768,512]{1,0:T(8,128)(2,1)}, u32[]{:S(2)}, u32[]{:S(2)}) collective-permute-start(bf16[768,512]{1,0:T(8,128)(2,1)} %copy-done.8), channel_id=1, source_target_pairs={{2,0},{3,1},{4,2},{5,3},{6,4},{7,5},{8,6},{9,7},{10,8},{11,9},{12,... | collective-permute-start | bytes 2359304 | tf_op jit(solution)/shard_map/ppermute | solution.py:421
  27.3 0.0 copy-done.3
  27.3 2.6 %shard_map.38.refs_3_ = bf16[512,640]{1,0:T(8,128)(2,1)S(1)} custom-call(s32[8]{0:T(128)S(1)} %stack.51.s, bf16[256,1024]{1,0:T(8,128)(2,1)S(1)} %copy-done.4, bf16[256,1024]{1,0:T(8,128)(2,1)S(1)} %copy-done.1, bf16[256,1024]{1,0:T(8,128)(2,1)S(1)} %copy-done.3, bf16[256,1024]{1,0:T(8,128)(2,1)S(1)} %collective-permute-done.2.refs_3_.refs_1_, ...), custom_call_target="tpu_custom_call" | custom-call | tf_op jit(solution)/shard_map/pallas_call | solution.py:53
  29.9 0.0 copy-start.5
  29.9 0.8 copy-done.5
  30.7 3.5 %all-to-all-done.refs_0_ = bf16[8,224,128]{2,1,0:T(8,128)(2,1)} async-done(((bf16[8,224,128]{2,1,0:T(8,128)(2,1)}), bf16[8,224,128]{2,1,0:T(8,128)(2,1)}, u32[]{:S(2)}, u32[]{:S(2)}) %all-to-all-start) | async-done | bytes 458784 | tf_op jit(solution)/shard_map/all_to_all | solution.py:429
  34.2 1.0 %shard_map.40 = bf16[1024,128]{1,0:T(8,128)(2,1)S(1)} custom-call(s32[8]{0:T(128)S(1)} %stack.51.s, bf16[8,224,128]{2,1,0:T(8,128)(2,1)} %all-to-all-done.refs_0_), custom_call_target="tpu_custom_call" | custom-call | tf_op jit(solution)/shard_map/pallas_call | solution.py:53
  35.2 0.0 copy-start.6
  35.3 14.8 %collective-permute-done.3.refs_0_.refs_4_ = bf16[768,512]{1,0:T(8,128)(2,1)} collective-permute-done((bf16[768,512]{1,0:T(8,128)(2,1)}, bf16[768,512]{1,0:T(8,128)(2,1)}, u32[]{:S(2)}, u32[]{:S(2)}) %collective-permute-start.3) | collective-permute-done | bytes 786464 | tf_op jit(solution)/shard_map/ppermute | solution.py:421
  50.1 0.0 collective-permute-done.4.refs_1_.refs_5_
  50.1 1.8 %shard_map.41 = (bf16[256,512]{1,0:T(8,128)(2,1)S(1)}, bf16[256,512]{1,0:T(8,128)(2,1)S(1)}) custom-call(s32[8]{0:T(128)S(1)} %stack.51.s, bf16[768,512]{1,0:T(8,128)(2,1)} %collective-permute-done.3.refs_0_.refs_4_, bf16[768,512]{1,0:T(8,128)(2,1)} %collective-permute-done.4.refs_1_.refs_5_), custom_call_target="tpu_custom_call" | custom-call | tf_op jit(solution)/shard_map/pallas_call | solution.py:53
  51.9 4.3 %collective-permute-start.6 = (bf16[256,512]{1,0:T(8,128)(2,1)S(1)}, bf16[256,512]{1,0:T(8,128)(2,1)S(1)}, u32[]{:S(2)}, u32[]{:S(2)}) collective-permute-start(bf16[256,512]{1,0:T(8,128)(2,1)S(1)} %get-tuple-element.33), channel_id=1, source_target_pairs={{2,4},{3,5},{4,2},{5,3},{6,8},{7,9},{8,6},{9,7},{10,12},{11,13},{1... | collective-permute-start | bytes 786440 | tf_op jit(solution)/shard_map/ppermute | solution.py:421
  56.2 1.9 %collective-permute-start.8 = (bf16[1024,128]{1,0:T(8,128)(2,1)S(1)}, bf16[1024,128]{1,0:T(8,128)(2,1)S(1)}, u32[]{:S(2)}, u32[]{:S(2)}) collective-permute-start(bf16[1024,128]{1,0:T(8,128)(2,1)S(1)} %shard_map.40), channel_id=1, source_target_pairs={{0,16},{1,17},{2,18},{3,19},{4,20},{5,21},{6,22},{7,23},{16,32},{1... | collective-permute-start | bytes 786440 | tf_op jit(solution)/shard_map/ppermute | solution.py:421
  58.1 0.1 collective-permute-start.5
  58.2 0.0 copy-done.6
  58.2 5.5 %shard_map.42 = (f32[512,512]{1,0:T(8,128)S(1)}, f32[512,128]{1,0:T(8,128)S(1)}) custom-call(s32[8]{0:T(128)S(1)} %stack.51.s, bf16[256,1024]{1,0:T(8,128)(2,1)S(1)} %copy-done.4, bf16[256,1024]{1,0:T(8,128)(2,1)S(1)} %collective-permute-done.2.refs_3_.refs_1_, bf16[256,512]{1,0:T(8,128)(2,1)S(1)} %get-tuple-element.35.refs_2_, ...), custom_call_target="tpu_custom_call" | custom-call | tf_op jit(solution)/shard_map/pallas_call | solution.py:53
  63.7 0.0 collective-permute-done.5.refs_2_
  63.7 0.7 collective-permute-done.6.refs_3_
  64.4 1.3 %shard_map.43 = (bf16[128,640]{1,0:T(8,128)(2,1)S(1)}, bf16[128,640]{1,0:T(8,128)(2,1)S(1)}) custom-call(s32[8]{0:T(128)S(1)} %stack.51.s, bf16[128,512]{1,0:T(8,128)(2,1)S(1)} %get-tuple-element.39.refs_0_, bf16[256,512]{1,0:T(8,128)(2,1)S(1)} %get-tuple-element.40.refs_1_, bf16[128,512]{1,0:T(8,128)(2,1)S(1)} %collective-permute-done.5.refs_2_, ...), custom_call_target="tpu_custom_call" | custom-call | tf_op jit(solution)/shard_map/pallas_call | solution.py:53
  65.7 6.1 %collective-permute-done.8.refs_1_ = bf16[1024,128]{1,0:T(8,128)(2,1)S(1)} collective-permute-done((bf16[1024,128]{1,0:T(8,128)(2,1)S(1)}, bf16[1024,128]{1,0:T(8,128)(2,1)S(1)}, u32[]{:S(2)}, u32[]{:S(2)}) %collective-permute-start.8) | collective-permute-done | bytes 262176 | tf_op jit(solution)/shard_map/ppermute | solution.py:421
  71.8 2.6 %shard_map.44 = bf16[8,112,128]{2,1,0:T(8,128)(2,1)} custom-call(s32[8]{0:T(128)S(1)} %stack.51.s, bf16[8,224,128]{2,1,0:T(8,128)(2,1)} %all-to-all-done.refs_0_, bf16[1024,128]{1,0:T(8,128)(2,1)S(1)} %collective-permute-done.8.refs_1_), custom_call_target="tpu_custom_call" | custom-call | tf_op jit(solution)/shard_map/pallas_call | solution.py:53
  74.4 3.4 %all-to-all-start.1 = ((bf16[8,112,128]{2,1,0:T(8,128)(2,1)}), bf16[8,112,128]{2,1,0:T(8,128)(2,1)S(1)}, u32[]{:S(2)}, u32[]{:S(2)}) async-start(bf16[8,112,128]{2,1,0:T(8,128)(2,1)} %shard_map.44), calls=%async_computation.1 | async-start | bytes 458752 | tf_op jit(solution)/shard_map/all_to_all | solution.py:429
  77.8 1.4 %collective-permute-start.7 = (bf16[128,640]{1,0:T(8,128)(2,1)S(1)}, bf16[128,640]{1,0:T(8,128)(2,1)S(1)}, u32[]{:S(2)}, u32[]{:S(2)}) collective-permute-start(bf16[128,640]{1,0:T(8,128)(2,1)S(1)} %get-tuple-element.46), channel_id=1, source_target_pairs={{0,2},{1,3},{2,0},{3,1},{4,6},{5,7},{6,4},{7,5},{8,10},{9,11},{10,... | collective-permute-start | bytes 491528 | tf_op jit(solution)/shard_map/ppermute | solution.py:421
  79.2 8.9 %collective-permute-done.7.refs_3_ = bf16[128,640]{1,0:T(8,128)(2,1)S(1)} collective-permute-done((bf16[128,640]{1,0:T(8,128)(2,1)S(1)}, bf16[128,640]{1,0:T(8,128)(2,1)S(1)}, u32[]{:S(2)}, u32[]{:S(2)}) %collective-permute-start.7) | collective-permute-done | bytes 163872 | tf_op jit(solution)/shard_map/ppermute | solution.py:421
  88.1 0.7 all-to-all-done.1.refs_4_
  88.8 2.8 %shard_map.45 = (bf16[256,512]{1,0:T(8,128)(2,1)S(1)}, bf16[256,512]{1,0:T(8,128)(2,1)S(1)}) custom-call(s32[8]{0:T(128)S(1)} %stack.51.s, f32[512,512]{1,0:T(8,128)S(1)} %get-tuple-element.43.refs_0_, f32[512,128]{1,0:T(8,128)S(1)} %get-tuple-element.44.refs_1_, bf16[128,640]{1,0:T(8,128)(2,1)S(1)} %get-tuple-element.45.refs_2_, ...), custom_call_target="tpu_custom_call" | custom-call | tf_op jit(solution)/shard_map/pallas_call | solution.py:53
  91.6 1.5 %collective-permute-start.9 = (bf16[256,512]{1,0:T(8,128)(2,1)S(1)}, bf16[256,512]{1,0:T(8,128)(2,1)S(1)}, u32[]{:S(2)}, u32[]{:S(2)}) collective-permute-start(bf16[256,512]{1,0:T(8,128)(2,1)S(1)} %get-tuple-element.48), channel_id=1, source_target_pairs={{0,1},{1,0},{2,3},{3,2},{4,5},{5,4},{6,7},{7,6},{8,9},{9,8},{10,11... | collective-permute-start | bytes 786440 | tf_op jit(solution)/shard_map/ppermute | solution.py:421
  93.1 1.2 %collective-permute-done.9.theirs = bf16[256,512]{1,0:T(8,128)(2,1)S(1)} collective-permute-done((bf16[256,512]{1,0:T(8,128)(2,1)S(1)}, bf16[256,512]{1,0:T(8,128)(2,1)S(1)}, u32[]{:S(2)}, u32[]{:S(2)}) %collective-permute-start.9) | collective-permute-done | bytes 262176 | tf_op jit(solution)/shard_map/ppermute | solution.py:421
  94.2 1.3 %shard_map.46 = bf16[256,1024]{1,0:T(8,128)(2,1)} custom-call(s32[8]{0:T(128)S(1)} %stack.51.s, bf16[256,512]{1,0:T(8,128)(2,1)S(1)} %get-tuple-element.47.mine, bf16[256,512]{1,0:T(8,128)(2,1)S(1)} %collective-permute-done.9.theirs), custom_call_target="tpu_custom_call" | custom-call | tf_op jit(solution)/shard_map/pallas_call | solution.py:387
Async XLA Ops:
  0.0 2.4 %collective-permute-start = (bf16[256,1024]{1,0:T(8,128)(2,1)}, bf16[256,1024]{1,0:T(8,128)(2,1)S(1)}, u32[]{:S(2)}, u32[]{:S(2)}) collective-permute-start(bf16[256,1024]{1,0:T(8,128)(2,1)} %refs_1_.5), channel_id=1, source_target_pairs={{0,1},{1,0},{2,3},{3,2},{4,5},{5,4},{6,7},{7,6},{8,9},{9,8},{10,11... | collective-permute-start | bytes 1572872 | tf_op jit(solution)/shard_map/ppermute | solution.py:421
  0.7 2.5 %collective-permute-start.1 = (bf16[256,1024]{1,0:T(8,128)(2,1)}, bf16[256,1024]{1,0:T(8,128)(2,1)S(1)}, u32[]{:S(2)}, u32[]{:S(2)}) collective-permute-start(bf16[256,1024]{1,0:T(8,128)(2,1)} %refs_2_.3), channel_id=1, source_target_pairs={{0,1},{1,0},{2,3},{3,2},{4,5},{5,4},{6,7},{7,6},{8,9},{9,8},{10,11... | collective-permute-start | bytes 1572872 | tf_op jit(solution)/shard_map/ppermute | solution.py:421
  0.7 6.6 %collective-permute-start.2 = (bf16[256,1024]{1,0:T(8,128)(2,1)}, bf16[256,1024]{1,0:T(8,128)(2,1)S(1)}, u32[]{:S(2)}, u32[]{:S(2)}) collective-permute-start(bf16[256,1024]{1,0:T(8,128)(2,1)} %refs_0_.7), channel_id=1, source_target_pairs={{0,1},{1,0},{2,3},{3,2},{4,5},{5,4},{6,7},{7,6},{8,9},{9,8},{10,11... | collective-permute-start | bytes 1572872 | tf_op jit(solution)/shard_map/ppermute | solution.py:421
  3.2 1.0 %copy-start = (bf16[256,1024]{1,0:T(8,128)(2,1)S(1)}, bf16[256,1024]{1,0:T(8,128)(2,1)}, u32[]{:S(2)}) copy-start(bf16[256,1024]{1,0:T(8,128)(2,1)} %refs_1_.5) | copy-start | bytes 1572868
  4.2 1.0 %copy-start.2 = (bf16[256,1024]{1,0:T(8,128)(2,1)S(1)}, bf16[256,1024]{1,0:T(8,128)(2,1)}, u32[]{:S(2)}) copy-start(bf16[256,1024]{1,0:T(8,128)(2,1)} %refs_2_.3) | copy-start | bytes 1572868
  5.3 2.0 %copy-start.1 = (bf16[256,1024]{1,0:T(8,128)(2,1)S(1)}, bf16[256,1024]{1,0:T(8,128)(2,1)}, u32[]{:S(2)}) copy-start(bf16[256,1024]{1,0:T(8,128)(2,1)} %refs_1_.5) | copy-start | bytes 1572868
  5.3 2.0 %copy-start.4 = (bf16[256,1024]{1,0:T(8,128)(2,1)S(1)}, bf16[256,1024]{1,0:T(8,128)(2,1)}, u32[]{:S(2)}) copy-start(bf16[256,1024]{1,0:T(8,128)(2,1)} %refs_0_.7) | copy-start | bytes 1572868
  6.3 0.9 copy-start.9
  7.2 1.5 %copy-start.8 = (bf16[768,512]{1,0:T(8,128)(2,1)}, bf16[768,512]{1,0:T(8,128)(2,1)S(1)}, u32[]{:S(2)}) copy-start(bf16[768,512]{1,0:T(8,128)(2,1)S(1)} %get-tuple-element.32) | copy-start | bytes 2359300
  8.7 0.8 copy-start.7
  9.5 17.8 %copy-start.3 = (bf16[256,1024]{1,0:T(8,128)(2,1)S(1)}, bf16[256,1024]{1,0:T(8,128)(2,1)}, u32[]{:S(2)}) copy-start(bf16[256,1024]{1,0:T(8,128)(2,1)} %refs_2_.3) | copy-start | bytes 1572868
  9.5 24.7 %all-to-all-start = ((bf16[8,224,128]{2,1,0:T(8,128)(2,1)}), bf16[8,224,128]{2,1,0:T(8,128)(2,1)}, u32[]{:S(2)}, u32[]{:S(2)}) async-start(bf16[8,224,128]{2,1,0:T(8,128)(2,1)} %copy-done.7), calls=%async_computation | async-start | bytes 917504 | tf_op jit(solution)/shard_map/all_to_all | solution.py:429
  17.8 32.3 %collective-permute-start.3 = (bf16[768,512]{1,0:T(8,128)(2,1)}, bf16[768,512]{1,0:T(8,128)(2,1)}, u32[]{:S(2)}, u32[]{:S(2)}) collective-permute-start(bf16[768,512]{1,0:T(8,128)(2,1)} %copy-done.9), channel_id=1, source_target_pairs={{0,2},{1,3},{2,4},{3,5},{4,6},{5,7},{6,8},{7,9},{8,10},{9,11},{10,... | collective-permute-start | bytes 2359304 | tf_op jit(solution)/shard_map/ppermute | solution.py:421
  21.2 28.9 %collective-permute-start.4 = (bf16[768,512]{1,0:T(8,128)(2,1)}, bf16[768,512]{1,0:T(8,128)(2,1)}, u32[]{:S(2)}, u32[]{:S(2)}) collective-permute-start(bf16[768,512]{1,0:T(8,128)(2,1)} %copy-done.8), channel_id=1, source_target_pairs={{2,0},{3,1},{4,2},{5,3},{6,4},{7,5},{8,6},{9,7},{10,8},{11,9},{12,... | collective-permute-start | bytes 2359304 | tf_op jit(solution)/shard_map/ppermute | solution.py:421
  29.9 0.8 copy-start.5
  35.2 23.0 %copy-start.6 = (bf16[512,640]{1,0:T(8,128)(2,1)S(1)}, bf16[512,640]{1,0:T(8,128)(2,1)}, u32[]{:S(2)}) copy-start(bf16[512,640]{1,0:T(8,128)(2,1)} %copy-done.5) | copy-start | bytes 1966084
  51.9 12.5 %collective-permute-start.6 = (bf16[256,512]{1,0:T(8,128)(2,1)S(1)}, bf16[256,512]{1,0:T(8,128)(2,1)S(1)}, u32[]{:S(2)}, u32[]{:S(2)}) collective-permute-start(bf16[256,512]{1,0:T(8,128)(2,1)S(1)} %get-tuple-element.33), channel_id=1, source_target_pairs={{2,4},{3,5},{4,2},{5,3},{6,8},{7,9},{8,6},{9,7},{10,12},{11,13},{1... | collective-permute-start | bytes 786440 | tf_op jit(solution)/shard_map/ppermute | solution.py:421
  56.2 15.6 %collective-permute-start.8 = (bf16[1024,128]{1,0:T(8,128)(2,1)S(1)}, bf16[1024,128]{1,0:T(8,128)(2,1)S(1)}, u32[]{:S(2)}, u32[]{:S(2)}) collective-permute-start(bf16[1024,128]{1,0:T(8,128)(2,1)S(1)} %shard_map.40), channel_id=1, source_target_pairs={{0,16},{1,17},{2,18},{3,19},{4,20},{5,21},{6,22},{7,23},{16,32},{1... | collective-permute-start | bytes 786440 | tf_op jit(solution)/shard_map/ppermute | solution.py:421
  58.1 5.6 %collective-permute-start.5 = (bf16[128,512]{1,0:T(8,128)(2,1)S(1)}, bf16[128,512]{1,0:T(8,128)(2,1)S(1)}, u32[]{:S(2)}, u32[]{:S(2)}) collective-permute-start(bf16[128,512]{1,0:T(8,128)(2,1)S(1)} %get-tuple-element.39.refs_0_), channel_id=1, source_target_pairs={{0,2},{1,3},{2,0},{3,1},{4,6},{5,7},{6,4},{7,5},{8,10},{9,11},{10,... | collective-permute-start | bytes 393224 | tf_op jit(solution)/shard_map/ppermute | solution.py:421
  74.4 14.4 %all-to-all-start.1 = ((bf16[8,112,128]{2,1,0:T(8,128)(2,1)}), bf16[8,112,128]{2,1,0:T(8,128)(2,1)S(1)}, u32[]{:S(2)}, u32[]{:S(2)}) async-start(bf16[8,112,128]{2,1,0:T(8,128)(2,1)} %shard_map.44), calls=%async_computation.1 | async-start | bytes 458752 | tf_op jit(solution)/shard_map/all_to_all | solution.py:429
  77.8 10.3 %collective-permute-start.7 = (bf16[128,640]{1,0:T(8,128)(2,1)S(1)}, bf16[128,640]{1,0:T(8,128)(2,1)S(1)}, u32[]{:S(2)}, u32[]{:S(2)}) collective-permute-start(bf16[128,640]{1,0:T(8,128)(2,1)S(1)} %get-tuple-element.46), channel_id=1, source_target_pairs={{0,2},{1,3},{2,0},{3,1},{4,6},{5,7},{6,4},{7,5},{8,10},{9,11},{10,... | collective-permute-start | bytes 491528 | tf_op jit(solution)/shard_map/ppermute | solution.py:421
  91.6 2.6 %collective-permute-start.9 = (bf16[256,512]{1,0:T(8,128)(2,1)S(1)}, bf16[256,512]{1,0:T(8,128)(2,1)S(1)}, u32[]{:S(2)}, u32[]{:S(2)}) collective-permute-start(bf16[256,512]{1,0:T(8,128)(2,1)S(1)} %get-tuple-element.48), channel_id=1, source_target_pairs={{0,1},{1,0},{2,3},{3,2},{4,5},{5,4},{6,7},{7,6},{8,9},{9,8},{10,11... | collective-permute-start | bytes 786440 | tf_op jit(solution)/shard_map/ppermute | solution.py:421

commit v2 on v1

--- a/solution.py
+++ b/solution.py
@@ -23,44 +23,56 @@
 ROWS4, ROWS3 = 32, 64
 SEND = 3 * ROWS4 + 2 * ROWS3
 BACK = ROWS4 + ROWS3 + 16
-VMEM_LIMIT = 24 * 2**20
+VMEM_LIMIT = 10 * 2**20
 
 
 def shaped(*shape):
     return jax.ShapeDtypeStruct(shape, BF16)
 
 
-def call(body, outs, scalars, arrays, halves=0, extra=()):
+def call(body, outs, scalars, arrays, wide=(), extra=(), slow=False):
     def outer(s, *refs):
-        whole, rest = refs[:halves], list(refs[halves:])
-        if halves:
-            *rest, held, sems = rest
-            start = pl.multiple_of(s[0] * COLS, COLS)
-            copies = [
-                pltpu.make_async_copy(ref.at[:, pl.ds(start, COLS)], held.at[i], sems.at[i])
-                for i, ref in enumerate(whole)
-            ]
-            for copy in copies:
-                copy.start()
-            for copy in copies:
-                copy.wait()
-            rest = [held.at[i] for i in range(halves)] + rest
-        body(s, *rest)
-
-    scratch = list(extra)
-    if halves:
-        scratch += [pltpu.VMEM((halves, B, COLS), BF16), pltpu.SemaphoreType.DMA((halves,))]
+        start = pl.multiple_of(s[0] * COLS, COLS)
+        refs = [
+            ref.at[:, pl.ds(start, COLS)] if i in wide else ref for i, ref in enumerate(refs)
+        ]
+        body(s, *refs)
+
     return pl.pallas_call(
         outer,
-        out_shape=outs,
+        out_shape=[pltpu.HBM(o.shape, o.dtype) for o in outs] if slow else outs,
         in_specs=[pl.BlockSpec(memory_space=pltpu.SMEM)]
-        + [pl.BlockSpec(memory_space=pl.ANY)] * halves
-        + [pl.BlockSpec(memory_space=pltpu.VMEM)] * (len(arrays) - halves),
-        out_specs=[pl.BlockSpec(memory_space=pltpu.VMEM)] * len(outs),
-        scratch_shapes=scratch,
+        + [pl.BlockSpec(memory_space=pltpu.VMEM)] * len(arrays),
+        out_specs=[pl.BlockSpec(memory_space=pltpu.HBM if slow else pltpu.VMEM)] * len(outs),
+        scratch_shapes=list(extra),
         compiler_params=pltpu.CompilerParams(vmem_limit_bytes=VMEM_LIMIT),
         cost_estimate=pl.CostEstimate(flops=0, bytes_accessed=0, transcendentals=0),
     )(scalars, *arrays)
+
+
+def half_body(s, q, k, v, out, sems):
+    start = pl.multiple_of(s[0] * COLS, COLS)
+    copies = [
+        pltpu.make_async_copy(ref.at[:, pl.ds(start, COLS)], out.at[i], sems.at[i])
+        for i, ref in enumerate((q, k, v))
+    ]
+    for copy in copies:
+        copy.start()
+    for copy in copies:
+        copy.wait()
+
+
+def half_columns(s, arrays):
+    return pl.pallas_call(
+        half_body,
+        out_shape=shaped(3, B, COLS),
+        in_specs=[pl.BlockSpec(memory_space=pltpu.SMEM)]
+        + [pl.BlockSpec(memory_space=pltpu.HBM)] * 3,
+        out_specs=pl.BlockSpec(memory_space=pltpu.VMEM),
+        scratch_shapes=[pltpu.SemaphoreType.DMA((3,))],
+        compiler_params=pltpu.CompilerParams(vmem_limit_bytes=VMEM_LIMIT),
+        cost_estimate=pl.CostEstimate(flops=0, bytes_accessed=0, transcendentals=0),
+    )(s, *(pltpu.with_memory_space_constraint(x, pltpu.HBM) for x in arrays))
 
 
 def pool_matrix(rows, width, level, scale):
@@ -170,39 +182,47 @@
     out_ref[row : row + rows, COLS:] = tile_of(values)
 
 
-def edge_body(s, k0, v0, k1, v1, rpay, lpay):
-    low_first = s[0] == 0
-    for n, pair in enumerate(((k0, k1), (v0, v1))):
-        low = jnp.where(low_first, pair[0][...], pair[1][...])
-        high = jnp.where(low_first, pair[1][...], pair[0][...])
-        rpay[n * B : (n + 1) * B] = high
-        lpay[n * B : (n + 1) * B] = low
-        rows = slice(2 * B + n * 128, 2 * B + (n + 1) * 128)
-        rpay[rows] = pooled(low, 1, n == 0)
-        lpay[rows] = pooled(high, 1, n == 0)
-
-
-def pool_body(s, q0, k0, v0, q1, k1, v1, q_one, q_two, apay):
+def edge_body(s, own, k1, v1, rout, lout, rpay, lpay, sems):
+    copies = []
+    for i, (pay, out) in enumerate(((rpay, rout), (lpay, lout))):
+        first = s[0] == 1 - i
+        for n, ref in enumerate((k1, v1)):
+            mine, other = own[1 + n], ref[...]
+            pay[n * B : (n + 1) * B] = jnp.where(first, mine, other)
+            pay[2 * B + n * 128 : 2 * B + (n + 1) * 128] = pooled(
+                jnp.where(first, other, mine), 1, n == 0
+            )
+        copies.append(pltpu.make_async_copy(pay, out, sems.at[i]))
+        copies[-1].start()
+    for copy in copies:
+        copy.wait()
+
+
+def pair_pay_body(s, own, q1, q_two):
+    q_two[:64] = pooled(own[0], 2, True)
+    q_two[64:] = pooled(q1[...], 2, True)
+
+
+def pool_body(s, own, q1, k1, v1, apay):
     half = s[1]
-    for at, refs in enumerate(((q0, k0, v0), (q1, k1, v1))):
-        q = refs[0][...]
-        q_one[at * 128 : (at + 1) * 128] = pooled(q, 1, True)
-        q_two[at * 64 : (at + 1) * 64] = pooled(q, 2, True)
-        three = [pooled(ref[...], 3, n < 2) for n, ref in enumerate(refs)]
-        four = [pooled(ref[...], 4, n < 2) for n, ref in enumerate(refs)]
+    for at in (0, 1):
+        whole = (own[0], own[1], own[2]) if at == 0 else (q1[...], k1[...], v1[...])
+        three = [pooled(x, 3, n < 2) for n, x in enumerate(whole)]
+        four = [pooled(x, 4, n < 2) for n, x in enumerate(whole)]
         for j in range(RING):
             cols = slice((j % HEADS) * DH, (j % HEADS + 1) * DH)
             for n in range(3):
                 apay[j, n * ROWS4 + at * 16 : n * ROWS4 + (at + 1) * 16] = four[n][:, cols]
-            first = jnp.where(half == j // HEADS, three[0][:, cols], three[1][:, cols])
+            first = jnp.where(half == j // HEADS, three[1][:, cols], three[0][:, cols])
             base = 3 * ROWS4
             apay[j, base + at * 32 : base + (at + 1) * 32] = first
             base += ROWS3
             apay[j, base + at * 32 : base + (at + 1) * 32] = three[2][:, cols]
 
 
-def near_body(s, q0, k0, v0, q1, k1, v1, out):
-    for at, q in enumerate((q0, q1)):
+def near_body(s, own, q1, k1, v1, out):
+    k0, v0 = own.at[1], own.at[2]
+    for at, q in enumerate((own.at[0], q1)):
         attend_to(
             out,
             at * B,
@@ -213,29 +233,32 @@
         )
 
 
-def derive_body(s, rin, lin, bpay, kept):
+def level_two(ref, n):
+    near = pooled(ref[n * B : (n + 1) * B], 2, n == 0)
+    far = pooled(ref[2 * B + n * 128 : 2 * B + (n + 1) * 128], 1, n == 0)
+    return jnp.concatenate([near, far], axis=0)
+
+
+def derive_body(s, rin, lin, bpay):
     odd = s[7] == 1
     for n in (0, 1):
-        sides = []
-        for ref in (rin, lin):
-            near = pooled(ref[n * B : (n + 1) * B], 2, n == 0)
-            far = pooled(ref[2 * B + n * 128 : 2 * B + (n + 1) * 128], 1, n == 0)
-            sides.append((near, far))
-        for i in (0, 1):
-            rows = slice(n * 128 + i * 64, n * 128 + (i + 1) * 64)
-            bpay[rows] = jnp.where(odd, sides[0][i], sides[1][i])
-            kept[rows] = jnp.where(odd, sides[1][i], sides[0][i])
-
-
-def far_body(s, q0, q1, q_one, near, rin, lin, out, tile, out0, out1):
+        bpay[n * 128 : (n + 1) * 128] = jnp.where(odd, level_two(rin, n), level_two(lin, n))
+
+
+def sides(s):
+    left = jnp.where(s[2] == 1, 0.0, ABSENT).astype(F32)
+    right = jnp.where(s[3] == 1, 0.0, ABSENT).astype(F32)
+    return left, right
+
+
+def far_body(s, own, q1, rin, lin, out):
     first = s[0] == 0
-    bias_left = jnp.where(s[2] == 1, 0.0, ABSENT).astype(F32)
-    bias_right = jnp.where(s[3] == 1, 0.0, ABSENT).astype(F32)
-    for at, q in enumerate((q0, q1)):
+    bias_left, bias_right = sides(s)
+    for at, q in enumerate((own.at[0], q1)):
         left = first if at == 0 else jnp.logical_not(first)
         bias = jnp.where(left, bias_left, bias_right)
         attend_to(
-            out0,
+            out,
             at * B,
             lambda cols: q[:, cols],
             lambda cols: [
@@ -249,9 +272,11 @@
             1.0,
         )
 
+
+def one_body(s, own, q1, near, far, rin, lin, out, one):
     def coarse(cols):
         parts = []
-        for ref, bias in ((rin, bias_left), (lin, bias_right)):
+        for ref, bias in zip((rin, lin), sides(s)):
             keys = pooled(ref[:B, cols], 1, True)
             values = pooled(ref[B : 2 * B, cols], 1, False)
             keys = jnp.concatenate([keys, ref[2 * B : 2 * B + 128, cols]], axis=0)
@@ -259,30 +284,36 @@
             parts.append((keys, values, bias))
         return parts
 
-    attend_to(out1, 0, lambda cols: q_one[:, cols], coarse, B, 2.0)
+    q_one = jnp.concatenate([pooled(own[0], 1, True), pooled(q1[...], 1, True)], axis=0)
+    attend_to(one, 0, lambda cols: q_one[:, cols], coarse, B, 2.0)
     for at in (0, 1):
         rows = slice(at * B, (at + 1) * B)
-        one = spread(out1[at * 128 : (at + 1) * 128], B, 1)
-        outs, weights = merged([unpacked(near[rows]), unpacked(out0[rows]), one])
+        level_one = spread(one[at * 128 : (at + 1) * 128], B, 1)
+        outs, weights = merged([unpacked(near[rows]), unpacked(far[rows]), level_one])
         for h in range(HEADS):
             out[rows, h * DH : (h + 1) * DH] = outs[h]
-        tile[rows] = weights
-
-
-def pair_body(s, q_two, kept, pin, bin_, mine, theirs):
+        out[rows, COLS:] = weights
+
+
+def pair_body(s, q_two, rin, lin, pin, bin_, mine, theirs):
     bias = jnp.where(s[4] == 1, 0.0, ABSENT).astype(F32)
+    odd = s[7] == 1
+    kept = [
+        jnp.concatenate(
+            [
+                jnp.where(odd, level_two(lin, n), level_two(rin, n)),
+                bin_[n * 128 : (n + 1) * 128],
+            ],
+            axis=0,
+        )
+        for n in (0, 1)
+    ]
     for out, ref in ((mine, q_two), (theirs, pin)):
         attend_to(
             out,
             0,
             lambda cols: ref[:, cols],
-            lambda cols: [
-                (
-                    jnp.concatenate([kept[:128, cols], bin_[:128, cols]], axis=0),
-                    jnp.concatenate([kept[128:, cols], bin_[128:, cols]], axis=0),
-                    bias,
-                ),
-            ],
+            lambda cols: [(kept[0][:, cols], kept[1][:, cols], bias)],
             128,
             4.0,
             4,
@@ -290,7 +321,7 @@
 
 
 def row_pay_body(s, ain, xpay):
-    other = (1 - s[1]) * HEADS
+    same = s[1] * HEADS
     for j in range(RING):
         xpay[j * ROWS4 : (j + 1) * ROWS4] = ain[j, ROWS4 : 2 * ROWS4]
         xpay[B + j * ROWS4 : B + (j + 1) * ROWS4] = ain[j, 2 * ROWS4 : 3 * ROWS4]
@@ -298,7 +329,7 @@
         for n in (0, 1):
             base = 3 * ROWS4 + n * ROWS3
             to = (2 + n) * B + j * ROWS3
-            xpay[to : to + ROWS3] = ain[other + j, base : base + ROWS3]
+            xpay[to : to + ROWS3] = ain[same + j, base : base + ROWS3]
 
 
 def row_body(s, ain, xin, back):
@@ -312,10 +343,10 @@
     q4 = jnp.concatenate([ain[j, :ROWS4] for j in range(RING)], axis=0)
     ((o4, value4),) = attend([(q4, [(xin[:B], xin[B : 2 * B], bias)])], 16.0)
     parts = [
-        (rows3(other, base), rows3(other, base + ROWS3), None),
+        (rows3(mine, base), rows3(mine, base + ROWS3), None),
         (xin[2 * B : 3 * B], xin[3 * B :], bias),
     ]
-    ((o3, value3),) = attend([(rows3(mine, base), parts)], 8.0)
+    ((o3, value3),) = attend([(rows3(other, base), parts)], 8.0)
     row = lax.broadcasted_iota(jnp.int32, (ROWS4 + ROWS3, 128), 0)
     col = lax.broadcasted_iota(jnp.int32, (ROWS4 + ROWS3, 128), 1)
     term = lax.broadcasted_iota(jnp.int32, (16, 128), 0)
@@ -335,8 +366,8 @@
         back[j, ROWS4 + ROWS3 :] = three.astype(BF16)
 
 
-def merge_body(s, fine, tile, two, two_back, row_back, mine, send):
-    low = s[1] * HEADS
+def merge_body(s, fine, two, two_back, row_back, mine, send):
+    low = (1 - s[1]) * HEADS
     row = lax.broadcasted_iota(jnp.int32, (ROWS4 + ROWS3, 128), 0)
     lane = lax.broadcasted_iota(jnp.int32, (ROWS4 + ROWS3, 128), 1)
 
@@ -364,7 +395,7 @@
     for at, out in enumerate((mine, send)):
         rows = slice(at * B, (at + 1) * B)
         outs, _ = merged(
-            [(fine[rows], tile[rows]), spread(coarse[at * 64 : (at + 1) * 64], B, 2)]
+            [(fine[rows, :COLS], fine[rows, COLS:]), spread(coarse[at * 64 : (at + 1) * 64], B, 2)]
         )
         for h in range(HEADS):
             out[:, h * DH : (h + 1) * DH] = outs[h].astype(BF16)
@@ -409,7 +440,7 @@
 LEFT = pairs_of(lambda chip: chip - 1)
 PAIR = pairs_of(lambda chip: chip ^ 1)
 BOUND = pairs_of(lambda chip: chip + 1 if chip % 2 else chip - 1)
-ROW = pairs_of(lambda chip: chip + RING if chip % RING < RING // 2 else chip - RING)
+ROW = pairs_of(lambda chip: chip - RING if chip % RING < RING // 2 else chip + RING)
 LINES = [
     [2 * (row * RING + z) + core for z in range(RING)]
     for row in range(CHIPS // RING)
@@ -440,54 +471,59 @@
     has_left = chip >= 1
     has_right = chip <= CHIPS - 2
     has_pair = jnp.where(odd == 1, chip <= CHIPS - 3, chip >= 2)
-    has_row = jnp.where(half == 0, row >= 1, row <= CHIPS // RING - 2)
+    has_row = jnp.where(half == 1, row >= 1, row <= CHIPS // RING - 2)
     s = jnp.stack(
         [core, half, has_left, has_right, has_pair, z % HEADS, has_row, odd]
     ).astype(jnp.int32)
 
-    own = (query_rows, key_rows, value_rows)
-    got = [None, send_to(key_rows, SWAP), send_to(value_rows, SWAP)]
-    got[0] = send_to(query_rows, SWAP)
-    fine = (*own, *got)
+    own = half_columns(s, (query_rows, key_rows, value_rows))
+    q1, k1, v1 = [send_to(x, SWAP) for x in (query_rows, key_rows, value_rows)]
+    (apay,) = call(pool_body, (shaped(RING, SEND, DH),), s, (own, q1, k1, v1), wide=(1, 2, 3))
+    ain = line_swap(apay)
+    s, _ = after(s, apay)
+    pay = shaped(3 * B, COLS)
     rpay, lpay = call(
-        edge_body, (shaped(3 * B, COLS), shaped(3 * B, COLS)), s, (*own[1:], *got[1:]), halves=4
+        edge_body,
+        (pay, pay),
+        s,
+        (own, k1, v1),
+        wide=(1, 2),
+        extra=[pltpu.VMEM(pay.shape, BF16)] * 2 + [pltpu.SemaphoreType.DMA((2,))],
+        slow=True,
     )
     rin = send_to(rpay, RIGHT)
     lin = send_to(lpay, LEFT)
-    s, rpay = after(s, rpay)
-    outs = (shaped(B, COLS), shaped(128, COLS), shaped(RING, SEND, DH))
-    q_one, q_two, apay = call(pool_body, outs, s, fine, halves=6)
-    ain = line_swap(apay)
-    pin = send_to(q_two, PAIR)
-    (near,) = call(near_body, (shaped(2 * B, PACK),), s, fine, halves=6)
-    s, near = after(s, near)
+    s, _ = after(s, (rpay, lpay))
     (xpay,) = call(row_pay_body, (shaped(4 * B, DH),), s, (ain,))
     xin = send_to(xpay, ROW)
     s, _ = after(s, xpay)
-    bpay, kept = call(derive_body, (shaped(B, COLS), shaped(B, COLS)), s, (rin, lin))
+    (near,) = call(near_body, (shaped(2 * B, PACK),), s, (own, q1, k1, v1), wide=(1, 2, 3))
+    (q_two,) = call(pair_pay_body, (shaped(128, COLS),), s, (own, q1), wide=(1,))
+    pin = send_to(q_two, PAIR)
+    s, _ = after(s, (near, q_two))
+    (back,) = call(row_body, (shaped(RING, BACK, DH),), s, (ain, xin))
+    row_back = line_swap(back)
+    s, _ = after(s, back)
+    (bpay,) = call(derive_body, (shaped(B, COLS),), s, (rin, lin))
     bin_ = send_to(bpay, BOUND)
     s, _ = after(s, bpay)
-    far, far_tile = call(
-        far_body,
-        (jax.ShapeDtypeStruct((2 * B, COLS), F32), jax.ShapeDtypeStruct((2 * B, 128), F32)),
-        s,
-        (query_rows, got[0], q_one, near, rin, lin),
-        halves=2,
-        extra=[pltpu.VMEM((2 * B, PACK), BF16), pltpu.VMEM((B, PACK), BF16)],
-    )
-    s, far = after(s, far)
+    (far,) = call(far_body, (shaped(2 * B, PACK),), s, (own, q1, rin, lin), wide=(1,))
+    s, _ = after(s, (far, row_back))
     two, theirs = call(
-        pair_body, (shaped(128, PACK), shaped(128, PACK)), s, (q_two, kept, pin, bin_)
+        pair_body, (shaped(128, PACK), shaped(128, PACK)), s, (q_two, rin, lin, pin, bin_)
     )
     two_back = send_to(theirs, PAIR)
-    s, two = after(s, two)
-    (back,) = call(row_body, (shaped(RING, BACK, DH),), s, (ain, xin))
-    row_back = line_swap(back)
+    s, _ = after(s, theirs)
+    (fine,) = call(
+        one_body,
+        (jax.ShapeDtypeStruct((2 * B, PACK), F32),),
+        s,
+        (own, q1, near, far, rin, lin),
+        wide=(1,),
+        extra=[pltpu.VMEM((B, PACK), BF16)],
+    )
     mine, send = call(
-        merge_body,
-        (shaped(B, COLS), shaped(B, COLS)),
-        s,
-        (far, far_tile, two, two_back, row_back),
+        merge_body, (shaped(B, COLS), shaped(B, COLS)), s, (fine, two, two_back, row_back)
     )
     return join(s, mine, send_to(send, SWAP))
 

time: 96.4 us -> 81.2 us (0.84)
  waiting for transfers between devices: 37.8 us -> 12.7 us
  starting transfers between devices: 31.5 us -> 38 us
  Pallas kernels: 21.4 us -> 26.7 us
  local copies, waits for them, and re-layouts: 4.66 us -> 2.82 us
    ppermute x10, waiting for transfers between devices: 33.6 us -> 7.86 us  [send_to(): return lax.ppermute(x, 'seq', pairs)]
    ppermute x10, starting transfers between devices: 19.8 us -> 25.8 us  [send_to(): return lax.ppermute(x, 'seq', pairs)]
    pallas_call x9 -> x12, Pallas kernels: 20.1 us -> 25.4 us  [the longest x11 23.7 us: call(): pl.pallas_call(outer, out_shape=[pltpu.HBM(o.shape, o.dtype) for o in out...]
    unnamed x20 -> x12, local copies, waits for them, and re-layouts: 4.58 us -> 2.74 us
  transfers between devices with their start and end apart: 12 -> 12, of which waited for: 9 -> 7; matrix products, arithmetic and copies ran while one was open for 0% -> 0% of each run, Pallas kernels for 12% -> 22%
where the time goes in v2:
time: 81.2 us; the launch traced here: 80.6 us
  starting transfers between devices  38 us (47%)
  Pallas kernels  26.7 us (33%)
  waiting for transfers between devices  12.7 us (16%)
  local copies, waits for them, and re-layouts  2.82 us (3%)
    ppermute x10, starting transfers between devices, send_to(): return lax.ppermute(x, 'seq', pairs)  25.8 us
    pallas_call x11, Pallas kernels, call(): pl.pallas_call(outer, out_shape=[pltpu.HBM(o.shape, o.dtype) for o in out...  23.7 us
    all_to_all x2, starting transfers between devices, line_swap(): return lax.all_to_all(x, 'seq', 0, 0, axis_index_groups=LINES)  12.2 us
    ppermute x10, waiting for transfers between devices, send_to(): return lax.ppermute(x, 'seq', pairs)  7.86 us
    all_to_all x2, waiting for transfers between devices, line_swap(): return lax.all_to_all(x, 'seq', 0, 0, axis_index_groups=LINES)  4.85 us
    unnamed x12, local copies, waits for them, and re-layouts  2.74 us
    pallas_call x1, Pallas kernels, half_columns(): pl.pallas_call(half_body, out_shape=shaped(3, B, COLS), in_specs=[pl.Bloc...  1.68 us
  transfers between devices with their start and end apart: 12, of which 7 were waited for; matrix products, arithmetic and copies ran while one was open for 0% of the time, Pallas kernels for 22%

profile of v2, /device:TPU:25, one launch (start us, length us, event | category | flops | bytes accessed | tf_op | source)
XLA Modules:
  0.0 80.6 jit_solution(10234986597438342882)
XLA Ops:
  0.0 0.7 collective-permute-start
  0.7 0.0 collective-permute-start.1
  0.7 0.5 collective-permute-start.2
  1.2 0.1 stack.51.s
  1.3 1.7 %shard_map.37.refs_0_ = bf16[3,256,512]{2,1,0:T(8,128)(2,1)S(1)} custom-call(s32[8]{0:T(128)S(1)} %stack.51.s, bf16[256,1024]{1,0:T(8,128)(2,1)} %q.1, bf16[256,1024]{1,0:T(8,128)(2,1)} %k.1, bf16[256,1024]{1,0:T(8,128)(2,1)} %v.1), custom_call_target="tpu_custom_call" | custom-call | tf_op jit(solution)/shard_map/pallas_call | solution.py:66
  3.0 0.0 collective-permute-done.refs_1_
  3.0 0.2 collective-permute-done.1.refs_2_.refs_1_
  3.2 0.7 collective-permute-done.2.refs_3_.refs_2_
  3.9 0.0 copy-start
  3.9 1.9 %shard_map.38 = bf16[8,224,128]{2,1,0:T(8,128)(2,1)} custom-call(s32[8]{0:T(128)S(1)} %stack.51.s, bf16[3,256,512]{2,1,0:T(8,128)(2,1)S(1)} %shard_map.37.refs_0_, bf16[256,1024]{1,0:T(8,128)(2,1)S(1)} %collective-permute-done.refs_1_, bf16[256,1024]{1,0:T(8,128)(2,1)S(1)} %collective-permute-done.1.refs_2_.refs_1_, ...), custom_call_target="tpu_custom_call" | custom-call | tf_op jit(solution)/shard_map/pallas_call | solution.py:41
  5.9 8.2 %all-to-all-start = ((bf16[8,224,128]{2,1,0:T(8,128)(2,1)}), bf16[8,224,128]{2,1,0:T(8,128)(2,1)}, u32[]{:S(2)}, u32[]{:S(2)}) async-start(bf16[8,224,128]{2,1,0:T(8,128)(2,1)} %shard_map.38), calls=%async_computation | async-start | bytes 917504 | tf_op jit(solution)/shard_map/all_to_all | solution.py:460
  14.0 0.0 copy-done
  14.0 2.0 %shard_map.39 = (bf16[768,512]{1,0:T(8,128)(2,1)}, bf16[768,512]{1,0:T(8,128)(2,1)}) custom-call(s32[8]{0:T(128)S(1)} %stack.51.s, bf16[3,256,512]{2,1,0:T(8,128)(2,1)S(1)} %shard_map.37.refs_0_, bf16[256,1024]{1,0:T(8,128)(2,1)S(1)} %collective-permute-done.1.refs_2_.refs_1_, bf16[256,1024]{1,0:T(8,128)(2,1)S(1)} %collective-permute-done.2.refs_3_.refs_2_), custom_call_target="tpu_custom_call" | custom-call | tf_op jit(solution)/shard_map/pallas_call | solution.py:41
  16.1 3.4 %collective-permute-start.4 = (bf16[768,512]{1,0:T(8,128)(2,1)}, bf16[768,512]{1,0:T(8,128)(2,1)S(1)}, u32[]{:S(2)}, u32[]{:S(2)}) collective-permute-start(bf16[768,512]{1,0:T(8,128)(2,1)} %get-tuple-element.20), channel_id=1, source_target_pairs={{0,2},{1,3},{2,4},{3,5},{4,6},{5,7},{6,8},{7,9},{8,10},{9,11},{10,... | collective-permute-start | bytes 2359304 | tf_op jit(solution)/shard_map/ppermute | solution.py:452
  19.4 6.1 %collective-permute-start.5 = (bf16[768,512]{1,0:T(8,128)(2,1)}, bf16[768,512]{1,0:T(8,128)(2,1)S(1)}, u32[]{:S(2)}, u32[]{:S(2)}) collective-permute-start(bf16[768,512]{1,0:T(8,128)(2,1)} %get-tuple-element.21), channel_id=1, source_target_pairs={{2,0},{3,1},{4,2},{5,3},{6,4},{7,5},{8,6},{9,7},{10,8},{11,9},{12,... | collective-permute-start | bytes 2359304 | tf_op jit(solution)/shard_map/ppermute | solution.py:452
  25.6 4.8 %all-to-all-done.refs_0_ = bf16[8,224,128]{2,1,0:T(8,128)(2,1)} async-done(((bf16[8,224,128]{2,1,0:T(8,128)(2,1)}), bf16[8,224,128]{2,1,0:T(8,128)(2,1)}, u32[]{:S(2)}, u32[]{:S(2)}) %all-to-all-start) | async-done | bytes 458784 | tf_op jit(solution)/shard_map/all_to_all | solution.py:460
  30.4 1.0 %shard_map.40 = bf16[1024,128]{1,0:T(8,128)(2,1)S(1)} custom-call(s32[8]{0:T(128)S(1)} %stack.51.s, bf16[8,224,128]{2,1,0:T(8,128)(2,1)} %all-to-all-done.refs_0_), custom_call_target="tpu_custom_call" | custom-call | tf_op jit(solution)/shard_map/pallas_call | solution.py:41
  31.5 4.6 %collective-permute-start.3 = (bf16[1024,128]{1,0:T(8,128)(2,1)S(1)}, bf16[1024,128]{1,0:T(8,128)(2,1)S(1)}, u32[]{:S(2)}, u32[]{:S(2)}) collective-permute-start(bf16[1024,128]{1,0:T(8,128)(2,1)S(1)} %shard_map.40), channel_id=1, source_target_pairs={{8,24},{9,25},{10,26},{11,27},{12,28},{13,29},{14,30},{15,31},{16,... | collective-permute-start | bytes 786440 | tf_op jit(solution)/shard_map/ppermute | solution.py:452
  36.1 0.0 copy-start.1
  36.1 1.0 %copy-done.1 = bf16[256,1024]{1,0:T(8,128)(2,1)S(1)} copy-done((bf16[256,1024]{1,0:T(8,128)(2,1)S(1)}, bf16[256,1024]{1,0:T(8,128)(2,1)}, u32[]{:S(2)}) %copy-start.1) | copy-done | bytes 524312
  37.1 2.4 %shard_map.41.refs_2_ = bf16[512,640]{1,0:T(8,128)(2,1)S(1)} custom-call(s32[8]{0:T(128)S(1)} %stack.51.s, bf16[3,256,512]{2,1,0:T(8,128)(2,1)S(1)} %shard_map.37.refs_0_, bf16[256,1024]{1,0:T(8,128)(2,1)S(1)} %collective-permute-done.refs_1_, bf16[256,1024]{1,0:T(8,128)(2,1)S(1)} %collective-permute-done.1.refs_2_.refs_1_, bf16[256,1024]{1,0:T(8,128)(2,1)S(1)} %copy-done.1), custom_call_target="tpu_custom_call" | custom-call | tf_op jit(solution)/shard_map/pallas_call | solution.py:41
  39.5 0.0 copy-start.2
  39.5 0.8 %copy-done.2 = bf16[512,640]{1,0:T(8,128)(2,1)} copy-done((bf16[512,640]{1,0:T(8,128)(2,1)}, bf16[512,640]{1,0:T(8,128)(2,1)S(1)}, u32[]{:S(2)}) %copy-start.2) | copy-done | bytes 655384
  40.4 1.4 %shard_map.42.refs_0_ = bf16[128,512]{1,0:T(8,128)(2,1)} custom-call(s32[8]{0:T(128)S(1)} %stack.51.s, bf16[3,256,512]{2,1,0:T(8,128)(2,1)S(1)} %shard_map.37.refs_0_, bf16[256,1024]{1,0:T(8,128)(2,1)S(1)} %collective-permute-done.refs_1_), custom_call_target="tpu_custom_call" | custom-call | tf_op jit(solution)/shard_map/pallas_call | solution.py:41
  41.8 0.0 collective-permute-done.3.refs_1_
  41.8 2.6 %shard_map.43 = bf16[8,112,128]{2,1,0:T(8,128)(2,1)} custom-call(s32[8]{0:T(128)S(1)} %stack.51.s, bf16[8,224,128]{2,1,0:T(8,128)(2,1)} %all-to-all-done.refs_0_, bf16[1024,128]{1,0:T(8,128)(2,1)S(1)} %collective-permute-done.3.refs_1_), custom_call_target="tpu_custom_call" | custom-call | tf_op jit(solution)/shard_map/pallas_call | solution.py:41
  44.3 4.0 %all-to-all-start.1 = ((bf16[8,112,128]{2,1,0:T(8,128)(2,1)}), bf16[8,112,128]{2,1,0:T(8,128)(2,1)}, u32[]{:S(2)}, u32[]{:S(2)}) async-start(bf16[8,112,128]{2,1,0:T(8,128)(2,1)} %shard_map.43), calls=%async_computation.1 | async-start | bytes 458752 | tf_op jit(solution)/shard_map/all_to_all | solution.py:460
  48.4 0.0 collective-permute-done.4.refs_0_.refs_2_.refs_1_.refs_4_
  48.4 0.0 collective-permute-done.5.refs_1_.refs_3_.refs_2_.refs_5_
  48.4 1.6 %shard_map.44 = bf16[256,512]{1,0:T(8,128)(2,1)} custom-call(s32[8]{0:T(128)S(1)} %stack.51.s, bf16[768,512]{1,0:T(8,128)(2,1)S(1)} %collective-permute-done.4.refs_0_.refs_2_.refs_1_.refs_4_, bf16[768,512]{1,0:T(8,128)(2,1)S(1)} %collective-permute-done.5.refs_1_.refs_3_.refs_2_.refs_5_), custom_call_target="tpu_custom_call" | custom-call | tf_op jit(solution)/shard_map/pallas_call | solution.py:41
  50.0 7.6 %collective-permute-start.7 = (bf16[256,512]{1,0:T(8,128)(2,1)}, bf16[256,512]{1,0:T(8,128)(2,1)}, u32[]{:S(2)}, u32[]{:S(2)}) collective-permute-start(bf16[256,512]{1,0:T(8,128)(2,1)} %shard_map.44), channel_id=1, source_target_pairs={{2,4},{3,5},{4,2},{5,3},{6,8},{7,9},{8,6},{9,7},{10,12},{11,13},{1... | collective-permute-start | bytes 786440 | tf_op jit(solution)/shard_map/ppermute | solution.py:452
  57.7 0.1 collective-permute-start.6
  57.8 2.0 %shard_map.45.refs_3_ = bf16[512,640]{1,0:T(8,128)(2,1)S(1)} custom-call(s32[8]{0:T(128)S(1)} %stack.51.s, bf16[3,256,512]{2,1,0:T(8,128)(2,1)S(1)} %shard_map.37.refs_0_, bf16[256,1024]{1,0:T(8,128)(2,1)S(1)} %collective-permute-done.refs_1_, bf16[768,512]{1,0:T(8,128)(2,1)S(1)} %collective-permute-done.4.refs_0_.refs_2_.refs_1_.refs_4_, ...), custom_call_target="tpu_custom_call" | custom-call | tf_op jit(solution)/shard_map/pallas_call | solution.py:41
  59.8 0.0 copy-start.4
  59.8 0.9 %copy-done.4 = bf16[512,640]{1,0:T(8,128)(2,1)} copy-done((bf16[512,640]{1,0:T(8,128)(2,1)}, bf16[512,640]{1,0:T(8,128)(2,1)S(1)}, u32[]{:S(2)}) %copy-start.4) | copy-done | bytes 655384
  60.6 0.0 copy-start.3
  60.6 0.0 all-to-all-done.1.refs_3_
  60.6 0.0 copy-start.5
  60.6 1.5 %collective-permute-done.6.refs_3_ = bf16[128,512]{1,0:T(8,128)(2,1)} collective-permute-done((bf16[128,512]{1,0:T(8,128)(2,1)}, bf16[128,512]{1,0:T(8,128)(2,1)}, u32[]{:S(2)}, u32[]{:S(2)}) %collective-permute-start.6) | collective-permute-done | bytes 131104 | tf_op jit(solution)/shard_map/ppermute | solution.py:452
  62.2 3.4 %collective-permute-done.7.refs_4_ = bf16[256,512]{1,0:T(8,128)(2,1)} collective-permute-done((bf16[256,512]{1,0:T(8,128)(2,1)}, bf16[256,512]{1,0:T(8,128)(2,1)}, u32[]{:S(2)}, u32[]{:S(2)}) %collective-permute-start.7) | collective-permute-done | bytes 262176 | tf_op jit(solution)/shard_map/ppermute | solution.py:452
  65.5 2.2 %shard_map.46 = (bf16[128,640]{1,0:T(8,128)(2,1)S(1)}, bf16[128,640]{1,0:T(8,128)(2,1)S(1)}) custom-call(s32[8]{0:T(128)S(1)} %stack.51.s, bf16[128,512]{1,0:T(8,128)(2,1)} %shard_map.42.refs_0_, bf16[768,512]{1,0:T(8,128)(2,1)S(1)} %collective-permute-done.4.refs_0_.refs_2_.refs_1_.refs_4_, ...), custom_call_target="tpu_custom_call" | custom-call | tf_op jit(solution)/shard_map/pallas_call | solution.py:41
  67.7 0.3 collective-permute-start.8
  68.0 0.0 copy-done.3
  68.0 0.0 copy-done.5
  68.0 3.3 %shard_map.47.refs_0_ = f32[512,640]{1,0:T(8,128)S(1)} custom-call(s32[8]{0:T(128)S(1)} %stack.51.s, bf16[3,256,512]{2,1,0:T(8,128)(2,1)S(1)} %shard_map.37.refs_0_, bf16[256,1024]{1,0:T(8,128)(2,1)S(1)} %collective-permute-done.refs_1_, bf16[512,640]{1,0:T(8,128)(2,1)S(1)} %copy-done.3, bf16[512,640]{1,0:T(8,128)(2,1)S(1)} %copy-done.5, ...), custom_call_target="tpu_custom_call" | custom-call | tf_op jit(solution)/shard_map/pallas_call | solution.py:41
  71.3 0.8 %collective-permute-done.8.refs_2_ = bf16[128,640]{1,0:T(8,128)(2,1)S(1)} collective-permute-done((bf16[128,640]{1,0:T(8,128)(2,1)S(1)}, bf16[128,640]{1,0:T(8,128)(2,1)S(1)}, u32[]{:S(2)}, u32[]{:S(2)}) %collective-permute-start.8) | collective-permute-done | bytes 163872 | tf_op jit(solution)/shard_map/ppermute | solution.py:452
  72.2 3.2 %shard_map.48 = (bf16[256,512]{1,0:T(8,128)(2,1)S(1)}, bf16[256,512]{1,0:T(8,128)(2,1)S(1)}) custom-call(s32[8]{0:T(128)S(1)} %stack.51.s, f32[512,640]{1,0:T(8,128)S(1)} %shard_map.47.refs_0_, bf16[128,640]{1,0:T(8,128)(2,1)S(1)} %get-tuple-element.30.refs_1_, bf16[128,640]{1,0:T(8,128)(2,1)S(1)} %collective-permute-done.8.refs_2_, ...), custom_call_target="tpu_custom_call" | custom-call | tf_op jit(solution)/shard_map/pallas_call | solution.py:41
  75.4 2.6 %collective-permute-start.9 = (bf16[256,512]{1,0:T(8,128)(2,1)S(1)}, bf16[256,512]{1,0:T(8,128)(2,1)S(1)}, u32[]{:S(2)}, u32[]{:S(2)}) collective-permute-start(bf16[256,512]{1,0:T(8,128)(2,1)S(1)} %get-tuple-element.32), channel_id=1, source_target_pairs={{0,1},{1,0},{2,3},{3,2},{4,5},{5,4},{6,7},{7,6},{8,9},{9,8},{10,11... | collective-permute-start | bytes 786440 | tf_op jit(solution)/shard_map/ppermute | solution.py:452
  78.0 1.2 %collective-permute-done.9.theirs = bf16[256,512]{1,0:T(8,128)(2,1)S(1)} collective-permute-done((bf16[256,512]{1,0:T(8,128)(2,1)S(1)}, bf16[256,512]{1,0:T(8,128)(2,1)S(1)}, u32[]{:S(2)}, u32[]{:S(2)}) %collective-permute-start.9) | collective-permute-done | bytes 262176 | tf_op jit(solution)/shard_map/ppermute | solution.py:452
  79.1 1.3 %shard_map.49 = bf16[256,1024]{1,0:T(8,128)(2,1)} custom-call(s32[8]{0:T(128)S(1)} %stack.51.s, bf16[256,512]{1,0:T(8,128)(2,1)S(1)} %get-tuple-element.31.mine, bf16[256,512]{1,0:T(8,128)(2,1)S(1)} %collective-permute-done.9.theirs), custom_call_target="tpu_custom_call" | custom-call | tf_op jit(solution)/shard_map/pallas_call | solution.py:418
Async XLA Ops:
  0.0 3.0 %collective-permute-start = (bf16[256,1024]{1,0:T(8,128)(2,1)}, bf16[256,1024]{1,0:T(8,128)(2,1)S(1)}, u32[]{:S(2)}, u32[]{:S(2)}) collective-permute-start(bf16[256,1024]{1,0:T(8,128)(2,1)} %q.1), channel_id=1, source_target_pairs={{0,1},{1,0},{2,3},{3,2},{4,5},{5,4},{6,7},{7,6},{8,9},{9,8},{10,11... | collective-permute-start | bytes 1572872 | tf_op jit(solution)/shard_map/ppermute | solution.py:452
  0.7 2.5 %collective-permute-start.1 = (bf16[256,1024]{1,0:T(8,128)(2,1)}, bf16[256,1024]{1,0:T(8,128)(2,1)S(1)}, u32[]{:S(2)}, u32[]{:S(2)}) collective-permute-start(bf16[256,1024]{1,0:T(8,128)(2,1)} %k.1), channel_id=1, source_target_pairs={{0,1},{1,0},{2,3},{3,2},{4,5},{5,4},{6,7},{7,6},{8,9},{9,8},{10,11... | collective-permute-start | bytes 1572872 | tf_op jit(solution)/shard_map/ppermute | solution.py:452
  0.7 3.2 %collective-permute-start.2 = (bf16[256,1024]{1,0:T(8,128)(2,1)}, bf16[256,1024]{1,0:T(8,128)(2,1)S(1)}, u32[]{:S(2)}, u32[]{:S(2)}) collective-permute-start(bf16[256,1024]{1,0:T(8,128)(2,1)} %v.1), channel_id=1, source_target_pairs={{0,1},{1,0},{2,3},{3,2},{4,5},{5,4},{6,7},{7,6},{8,9},{9,8},{10,11... | collective-permute-start | bytes 1572872 | tf_op jit(solution)/shard_map/ppermute | solution.py:452
  3.9 10.1 %copy-start = (bf16[256,1024]{1,0:T(8,128)(2,1)}, bf16[256,1024]{1,0:T(8,128)(2,1)S(1)}, u32[]{:S(2)}) copy-start(bf16[256,1024]{1,0:T(8,128)(2,1)S(1)} %collective-permute-done.2.refs_3_.refs_2_) | copy-start | bytes 1572868
  5.9 24.6 %all-to-all-start = ((bf16[8,224,128]{2,1,0:T(8,128)(2,1)}), bf16[8,224,128]{2,1,0:T(8,128)(2,1)}, u32[]{:S(2)}, u32[]{:S(2)}) async-start(bf16[8,224,128]{2,1,0:T(8,128)(2,1)} %shard_map.38), calls=%async_computation | async-start | bytes 917504 | tf_op jit(solution)/shard_map/all_to_all | solution.py:460
  16.1 32.3 %collective-permute-start.4 = (bf16[768,512]{1,0:T(8,128)(2,1)}, bf16[768,512]{1,0:T(8,128)(2,1)S(1)}, u32[]{:S(2)}, u32[]{:S(2)}) collective-permute-start(bf16[768,512]{1,0:T(8,128)(2,1)} %get-tuple-element.20), channel_id=1, source_target_pairs={{0,2},{1,3},{2,4},{3,5},{4,6},{5,7},{6,8},{7,9},{8,10},{9,11},{10,... | collective-permute-start | bytes 2359304 | tf_op jit(solution)/shard_map/ppermute | solution.py:452
  19.4 29.0 %collective-permute-start.5 = (bf16[768,512]{1,0:T(8,128)(2,1)}, bf16[768,512]{1,0:T(8,128)(2,1)S(1)}, u32[]{:S(2)}, u32[]{:S(2)}) collective-permute-start(bf16[768,512]{1,0:T(8,128)(2,1)} %get-tuple-element.21), channel_id=1, source_target_pairs={{2,0},{3,1},{4,2},{5,3},{6,4},{7,5},{8,6},{9,7},{10,8},{11,9},{12,... | collective-permute-start | bytes 2359304 | tf_op jit(solution)/shard_map/ppermute | solution.py:452
  31.5 10.3 %collective-permute-start.3 = (bf16[1024,128]{1,0:T(8,128)(2,1)S(1)}, bf16[1024,128]{1,0:T(8,128)(2,1)S(1)}, u32[]{:S(2)}, u32[]{:S(2)}) collective-permute-start(bf16[1024,128]{1,0:T(8,128)(2,1)S(1)} %shard_map.40), channel_id=1, source_target_pairs={{8,24},{9,25},{10,26},{11,27},{12,28},{13,29},{14,30},{15,31},{16,... | collective-permute-start | bytes 786440 | tf_op jit(solution)/shard_map/ppermute | solution.py:452
  36.1 1.0 %copy-start.1 = (bf16[256,1024]{1,0:T(8,128)(2,1)S(1)}, bf16[256,1024]{1,0:T(8,128)(2,1)}, u32[]{:S(2)}) copy-start(bf16[256,1024]{1,0:T(8,128)(2,1)} %copy-done) | copy-start | bytes 1572868
  39.5 0.8 %copy-start.2 = (bf16[512,640]{1,0:T(8,128)(2,1)}, bf16[512,640]{1,0:T(8,128)(2,1)S(1)}, u32[]{:S(2)}) copy-start(bf16[512,640]{1,0:T(8,128)(2,1)S(1)} %shard_map.41.refs_2_) | copy-start | bytes 1966084
  44.3 16.3 %all-to-all-start.1 = ((bf16[8,112,128]{2,1,0:T(8,128)(2,1)}), bf16[8,112,128]{2,1,0:T(8,128)(2,1)}, u32[]{:S(2)}, u32[]{:S(2)}) async-start(bf16[8,112,128]{2,1,0:T(8,128)(2,1)} %shard_map.43), calls=%async_computation.1 | async-start | bytes 458752 | tf_op jit(solution)/shard_map/all_to_all | solution.py:460
  50.0 15.5 %collective-permute-start.7 = (bf16[256,512]{1,0:T(8,128)(2,1)}, bf16[256,512]{1,0:T(8,128)(2,1)}, u32[]{:S(2)}, u32[]{:S(2)}) collective-permute-start(bf16[256,512]{1,0:T(8,128)(2,1)} %shard_map.44), channel_id=1, source_target_pairs={{2,4},{3,5},{4,2},{5,3},{6,8},{7,9},{8,6},{9,7},{10,12},{11,13},{1... | collective-permute-start | bytes 786440 | tf_op jit(solution)/shard_map/ppermute | solution.py:452
  57.7 4.5 %collective-permute-start.6 = (bf16[128,512]{1,0:T(8,128)(2,1)}, bf16[128,512]{1,0:T(8,128)(2,1)}, u32[]{:S(2)}, u32[]{:S(2)}) collective-permute-start(bf16[128,512]{1,0:T(8,128)(2,1)} %shard_map.42.refs_0_), channel_id=1, source_target_pairs={{0,2},{1,3},{2,0},{3,1},{4,6},{5,7},{6,4},{7,5},{8,10},{9,11},{10,... | collective-permute-start | bytes 393224 | tf_op jit(solution)/shard_map/ppermute | solution.py:452
  59.8 0.9 %copy-start.4 = (bf16[512,640]{1,0:T(8,128)(2,1)}, bf16[512,640]{1,0:T(8,128)(2,1)S(1)}, u32[]{:S(2)}) copy-start(bf16[512,640]{1,0:T(8,128)(2,1)S(1)} %shard_map.45.refs_3_) | copy-start | bytes 1966084
  60.6 7.4 %copy-start.3 = (bf16[512,640]{1,0:T(8,128)(2,1)S(1)}, bf16[512,640]{1,0:T(8,128)(2,1)}, u32[]{:S(2)}) copy-start(bf16[512,640]{1,0:T(8,128)(2,1)} %copy-done.2) | copy-start | bytes 1966084
  60.6 7.4 %copy-start.5 = (bf16[512,640]{1,0:T(8,128)(2,1)S(1)}, bf16[512,640]{1,0:T(8,128)(2,1)}, u32[]{:S(2)}) copy-start(bf16[512,640]{1,0:T(8,128)(2,1)} %copy-done.4) | copy-start | bytes 1966084
  67.7 4.4 %collective-permute-start.8 = (bf16[128,640]{1,0:T(8,128)(2,1)S(1)}, bf16[128,640]{1,0:T(8,128)(2,1)S(1)}, u32[]{:S(2)}, u32[]{:S(2)}) collective-permute-start(bf16[128,640]{1,0:T(8,128)(2,1)S(1)} %get-tuple-element.28), channel_id=1, source_target_pairs={{0,2},{1,3},{2,0},{3,1},{4,6},{5,7},{6,4},{7,5},{8,10},{9,11},{10,... | collective-permute-start | bytes 491528 | tf_op jit(solution)/shard_map/ppermute | solution.py:452
  75.4 3.7 %collective-permute-start.9 = (bf16[256,512]{1,0:T(8,128)(2,1)S(1)}, bf16[256,512]{1,0:T(8,128)(2,1)S(1)}, u32[]{:S(2)}, u32[]{:S(2)}) collective-permute-start(bf16[256,512]{1,0:T(8,128)(2,1)S(1)} %get-tuple-element.32), channel_id=1, source_target_pairs={{0,1},{1,0},{2,3},{3,2},{4,5},{5,4},{6,7},{7,6},{8,9},{9,8},{10,11... | collective-permute-start | bytes 786440 | tf_op jit(solution)/shard_map/ppermute | solution.py:452

commit v3 on v2

--- a/solution.py
+++ b/solution.py
@@ -24,6 +24,7 @@
 SEND = 3 * ROWS4 + 2 * ROWS3
 BACK = ROWS4 + ROWS3 + 16
 VMEM_LIMIT = 10 * 2**20
+EDGE = 3 * B
 
 
 def shaped(*shape):
@@ -179,10 +180,10 @@
         ):
             out_ref[row : row + rows, cols] = o
             values.append(value)
-    out_ref[row : row + rows, COLS:] = tile_of(values)
-
-
-def edge_body(s, own, k1, v1, rout, lout, rpay, lpay, sems):
+    out_ref[row : row + rows, COLS:PACK] = tile_of(values)
+
+
+def edge_body(s, own, q1, k1, v1, rout, lout, rpay, lpay, sems):
     copies = []
     for i, (pay, out) in enumerate(((rpay, rout), (lpay, lout))):
         first = s[0] == 1 - i
@@ -192,15 +193,12 @@
             pay[2 * B + n * 128 : 2 * B + (n + 1) * 128] = pooled(
                 jnp.where(first, other, mine), 1, n == 0
             )
+        for n, x in enumerate((own[0], q1[...])):
+            pay[EDGE + n * 64 : EDGE + (n + 1) * 64] = pooled(x, 2, True)
         copies.append(pltpu.make_async_copy(pay, out, sems.at[i]))
         copies[-1].start()
     for copy in copies:
         copy.wait()
-
-
-def pair_pay_body(s, own, q1, q_two):
-    q_two[:64] = pooled(own[0], 2, True)
-    q_two[64:] = pooled(q1[...], 2, True)
 
 
 def pool_body(s, own, q1, k1, v1, apay):
@@ -223,6 +221,8 @@
 def near_body(s, own, q1, k1, v1, out):
     k0, v0 = own.at[1], own.at[2]
     for at, q in enumerate((own.at[0], q1)):
+        rows = slice(at * B, (at + 1) * B)
+        out[rows, PACK:] = q[...]
         attend_to(
             out,
             at * B,
@@ -239,10 +239,10 @@
     return jnp.concatenate([near, far], axis=0)
 
 
-def derive_body(s, rin, lin, bpay):
-    odd = s[7] == 1
-    for n in (0, 1):
-        bpay[n * 128 : (n + 1) * 128] = jnp.where(odd, level_two(rin, n), level_two(lin, n))
+def block_body(s, own, k1, v1, bpay):
+    for n, ref in enumerate((k1, v1)):
+        bpay[n * 128 : n * 128 + 64] = pooled(own[1 + n], 2, n == 0)
+        bpay[n * 128 + 64 : (n + 1) * 128] = pooled(ref[...], 2, n == 0)
 
 
 def sides(s):
@@ -251,16 +251,17 @@
     return left, right
 
 
-def far_body(s, own, q1, rin, lin, out):
+def far_body(s, near, rin, lin, out, far):
     first = s[0] == 0
     bias_left, bias_right = sides(s)
-    for at, q in enumerate((own.at[0], q1)):
+    for at in (0, 1):
+        rows = slice(at * B, (at + 1) * B)
         left = first if at == 0 else jnp.logical_not(first)
         bias = jnp.where(left, bias_left, bias_right)
         attend_to(
-            out,
+            far,
             at * B,
-            lambda cols: q[:, cols],
+            lambda cols: near[rows, PACK + cols.start : PACK + cols.stop],
             lambda cols: [
                 (
                     jnp.where(left, rin[:B, cols], lin[:B, cols]),
@@ -271,31 +272,37 @@
             B,
             1.0,
         )
-
-
-def one_body(s, own, q1, near, far, rin, lin, out, one):
+        outs, weights = merged([unpacked(near[rows, :PACK]), unpacked(far[rows])])
+        for h in range(HEADS):
+            out[rows, h * DH : (h + 1) * DH] = outs[h].astype(BF16)
+        out[rows, COLS:PACK] = packed_tile(weights)
+        out[at * 128 : (at + 1) * 128, PACK:] = pooled(near[rows, PACK:], 1, True)
+
+
+def one_body(s, far, rin, lin, out, one):
     def coarse(cols):
         parts = []
         for ref, bias in zip((rin, lin), sides(s)):
             keys = pooled(ref[:B, cols], 1, True)
             values = pooled(ref[B : 2 * B, cols], 1, False)
             keys = jnp.concatenate([keys, ref[2 * B : 2 * B + 128, cols]], axis=0)
-            values = jnp.concatenate([values, ref[2 * B + 128 :, cols]], axis=0)
+            values = jnp.concatenate([values, ref[2 * B + 128 : EDGE, cols]], axis=0)
             parts.append((keys, values, bias))
         return parts
 
-    q_one = jnp.concatenate([pooled(own[0], 1, True), pooled(q1[...], 1, True)], axis=0)
-    attend_to(one, 0, lambda cols: q_one[:, cols], coarse, B, 2.0)
+    attend_to(
+        one, 0, lambda cols: far[:B, PACK + cols.start : PACK + cols.stop], coarse, B, 2.0
+    )
     for at in (0, 1):
         rows = slice(at * B, (at + 1) * B)
         level_one = spread(one[at * 128 : (at + 1) * 128], B, 1)
-        outs, weights = merged([unpacked(near[rows]), unpacked(far[rows]), level_one])
+        outs, weights = merged([unpacked(far[rows, :PACK]), level_one])
         for h in range(HEADS):
             out[rows, h * DH : (h + 1) * DH] = outs[h]
         out[rows, COLS:] = weights
 
 
-def pair_body(s, q_two, rin, lin, pin, bin_, mine, theirs):
+def pair_body(s, near, rin, lin, bin_, mine, theirs):
     bias = jnp.where(s[4] == 1, 0.0, ABSENT).astype(F32)
     odd = s[7] == 1
     kept = [
@@ -308,7 +315,9 @@
         )
         for n in (0, 1)
     ]
-    for out, ref in ((mine, q_two), (theirs, pin)):
+    own_two = jnp.concatenate([pooled(near[at * B : (at + 1) * B, PACK:], 2, True) for at in (0, 1)])
+    partner = jnp.where(odd, rin[EDGE:], lin[EDGE:])
+    for out, ref in ((theirs, partner), (mine, own_two)):
         attend_to(
             out,
             0,
@@ -439,7 +448,7 @@
 RIGHT = pairs_of(lambda chip: chip + 1)
 LEFT = pairs_of(lambda chip: chip - 1)
 PAIR = pairs_of(lambda chip: chip ^ 1)
-BOUND = pairs_of(lambda chip: chip + 1 if chip % 2 else chip - 1)
+BOUND = pairs_of(lambda chip: chip - 2 if chip % 2 else chip + 2)
 ROW = pairs_of(lambda chip: chip - RING if chip % RING < RING // 2 else chip + RING)
 LINES = [
     [2 * (row * RING + z) + core for z in range(RING)]
@@ -481,13 +490,13 @@
     (apay,) = call(pool_body, (shaped(RING, SEND, DH),), s, (own, q1, k1, v1), wide=(1, 2, 3))
     ain = line_swap(apay)
     s, _ = after(s, apay)
-    pay = shaped(3 * B, COLS)
+    pay = shaped(EDGE + 128, COLS)
     rpay, lpay = call(
         edge_body,
         (pay, pay),
         s,
-        (own, k1, v1),
-        wide=(1, 2),
+        (own, q1, k1, v1),
+        wide=(1, 2, 3),
         extra=[pltpu.VMEM(pay.shape, BF16)] * 2 + [pltpu.SemaphoreType.DMA((2,))],
         slow=True,
     )
@@ -497,20 +506,30 @@
     (xpay,) = call(row_pay_body, (shaped(4 * B, DH),), s, (ain,))
     xin = send_to(xpay, ROW)
     s, _ = after(s, xpay)
-    (near,) = call(near_body, (shaped(2 * B, PACK),), s, (own, q1, k1, v1), wide=(1, 2, 3))
-    (q_two,) = call(pair_pay_body, (shaped(128, COLS),), s, (own, q1), wide=(1,))
-    pin = send_to(q_two, PAIR)
-    s, _ = after(s, (near, q_two))
+    (bpay,) = call(block_body, (shaped(B, COLS),), s, (own, k1, v1), wide=(1, 2))
+    bin_ = send_to(bpay, BOUND)
+    s, _ = after(s, bpay)
+    (near,) = call(
+        near_body,
+        (shaped(2 * B, PACK + COLS),),
+        s,
+        (own, q1, k1, v1),
+        wide=(1, 2, 3),
+    )
+    s, _ = after(s, near)
     (back,) = call(row_body, (shaped(RING, BACK, DH),), s, (ain, xin))
     row_back = line_swap(back)
     s, _ = after(s, back)
-    (bpay,) = call(derive_body, (shaped(B, COLS),), s, (rin, lin))
-    bin_ = send_to(bpay, BOUND)
-    s, _ = after(s, bpay)
-    (far,) = call(far_body, (shaped(2 * B, PACK),), s, (own, q1, rin, lin), wide=(1,))
-    s, _ = after(s, (far, row_back))
+    (far,) = call(
+        far_body,
+        (shaped(2 * B, PACK + COLS),),
+        s,
+        (near, rin, lin),
+        extra=[pltpu.VMEM((2 * B, PACK), BF16)],
+    )
+    s, _ = after(s, far)
     two, theirs = call(
-        pair_body, (shaped(128, PACK), shaped(128, PACK)), s, (q_two, rin, lin, pin, bin_)
+        pair_body, (shaped(128, PACK), shaped(128, PACK)), s, (near, rin, lin, bin_)
     )
     two_back = send_to(theirs, PAIR)
     s, _ = after(s, theirs)
@@ -518,8 +537,7 @@
         one_body,
         (jax.ShapeDtypeStruct((2 * B, PACK), F32),),
         s,
-        (own, q1, near, far, rin, lin),
-        wide=(1,),
+        (far, rin, lin),
         extra=[pltpu.VMEM((B, PACK), BF16)],
     )
     mine, send = call(

time: 81.2 us -> 73.2 us (0.901)
  starting transfers between devices: 38 us -> 33.4 us
  local copies, waits for them, and re-layouts: 2.82 us -> 0.09 us
  waiting for transfers between devices: 12.7 us -> 11.8 us
    ppermute x10 -> x9, starting transfers between devices: 25.8 us -> 21.8 us  [send_to(): return lax.ppermute(x, 'seq', pairs)]
    unnamed x12 -> x4, local copies, waits for them, and re-layouts: 2.74 us -> 0.01 us
    ppermute x10 -> x9, waiting for transfers between devices: 7.86 us -> 7.07 us  [send_to(): return lax.ppermute(x, 'seq', pairs)]
    pallas_call x11 -> x10, Pallas kernels: 23.7 us -> 24.1 us  [call(): pl.pallas_call(outer, out_shape=[pltpu.HBM(o.shape, o.dtype) for o in out...]
  transfers between devices with their start and end apart: 12 -> 11, of which waited for: 7 -> 7; matrix products, arithmetic and copies ran while one was open for 0% -> 0% of each run, Pallas kernels for 22% -> 29%
where the time goes in v3:
time: 73.2 us; the launch traced here: 72.7 us
  starting transfers between devices  33.4 us (46%)
  Pallas kernels  27.1 us (37%)
  waiting for transfers between devices  11.8 us (16%)
    pallas_call x10, Pallas kernels, call(): pl.pallas_call(outer, out_shape=[pltpu.HBM(o.shape, o.dtype) for o in out...  24.1 us
    ppermute x9, starting transfers between devices, send_to(): return lax.ppermute(x, 'seq', pairs)  21.8 us
    all_to_all x2, starting transfers between devices, line_swap(): return lax.all_to_all(x, 'seq', 0, 0, axis_index_groups=LINES)  11.7 us
    ppermute x9, waiting for transfers between devices, send_to(): return lax.ppermute(x, 'seq', pairs)  7.07 us
    all_to_all x2, waiting for transfers between devices, line_swap(): return lax.all_to_all(x, 'seq', 0, 0, axis_index_groups=LINES)  4.7 us
    pallas_call x1, Pallas kernels, half_columns(): pl.pallas_call(half_body, out_shape=shaped(3, B, COLS), in_specs=[pl.Bloc...  1.68 us
  transfers between devices with their start and end apart: 11, of which 7 were waited for; matrix products, arithmetic and copies ran while one was open for 0% of the time, Pallas kernels for 29%

profile of v3, /device:TPU:25, one launch (start us, length us, event | category | flops | bytes accessed | tf_op | source)
XLA Modules:
  0.0 72.7 jit_solution(12407571645862351588)
XLA Ops:
  0.0 0.7 collective-permute-start
  0.7 0.0 collective-permute-start.1
  0.7 0.5 collective-permute-start.2
  1.2 0.1 stack.51.s
  1.3 1.7 %shard_map.37.refs_0_ = bf16[3,256,512]{2,1,0:T(8,128)(2,1)S(1)} custom-call(s32[8]{0:T(128)S(1)} %stack.51.s, bf16[256,1024]{1,0:T(8,128)(2,1)} %q.1, bf16[256,1024]{1,0:T(8,128)(2,1)} %k.1, bf16[256,1024]{1,0:T(8,128)(2,1)} %v.1), custom_call_target="tpu_custom_call" | custom-call | tf_op jit(solution)/shard_map/pallas_call | solution.py:67
  3.0 0.0 collective-permute-done.refs_1_
  3.0 0.2 collective-permute-done.1.refs_2_.refs_1_
  3.2 0.7 %collective-permute-done.2.refs_3_.refs_2_ = bf16[256,1024]{1,0:T(8,128)(2,1)S(1)} collective-permute-done((bf16[256,1024]{1,0:T(8,128)(2,1)}, bf16[256,1024]{1,0:T(8,128)(2,1)S(1)}, u32[]{:S(2)}, u32[]{:S(2)}) %collective-permute-start.2) | collective-permute-done | bytes 524320 | tf_op jit(solution)/shard_map/ppermute | solution.py:461
  3.9 1.9 %shard_map.38 = bf16[8,224,128]{2,1,0:T(8,128)(2,1)} custom-call(s32[8]{0:T(128)S(1)} %stack.51.s, bf16[3,256,512]{2,1,0:T(8,128)(2,1)S(1)} %shard_map.37.refs_0_, bf16[256,1024]{1,0:T(8,128)(2,1)S(1)} %collective-permute-done.refs_1_, bf16[256,1024]{1,0:T(8,128)(2,1)S(1)} %collective-permute-done.1.refs_2_.refs_1_, ...), custom_call_target="tpu_custom_call" | custom-call | tf_op jit(solution)/shard_map/pallas_call | solution.py:42
  5.8 8.2 %all-to-all-start = ((bf16[8,224,128]{2,1,0:T(8,128)(2,1)}), bf16[8,224,128]{2,1,0:T(8,128)(2,1)S(1)}, u32[]{:S(2)}, u32[]{:S(2)}) async-start(bf16[8,224,128]{2,1,0:T(8,128)(2,1)} %shard_map.38), calls=%async_computation | async-start | bytes 917504 | tf_op jit(solution)/shard_map/all_to_all | solution.py:469
  14.0 2.2 %shard_map.39 = (bf16[896,512]{1,0:T(8,128)(2,1)}, bf16[896,512]{1,0:T(8,128)(2,1)}) custom-call(s32[8]{0:T(128)S(1)} %stack.51.s, bf16[3,256,512]{2,1,0:T(8,128)(2,1)S(1)} %shard_map.37.refs_0_, bf16[256,1024]{1,0:T(8,128)(2,1)S(1)} %collective-permute-done.refs_1_, bf16[256,1024]{1,0:T(8,128)(2,1)S(1)} %collective-permute-done.1.refs_2_.refs_1_, ...), custom_call_target="tpu_custom_call" | custom-call | tf_op jit(solution)/shard_map/pallas_call | solution.py:42
  16.2 3.4 %collective-permute-start.4 = (bf16[896,512]{1,0:T(8,128)(2,1)}, bf16[896,512]{1,0:T(8,128)(2,1)}, u32[]{:S(2)}, u32[]{:S(2)}) collective-permute-start(bf16[896,512]{1,0:T(8,128)(2,1)} %get-tuple-element.20), channel_id=1, source_target_pairs={{0,2},{1,3},{2,4},{3,5},{4,6},{5,7},{6,8},{7,9},{8,10},{9,11},{10,... | collective-permute-start | bytes 2752520 | tf_op jit(solution)/shard_map/ppermute | solution.py:461
  19.6 6.1 %collective-permute-start.5 = (bf16[896,512]{1,0:T(8,128)(2,1)}, bf16[896,512]{1,0:T(8,128)(2,1)}, u32[]{:S(2)}, u32[]{:S(2)}) collective-permute-start(bf16[896,512]{1,0:T(8,128)(2,1)} %get-tuple-element.21), channel_id=1, source_target_pairs={{2,0},{3,1},{4,2},{5,3},{6,4},{7,5},{8,6},{9,7},{10,8},{11,9},{12,... | collective-permute-start | bytes 2752520 | tf_op jit(solution)/shard_map/ppermute | solution.py:461
  25.7 4.7 %all-to-all-done.refs_0_ = bf16[8,224,128]{2,1,0:T(8,128)(2,1)S(1)} async-done(((bf16[8,224,128]{2,1,0:T(8,128)(2,1)}), bf16[8,224,128]{2,1,0:T(8,128)(2,1)S(1)}, u32[]{:S(2)}, u32[]{:S(2)}) %all-to-all-start) | async-done | bytes 458784 | tf_op jit(solution)/shard_map/all_to_all | solution.py:469
  30.4 0.0 copy-start
  30.4 0.6 shard_map.40
  31.0 4.5 %collective-permute-start.3 = (bf16[1024,128]{1,0:T(8,128)(2,1)S(1)}, bf16[1024,128]{1,0:T(8,128)(2,1)S(1)}, u32[]{:S(2)}, u32[]{:S(2)}) collective-permute-start(bf16[1024,128]{1,0:T(8,128)(2,1)S(1)} %shard_map.40), channel_id=1, source_target_pairs={{8,24},{9,25},{10,26},{11,27},{12,28},{13,29},{14,30},{15,31},{16,... | collective-permute-start | bytes 786440 | tf_op jit(solution)/shard_map/ppermute | solution.py:461
  35.4 1.5 %shard_map.41 = bf16[256,512]{1,0:T(8,128)(2,1)} custom-call(s32[8]{0:T(128)S(1)} %stack.51.s, bf16[3,256,512]{2,1,0:T(8,128)(2,1)S(1)} %shard_map.37.refs_0_, bf16[256,1024]{1,0:T(8,128)(2,1)S(1)} %collective-permute-done.1.refs_2_.refs_1_, bf16[256,1024]{1,0:T(8,128)(2,1)S(1)} %collective-permute-done.2.refs_3_.refs_2_), custom_call_target="tpu_custom_call" | custom-call | tf_op jit(solution)/shard_map/pallas_call | solution.py:42
  37.0 0.0 copy-done
  37.0 1.9 %collective-permute-start.6 = (bf16[256,512]{1,0:T(8,128)(2,1)}, bf16[256,512]{1,0:T(8,128)(2,1)}, u32[]{:S(2)}, u32[]{:S(2)}) collective-permute-start(bf16[256,512]{1,0:T(8,128)(2,1)} %shard_map.41), channel_id=1, source_target_pairs={{0,4},{1,5},{4,8},{5,9},{6,2},{7,3},{8,12},{9,13},{10,6},{11,7},{1... | collective-permute-start | bytes 786440 | tf_op jit(solution)/shard_map/ppermute | solution.py:461
  38.9 0.0 copy-start.1
  38.9 2.5 %shard_map.42.refs_0_ = bf16[512,1152]{1,0:T(8,128)(2,1)S(1)} custom-call(s32[8]{0:T(128)S(1)} %stack.51.s, bf16[3,256,512]{2,1,0:T(8,128)(2,1)S(1)} %shard_map.37.refs_0_, bf16[256,1024]{1,0:T(8,128)(2,1)S(1)} %collective-permute-done.refs_1_, bf16[256,1024]{1,0:T(8,128)(2,1)S(1)} %collective-permute-done.1.refs_2_.refs_1_, ...), custom_call_target="tpu_custom_call" | custom-call | tf_op jit(solution)/shard_map/pallas_call | solution.py:42
  41.4 0.0 collective-permute-done.3.refs_1_
  41.4 0.0 copy-done.1
  41.4 2.1 %shard_map.43 = bf16[8,112,128]{2,1,0:T(8,128)(2,1)} custom-call(s32[8]{0:T(128)S(1)} %stack.51.s, bf16[8,224,128]{2,1,0:T(8,128)(2,1)S(1)} %copy-done.1, bf16[1024,128]{1,0:T(8,128)(2,1)S(1)} %collective-permute-done.3.refs_1_), custom_call_target="tpu_custom_call" | custom-call | tf_op jit(solution)/shard_map/pallas_call | solution.py:42
  43.5 3.5 %all-to-all-start.1 = ((bf16[8,112,128]{2,1,0:T(8,128)(2,1)}), bf16[8,112,128]{2,1,0:T(8,128)(2,1)S(1)}, u32[]{:S(2)}, u32[]{:S(2)}) async-start(bf16[8,112,128]{2,1,0:T(8,128)(2,1)} %shard_map.43), calls=%async_computation.1 | async-start | bytes 458752 | tf_op jit(solution)/shard_map/all_to_all | solution.py:469
  47.0 2.1 %collective-permute-done.4.refs_1_ = bf16[896,512]{1,0:T(8,128)(2,1)} collective-permute-done((bf16[896,512]{1,0:T(8,128)(2,1)}, bf16[896,512]{1,0:T(8,128)(2,1)}, u32[]{:S(2)}, u32[]{:S(2)}) %collective-permute-start.4) | collective-permute-done | bytes 917536 | tf_op jit(solution)/shard_map/ppermute | solution.py:461
  49.1 0.0 collective-permute-done.5.refs_2_
  49.1 4.0 %shard_map.44.refs_0_ = bf16[512,1152]{1,0:T(8,128)(2,1)S(1)} custom-call(s32[8]{0:T(128)S(1)} %stack.51.s, bf16[512,1152]{1,0:T(8,128)(2,1)S(1)} %shard_map.42.refs_0_, bf16[896,512]{1,0:T(8,128)(2,1)} %collective-permute-done.4.refs_1_, bf16[896,512]{1,0:T(8,128)(2,1)} %collective-permute-done.5.refs_2_), custom_call_target="tpu_custom_call" | custom-call | tf_op jit(solution)/shard_map/pallas_call | solution.py:42
  53.1 2.5 %collective-permute-done.6.refs_3_ = bf16[256,512]{1,0:T(8,128)(2,1)} collective-permute-done((bf16[256,512]{1,0:T(8,128)(2,1)}, bf16[256,512]{1,0:T(8,128)(2,1)}, u32[]{:S(2)}, u32[]{:S(2)}) %collective-permute-start.6) | collective-permute-done | bytes 262176 | tf_op jit(solution)/shard_map/ppermute | solution.py:461
  55.7 2.7 %shard_map.45 = (bf16[128,640]{1,0:T(8,128)(2,1)S(1)}, bf16[128,640]{1,0:T(8,128)(2,1)S(1)}) custom-call(s32[8]{0:T(128)S(1)} %stack.51.s, bf16[512,1152]{1,0:T(8,128)(2,1)S(1)} %shard_map.42.refs_0_, bf16[896,512]{1,0:T(8,128)(2,1)} %collective-permute-done.4.refs_1_, bf16[896,512]{1,0:T(8,128)(2,1)} %collective-permute-done.5.refs_2_, ...), custom_call_target="tpu_custom_call" | custom-call | tf_op jit(solution)/shard_map/pallas_call | solution.py:42
  58.3 0.3 collective-permute-start.7
  58.6 3.9 %shard_map.46.refs_0_ = f32[512,640]{1,0:T(8,128)S(1)} custom-call(s32[8]{0:T(128)S(1)} %stack.51.s, bf16[512,1152]{1,0:T(8,128)(2,1)S(1)} %shard_map.44.refs_0_, bf16[896,512]{1,0:T(8,128)(2,1)} %collective-permute-done.4.refs_1_, bf16[896,512]{1,0:T(8,128)(2,1)} %collective-permute-done.5.refs_2_), custom_call_target="tpu_custom_call" | custom-call | tf_op jit(solution)/shard_map/pallas_call | solution.py:42
  62.5 0.3 collective-permute-done.7.refs_2_
  62.8 0.0 all-to-all-done.1.refs_3_
  62.8 2.8 %shard_map.47 = (bf16[256,512]{1,0:T(8,128)(2,1)S(1)}, bf16[256,512]{1,0:T(8,128)(2,1)S(1)}) custom-call(s32[8]{0:T(128)S(1)} %stack.51.s, f32[512,640]{1,0:T(8,128)S(1)} %shard_map.46.refs_0_, bf16[128,640]{1,0:T(8,128)(2,1)S(1)} %get-tuple-element.30.refs_1_, bf16[128,640]{1,0:T(8,128)(2,1)S(1)} %collective-permute-done.7.refs_2_, ...), custom_call_target="tpu_custom_call" | custom-call | tf_op jit(solution)/shard_map/pallas_call | solution.py:42
  65.6 4.4 %collective-permute-start.8 = (bf16[256,512]{1,0:T(8,128)(2,1)S(1)}, bf16[256,512]{1,0:T(8,128)(2,1)S(1)}, u32[]{:S(2)}, u32[]{:S(2)}) collective-permute-start(bf16[256,512]{1,0:T(8,128)(2,1)S(1)} %get-tuple-element.32), channel_id=1, source_target_pairs={{0,1},{1,0},{2,3},{3,2},{4,5},{5,4},{6,7},{7,6},{8,9},{9,8},{10,11... | collective-permute-start | bytes 786440 | tf_op jit(solution)/shard_map/ppermute | solution.py:461
  70.0 1.2 %collective-permute-done.8.theirs = bf16[256,512]{1,0:T(8,128)(2,1)S(1)} collective-permute-done((bf16[256,512]{1,0:T(8,128)(2,1)S(1)}, bf16[256,512]{1,0:T(8,128)(2,1)S(1)}, u32[]{:S(2)}, u32[]{:S(2)}) %collective-permute-start.8) | collective-permute-done | bytes 262176 | tf_op jit(solution)/shard_map/ppermute | solution.py:461
  71.2 1.3 %shard_map.48 = bf16[256,1024]{1,0:T(8,128)(2,1)} custom-call(s32[8]{0:T(128)S(1)} %stack.51.s, bf16[256,512]{1,0:T(8,128)(2,1)S(1)} %get-tuple-element.31.mine, bf16[256,512]{1,0:T(8,128)(2,1)S(1)} %collective-permute-done.8.theirs), custom_call_target="tpu_custom_call" | custom-call | tf_op jit(solution)/shard_map/pallas_call | solution.py:427
Async XLA Ops:
  0.0 3.0 %collective-permute-start = (bf16[256,1024]{1,0:T(8,128)(2,1)}, bf16[256,1024]{1,0:T(8,128)(2,1)S(1)}, u32[]{:S(2)}, u32[]{:S(2)}) collective-permute-start(bf16[256,1024]{1,0:T(8,128)(2,1)} %q.1), channel_id=1, source_target_pairs={{0,1},{1,0},{2,3},{3,2},{4,5},{5,4},{6,7},{7,6},{8,9},{9,8},{10,11... | collective-permute-start | bytes 1572872 | tf_op jit(solution)/shard_map/ppermute | solution.py:461
  0.7 2.5 %collective-permute-start.1 = (bf16[256,1024]{1,0:T(8,128)(2,1)}, bf16[256,1024]{1,0:T(8,128)(2,1)S(1)}, u32[]{:S(2)}, u32[]{:S(2)}) collective-permute-start(bf16[256,1024]{1,0:T(8,128)(2,1)} %k.1), channel_id=1, source_target_pairs={{0,1},{1,0},{2,3},{3,2},{4,5},{5,4},{6,7},{7,6},{8,9},{9,8},{10,11... | collective-permute-start | bytes 1572872 | tf_op jit(solution)/shard_map/ppermute | solution.py:461
  0.7 3.2 %collective-permute-start.2 = (bf16[256,1024]{1,0:T(8,128)(2,1)}, bf16[256,1024]{1,0:T(8,128)(2,1)S(1)}, u32[]{:S(2)}, u32[]{:S(2)}) collective-permute-start(bf16[256,1024]{1,0:T(8,128)(2,1)} %v.1), channel_id=1, source_target_pairs={{0,1},{1,0},{2,3},{3,2},{4,5},{5,4},{6,7},{7,6},{8,9},{9,8},{10,11... | collective-permute-start | bytes 1572872 | tf_op jit(solution)/shard_map/ppermute | solution.py:461
  5.8 24.6 %all-to-all-start = ((bf16[8,224,128]{2,1,0:T(8,128)(2,1)}), bf16[8,224,128]{2,1,0:T(8,128)(2,1)S(1)}, u32[]{:S(2)}, u32[]{:S(2)}) async-start(bf16[8,224,128]{2,1,0:T(8,128)(2,1)} %shard_map.38), calls=%async_computation | async-start | bytes 917504 | tf_op jit(solution)/shard_map/all_to_all | solution.py:469
  16.2 32.9 %collective-permute-start.4 = (bf16[896,512]{1,0:T(8,128)(2,1)}, bf16[896,512]{1,0:T(8,128)(2,1)}, u32[]{:S(2)}, u32[]{:S(2)}) collective-permute-start(bf16[896,512]{1,0:T(8,128)(2,1)} %get-tuple-element.20), channel_id=1, source_target_pairs={{0,2},{1,3},{2,4},{3,5},{4,6},{5,7},{6,8},{7,9},{8,10},{9,11},{10,... | collective-permute-start | bytes 2752520 | tf_op jit(solution)/shard_map/ppermute | solution.py:461
  19.6 29.5 %collective-permute-start.5 = (bf16[896,512]{1,0:T(8,128)(2,1)}, bf16[896,512]{1,0:T(8,128)(2,1)}, u32[]{:S(2)}, u32[]{:S(2)}) collective-permute-start(bf16[896,512]{1,0:T(8,128)(2,1)} %get-tuple-element.21), channel_id=1, source_target_pairs={{2,0},{3,1},{4,2},{5,3},{6,4},{7,5},{8,6},{9,7},{10,8},{11,9},{12,... | collective-permute-start | bytes 2752520 | tf_op jit(solution)/shard_map/ppermute | solution.py:461
  30.4 6.6 %copy-start = (bf16[8,224,128]{2,1,0:T(8,128)(2,1)}, bf16[8,224,128]{2,1,0:T(8,128)(2,1)S(1)}, u32[]{:S(2)}) copy-start(bf16[8,224,128]{2,1,0:T(8,128)(2,1)S(1)} %all-to-all-done.refs_0_) | copy-start | bytes 1376260
  31.0 10.4 %collective-permute-start.3 = (bf16[1024,128]{1,0:T(8,128)(2,1)S(1)}, bf16[1024,128]{1,0:T(8,128)(2,1)S(1)}, u32[]{:S(2)}, u32[]{:S(2)}) collective-permute-start(bf16[1024,128]{1,0:T(8,128)(2,1)S(1)} %shard_map.40), channel_id=1, source_target_pairs={{8,24},{9,25},{10,26},{11,27},{12,28},{13,29},{14,30},{15,31},{16,... | collective-permute-start | bytes 786440 | tf_op jit(solution)/shard_map/ppermute | solution.py:461
  37.0 18.7 %collective-permute-start.6 = (bf16[256,512]{1,0:T(8,128)(2,1)}, bf16[256,512]{1,0:T(8,128)(2,1)}, u32[]{:S(2)}, u32[]{:S(2)}) collective-permute-start(bf16[256,512]{1,0:T(8,128)(2,1)} %shard_map.41), channel_id=1, source_target_pairs={{0,4},{1,5},{4,8},{5,9},{6,2},{7,3},{8,12},{9,13},{10,6},{11,7},{1... | collective-permute-start | bytes 786440 | tf_op jit(solution)/shard_map/ppermute | solution.py:461
  38.9 2.5 %copy-start.1 = (bf16[8,224,128]{2,1,0:T(8,128)(2,1)S(1)}, bf16[8,224,128]{2,1,0:T(8,128)(2,1)}, u32[]{:S(2)}) copy-start(bf16[8,224,128]{2,1,0:T(8,128)(2,1)} %copy-done) | copy-start | bytes 1376260
  43.5 19.3 %all-to-all-start.1 = ((bf16[8,112,128]{2,1,0:T(8,128)(2,1)}), bf16[8,112,128]{2,1,0:T(8,128)(2,1)S(1)}, u32[]{:S(2)}, u32[]{:S(2)}) async-start(bf16[8,112,128]{2,1,0:T(8,128)(2,1)} %shard_map.43), calls=%async_computation.1 | async-start | bytes 458752 | tf_op jit(solution)/shard_map/all_to_all | solution.py:469
  58.3 4.4 %collective-permute-start.7 = (bf16[128,640]{1,0:T(8,128)(2,1)S(1)}, bf16[128,640]{1,0:T(8,128)(2,1)S(1)}, u32[]{:S(2)}, u32[]{:S(2)}) collective-permute-start(bf16[128,640]{1,0:T(8,128)(2,1)S(1)} %get-tuple-element.28), channel_id=1, source_target_pairs={{0,2},{1,3},{2,0},{3,1},{4,6},{5,7},{6,4},{7,5},{8,10},{9,11},{10,... | collective-permute-start | bytes 491528 | tf_op jit(solution)/shard_map/ppermute | solution.py:461
  65.6 5.6 %collective-permute-start.8 = (bf16[256,512]{1,0:T(8,128)(2,1)S(1)}, bf16[256,512]{1,0:T(8,128)(2,1)S(1)}, u32[]{:S(2)}, u32[]{:S(2)}) collective-permute-start(bf16[256,512]{1,0:T(8,128)(2,1)S(1)} %get-tuple-element.32), channel_id=1, source_target_pairs={{0,1},{1,0},{2,3},{3,2},{4,5},{5,4},{6,7},{7,6},{8,9},{9,8},{10,11... | collective-permute-start | bytes 786440 | tf_op jit(solution)/shard_map/ppermute | solution.py:461

commit v4 on v3

--- a/solution.py
+++ b/solution.py
@@ -185,6 +185,7 @@
 
 def edge_body(s, own, q1, k1, v1, rout, lout, rpay, lpay, sems):
     copies = []
+    queries = [pooled(x, 2, True) for x in (own[0], q1[...])]
     for i, (pay, out) in enumerate(((rpay, rout), (lpay, lout))):
         first = s[0] == 1 - i
         for n, ref in enumerate((k1, v1)):
@@ -193,8 +194,8 @@
             pay[2 * B + n * 128 : 2 * B + (n + 1) * 128] = pooled(
                 jnp.where(first, other, mine), 1, n == 0
             )
-        for n, x in enumerate((own[0], q1[...])):
-            pay[EDGE + n * 64 : EDGE + (n + 1) * 64] = pooled(x, 2, True)
+        for n, x in enumerate(queries):
+            pay[EDGE + n * 64 : EDGE + (n + 1) * 64] = x
         copies.append(pltpu.make_async_copy(pay, out, sems.at[i]))
         copies[-1].start()
     for copy in copies:
@@ -203,10 +204,18 @@
 
 def pool_body(s, own, q1, k1, v1, apay):
     half = s[1]
+    matrices = [
+        jnp.concatenate(
+            [pool_matrix(B >> level, B, level, 1.0 / 2**level if mean else 1.0) for level in (3, 4)],
+            axis=0,
+        )
+        for mean in (True, False)
+    ]
     for at in (0, 1):
         whole = (own[0], own[1], own[2]) if at == 0 else (q1[...], k1[...], v1[...])
-        three = [pooled(x, 3, n < 2) for n, x in enumerate(whole)]
-        four = [pooled(x, 4, n < 2) for n, x in enumerate(whole)]
+        both = [jnp.dot(matrices[n == 2], x, preferred_element_type=F32) for n, x in enumerate(whole)]
+        three = [x[: B >> 3].astype(BF16) for x in both]
+        four = [x[B >> 3 :].astype(BF16) for x in both]
         for j in range(RING):
             cols = slice((j % HEADS) * DH, (j % HEADS + 1) * DH)
             for n in range(3):
@@ -233,9 +242,9 @@
         )
 
 
-def level_two(ref, n):
-    near = pooled(ref[n * B : (n + 1) * B], 2, n == 0)
-    far = pooled(ref[2 * B + n * 128 : 2 * B + (n + 1) * 128], 1, n == 0)
+def level_two(x, n):
+    near = pooled(x[n * B : (n + 1) * B], 2, n == 0)
+    far = pooled(x[2 * B + n * 128 : 2 * B + (n + 1) * 128], 1, n == 0)
     return jnp.concatenate([near, far], axis=0)
 
 
@@ -251,7 +260,7 @@
     return left, right
 
 
-def far_body(s, near, rin, lin, out, far):
+def far_body(s, near, rin, lin, out):
     first = s[0] == 0
     bias_left, bias_right = sides(s)
     for at in (0, 1):
@@ -259,7 +268,7 @@
         left = first if at == 0 else jnp.logical_not(first)
         bias = jnp.where(left, bias_left, bias_right)
         attend_to(
-            far,
+            out,
             at * B,
             lambda cols: near[rows, PACK + cols.start : PACK + cols.stop],
             lambda cols: [
@@ -272,14 +281,9 @@
             B,
             1.0,
         )
-        outs, weights = merged([unpacked(near[rows, :PACK]), unpacked(far[rows])])
-        for h in range(HEADS):
-            out[rows, h * DH : (h + 1) * DH] = outs[h].astype(BF16)
-        out[rows, COLS:PACK] = packed_tile(weights)
-        out[at * 128 : (at + 1) * 128, PACK:] = pooled(near[rows, PACK:], 1, True)
-
-
-def one_body(s, far, rin, lin, out, one):
+
+
+def one_body(s, near, far, rin, lin, out, one):
     def coarse(cols):
         parts = []
         for ref, bias in zip((rin, lin), sides(s)):
@@ -290,13 +294,12 @@
             parts.append((keys, values, bias))
         return parts
 
-    attend_to(
-        one, 0, lambda cols: far[:B, PACK + cols.start : PACK + cols.stop], coarse, B, 2.0
-    )
+    q_one = jnp.concatenate([pooled(near[at * B : (at + 1) * B, PACK:], 1, True) for at in (0, 1)])
+    attend_to(one, 0, lambda cols: q_one[:, cols], coarse, B, 2.0)
     for at in (0, 1):
         rows = slice(at * B, (at + 1) * B)
         level_one = spread(one[at * 128 : (at + 1) * 128], B, 1)
-        outs, weights = merged([unpacked(far[rows, :PACK]), level_one])
+        outs, weights = merged([unpacked(near[rows, :PACK]), unpacked(far[rows]), level_one])
         for h in range(HEADS):
             out[rows, h * DH : (h + 1) * DH] = outs[h]
         out[rows, COLS:] = weights
@@ -305,28 +308,24 @@
 def pair_body(s, near, rin, lin, bin_, mine, theirs):
     bias = jnp.where(s[4] == 1, 0.0, ABSENT).astype(F32)
     odd = s[7] == 1
+    beside = jnp.where(odd, lin[:EDGE], rin[:EDGE])
     kept = [
-        jnp.concatenate(
-            [
-                jnp.where(odd, level_two(lin, n), level_two(rin, n)),
-                bin_[n * 128 : (n + 1) * 128],
-            ],
-            axis=0,
-        )
+        jnp.concatenate([level_two(beside, n), bin_[n * 128 : (n + 1) * 128]], axis=0)
         for n in (0, 1)
     ]
-    own_two = jnp.concatenate([pooled(near[at * B : (at + 1) * B, PACK:], 2, True) for at in (0, 1)])
-    partner = jnp.where(odd, rin[EDGE:], lin[EDGE:])
-    for out, ref in ((theirs, partner), (mine, own_two)):
-        attend_to(
-            out,
-            0,
-            lambda cols: ref[:, cols],
-            lambda cols: [(kept[0][:, cols], kept[1][:, cols], bias)],
-            128,
-            4.0,
-            4,
-        )
+    queries = [pooled(near[at * B : (at + 1) * B, PACK:], 2, True) for at in (0, 1)]
+    queries.append(jnp.where(odd, rin[EDGE:], lin[EDGE:]))
+    queries = jnp.concatenate(queries, axis=0)
+    spans = [slice(h * DH, (h + 1) * DH) for h in range(HEADS)]
+    jobs = [(queries[:, cols], [(kept[0][:, cols], kept[1][:, cols], bias)]) for cols in spans]
+    values = []
+    for cols, (o, value) in zip(spans, attend(jobs, 4.0)):
+        mine[:, cols] = o[:128]
+        theirs[:, cols] = o[128:]
+        values.append(value)
+    tile = tile_of(values)
+    mine[:, COLS:] = tile[:128]
+    theirs[:, COLS:] = tile[128:]
 
 
 def row_pay_body(s, ain, xpay):
@@ -520,13 +519,7 @@
     (back,) = call(row_body, (shaped(RING, BACK, DH),), s, (ain, xin))
     row_back = line_swap(back)
     s, _ = after(s, back)
-    (far,) = call(
-        far_body,
-        (shaped(2 * B, PACK + COLS),),
-        s,
-        (near, rin, lin),
-        extra=[pltpu.VMEM((2 * B, PACK), BF16)],
-    )
+    (far,) = call(far_body, (shaped(2 * B, PACK),), s, (near, rin, lin))
     s, _ = after(s, far)
     two, theirs = call(
         pair_body, (shaped(128, PACK), shaped(128, PACK)), s, (near, rin, lin, bin_)
@@ -537,7 +530,7 @@
         one_body,
         (jax.ShapeDtypeStruct((2 * B, PACK), F32),),
         s,
-        (far, rin, lin),
+        (near, far, rin, lin),
         extra=[pltpu.VMEM((B, PACK), BF16)],
     )
     mine, send = call(

time: 73.2 us -> 71.6 us (0.978)
  Pallas kernels: 27.1 us -> 25.9 us
  starting transfers between devices: 33.4 us -> 32.2 us
  waiting for transfers between devices: 11.8 us -> 12.6 us
    pallas_call x10, Pallas kernels: 24.1 us -> 22.9 us  [call(): pl.pallas_call(outer, out_shape=[pltpu.HBM(o.shape, o.dtype) for o in out...]
    ppermute x9, starting transfers between devices: 21.8 us -> 20.6 us  [send_to(): return lax.ppermute(x, 'seq', pairs)]
    ppermute x9, waiting for transfers between devices: 7.07 us -> 7.92 us  [send_to(): return lax.ppermute(x, 'seq', pairs)]
  transfers between devices with their start and end apart: 11 -> 11, of which waited for: 7 -> 6; matrix products, arithmetic and copies ran while one was open for 0% -> 0% of each run, Pallas kernels for 29% -> 28%
where the time goes in v4:
time: 71.6 us; the launch traced here: 71.2 us
  starting transfers between devices  32.2 us (45%)
  Pallas kernels  25.9 us (36%)
  waiting for transfers between devices  12.6 us (18%)
    pallas_call x10, Pallas kernels, call(): pl.pallas_call(outer, out_shape=[pltpu.HBM(o.shape, o.dtype) for o in out...  22.9 us
    ppermute x9, starting transfers between devices, send_to(): return lax.ppermute(x, 'seq', pairs)  20.6 us
    all_to_all x2, starting transfers between devices, line_swap(): return lax.all_to_all(x, 'seq', 0, 0, axis_index_groups=LINES)  11.7 us
    ppermute x9, waiting for transfers between devices, send_to(): return lax.ppermute(x, 'seq', pairs)  7.92 us
    all_to_all x2, waiting for transfers between devices, line_swap(): return lax.all_to_all(x, 'seq', 0, 0, axis_index_groups=LINES)  4.69 us
    pallas_call x1, Pallas kernels, half_columns(): pl.pallas_call(half_body, out_shape=shaped(3, B, COLS), in_specs=[pl.Bloc...  1.68 us
  transfers between devices with their start and end apart: 11, of which 6 were waited for; matrix products, arithmetic and copies ran while one was open for 0% of the time, Pallas kernels for 28%

profile of v4, /device:TPU:25, one launch (start us, length us, event | category | flops | bytes accessed | tf_op | source)
XLA Modules:
  0.0 71.2 jit_solution(16072002896434328575)
XLA Ops:
  0.0 0.7 collective-permute-start
  0.7 0.0 collective-permute-start.1
  0.7 0.5 collective-permute-start.2
  1.2 0.1 stack.51.s
  1.3 1.7 %shard_map.37.refs_0_ = bf16[3,256,512]{2,1,0:T(8,128)(2,1)S(1)} custom-call(s32[8]{0:T(128)S(1)} %stack.51.s, bf16[256,1024]{1,0:T(8,128)(2,1)} %q.1, bf16[256,1024]{1,0:T(8,128)(2,1)} %k.1, bf16[256,1024]{1,0:T(8,128)(2,1)} %v.1), custom_call_target="tpu_custom_call" | custom-call | tf_op jit(solution)/shard_map/pallas_call | solution.py:67
  3.0 0.0 collective-permute-done.refs_1_
  3.0 0.2 collective-permute-done.1.refs_2_.refs_1_
  3.2 0.7 %collective-permute-done.2.refs_3_.refs_2_ = bf16[256,1024]{1,0:T(8,128)(2,1)S(1)} collective-permute-done((bf16[256,1024]{1,0:T(8,128)(2,1)}, bf16[256,1024]{1,0:T(8,128)(2,1)S(1)}, u32[]{:S(2)}, u32[]{:S(2)}) %collective-permute-start.2) | collective-permute-done | bytes 524320 | tf_op jit(solution)/shard_map/ppermute | solution.py:460
  3.9 1.7 %shard_map.38 = bf16[8,224,128]{2,1,0:T(8,128)(2,1)} custom-call(s32[8]{0:T(128)S(1)} %stack.51.s, bf16[3,256,512]{2,1,0:T(8,128)(2,1)S(1)} %shard_map.37.refs_0_, bf16[256,1024]{1,0:T(8,128)(2,1)S(1)} %collective-permute-done.refs_1_, bf16[256,1024]{1,0:T(8,128)(2,1)S(1)} %collective-permute-done.1.refs_2_.refs_1_, ...), custom_call_target="tpu_custom_call" | custom-call | tf_op jit(solution)/shard_map/pallas_call | solution.py:42
  5.6 8.2 %all-to-all-start = ((bf16[8,224,128]{2,1,0:T(8,128)(2,1)}), bf16[8,224,128]{2,1,0:T(8,128)(2,1)S(1)}, u32[]{:S(2)}, u32[]{:S(2)}) async-start(bf16[8,224,128]{2,1,0:T(8,128)(2,1)} %shard_map.38), calls=%async_computation | async-start | bytes 917504 | tf_op jit(solution)/shard_map/all_to_all | solution.py:468
  13.8 2.2 %shard_map.39 = (bf16[896,512]{1,0:T(8,128)(2,1)}, bf16[896,512]{1,0:T(8,128)(2,1)}) custom-call(s32[8]{0:T(128)S(1)} %stack.51.s, bf16[3,256,512]{2,1,0:T(8,128)(2,1)S(1)} %shard_map.37.refs_0_, bf16[256,1024]{1,0:T(8,128)(2,1)S(1)} %collective-permute-done.refs_1_, bf16[256,1024]{1,0:T(8,128)(2,1)S(1)} %collective-permute-done.1.refs_2_.refs_1_, ...), custom_call_target="tpu_custom_call" | custom-call | tf_op jit(solution)/shard_map/pallas_call | solution.py:42
  16.0 3.4 %collective-permute-start.4 = (bf16[896,512]{1,0:T(8,128)(2,1)}, bf16[896,512]{1,0:T(8,128)(2,1)}, u32[]{:S(2)}, u32[]{:S(2)}) collective-permute-start(bf16[896,512]{1,0:T(8,128)(2,1)} %get-tuple-element.20), channel_id=1, source_target_pairs={{0,2},{1,3},{2,4},{3,5},{4,6},{5,7},{6,8},{7,9},{8,10},{9,11},{10,... | collective-permute-start | bytes 2752520 | tf_op jit(solution)/shard_map/ppermute | solution.py:460
  19.4 6.1 %collective-permute-start.5 = (bf16[896,512]{1,0:T(8,128)(2,1)}, bf16[896,512]{1,0:T(8,128)(2,1)}, u32[]{:S(2)}, u32[]{:S(2)}) collective-permute-start(bf16[896,512]{1,0:T(8,128)(2,1)} %get-tuple-element.21), channel_id=1, source_target_pairs={{2,0},{3,1},{4,2},{5,3},{6,4},{7,5},{8,6},{9,7},{10,8},{11,9},{12,... | collective-permute-start | bytes 2752520 | tf_op jit(solution)/shard_map/ppermute | solution.py:460
  25.5 4.7 %all-to-all-done.refs_0_ = bf16[8,224,128]{2,1,0:T(8,128)(2,1)S(1)} async-done(((bf16[8,224,128]{2,1,0:T(8,128)(2,1)}), bf16[8,224,128]{2,1,0:T(8,128)(2,1)S(1)}, u32[]{:S(2)}, u32[]{:S(2)}) %all-to-all-start) | async-done | bytes 458784 | tf_op jit(solution)/shard_map/all_to_all | solution.py:468
  30.2 0.0 copy-start
  30.2 0.6 shard_map.40
  30.8 4.5 %collective-permute-start.3 = (bf16[1024,128]{1,0:T(8,128)(2,1)S(1)}, bf16[1024,128]{1,0:T(8,128)(2,1)S(1)}, u32[]{:S(2)}, u32[]{:S(2)}) collective-permute-start(bf16[1024,128]{1,0:T(8,128)(2,1)S(1)} %shard_map.40), channel_id=1, source_target_pairs={{8,24},{9,25},{10,26},{11,27},{12,28},{13,29},{14,30},{15,31},{16,... | collective-permute-start | bytes 786440 | tf_op jit(solution)/shard_map/ppermute | solution.py:460
  35.2 1.5 %shard_map.41 = bf16[256,512]{1,0:T(8,128)(2,1)} custom-call(s32[8]{0:T(128)S(1)} %stack.51.s, bf16[3,256,512]{2,1,0:T(8,128)(2,1)S(1)} %shard_map.37.refs_0_, bf16[256,1024]{1,0:T(8,128)(2,1)S(1)} %collective-permute-done.1.refs_2_.refs_1_, bf16[256,1024]{1,0:T(8,128)(2,1)S(1)} %collective-permute-done.2.refs_3_.refs_2_), custom_call_target="tpu_custom_call" | custom-call | tf_op jit(solution)/shard_map/pallas_call | solution.py:42
  36.8 0.0 copy-done
  36.8 1.9 %collective-permute-start.6 = (bf16[256,512]{1,0:T(8,128)(2,1)}, bf16[256,512]{1,0:T(8,128)(2,1)}, u32[]{:S(2)}, u32[]{:S(2)}) collective-permute-start(bf16[256,512]{1,0:T(8,128)(2,1)} %shard_map.41), channel_id=1, source_target_pairs={{0,4},{1,5},{4,8},{5,9},{6,2},{7,3},{8,12},{9,13},{10,6},{11,7},{1... | collective-permute-start | bytes 786440 | tf_op jit(solution)/shard_map/ppermute | solution.py:460
  38.7 0.0 copy-start.1
  38.7 2.5 %shard_map.42.refs_0_ = bf16[512,1152]{1,0:T(8,128)(2,1)S(1)} custom-call(s32[8]{0:T(128)S(1)} %stack.51.s, bf16[3,256,512]{2,1,0:T(8,128)(2,1)S(1)} %shard_map.37.refs_0_, bf16[256,1024]{1,0:T(8,128)(2,1)S(1)} %collective-permute-done.refs_1_, bf16[256,1024]{1,0:T(8,128)(2,1)S(1)} %collective-permute-done.1.refs_2_.refs_1_, ...), custom_call_target="tpu_custom_call" | custom-call | tf_op jit(solution)/shard_map/pallas_call | solution.py:42
  41.2 0.0 collective-permute-done.3.refs_1_
  41.2 0.0 copy-done.1
  41.2 2.1 %shard_map.43 = bf16[8,112,128]{2,1,0:T(8,128)(2,1)} custom-call(s32[8]{0:T(128)S(1)} %stack.51.s, bf16[8,224,128]{2,1,0:T(8,128)(2,1)S(1)} %copy-done.1, bf16[1024,128]{1,0:T(8,128)(2,1)S(1)} %collective-permute-done.3.refs_1_), custom_call_target="tpu_custom_call" | custom-call | tf_op jit(solution)/shard_map/pallas_call | solution.py:42
  43.3 3.5 %all-to-all-start.1 = ((bf16[8,112,128]{2,1,0:T(8,128)(2,1)}), bf16[8,112,128]{2,1,0:T(8,128)(2,1)S(1)}, u32[]{:S(2)}, u32[]{:S(2)}) async-start(bf16[8,112,128]{2,1,0:T(8,128)(2,1)} %shard_map.43), calls=%async_computation.1 | async-start | bytes 458752 | tf_op jit(solution)/shard_map/all_to_all | solution.py:468
  46.7 2.1 %collective-permute-done.4.refs_1_.refs_2_ = bf16[896,512]{1,0:T(8,128)(2,1)} collective-permute-done((bf16[896,512]{1,0:T(8,128)(2,1)}, bf16[896,512]{1,0:T(8,128)(2,1)}, u32[]{:S(2)}, u32[]{:S(2)}) %collective-permute-start.4) | collective-permute-done | bytes 917536 | tf_op jit(solution)/shard_map/ppermute | solution.py:460
  48.9 0.0 collective-permute-done.5.refs_2_.refs_3_
  48.9 2.9 %shard_map.44.refs_1_ = bf16[512,640]{1,0:T(8,128)(2,1)S(1)} custom-call(s32[8]{0:T(128)S(1)} %stack.51.s, bf16[512,1152]{1,0:T(8,128)(2,1)S(1)} %shard_map.42.refs_0_, bf16[896,512]{1,0:T(8,128)(2,1)} %collective-permute-done.4.refs_1_.refs_2_, bf16[896,512]{1,0:T(8,128)(2,1)} %collective-permute-done.5.refs_2_.refs_3_), custom_call_target="tpu_custom_call" | custom-call | tf_op jit(solution)/shard_map/pallas_call | solution.py:42
  51.8 3.7 %collective-permute-done.6.refs_3_ = bf16[256,512]{1,0:T(8,128)(2,1)} collective-permute-done((bf16[256,512]{1,0:T(8,128)(2,1)}, bf16[256,512]{1,0:T(8,128)(2,1)}, u32[]{:S(2)}, u32[]{:S(2)}) %collective-permute-start.6) | collective-permute-done | bytes 262176 | tf_op jit(solution)/shard_map/ppermute | solution.py:460
  55.5 2.4 %shard_map.45 = (bf16[128,640]{1,0:T(8,128)(2,1)S(1)}, bf16[128,640]{1,0:T(8,128)(2,1)S(1)}) custom-call(s32[8]{0:T(128)S(1)} %stack.51.s, bf16[512,1152]{1,0:T(8,128)(2,1)S(1)} %shard_map.42.refs_0_, bf16[896,512]{1,0:T(8,128)(2,1)} %collective-permute-done.4.refs_1_.refs_2_, bf16[896,512]{1,0:T(8,128)(2,1)} %collective-permute-done.5.refs_2_.refs_3_, ...), custom_call_target="tpu_custom_call" | custom-call | tf_op jit(solution)/shard_map/pallas_call | solution.py:42
  57.9 0.3 collective-permute-start.7
  58.2 4.2 %shard_map.46.refs_0_ = f32[512,640]{1,0:T(8,128)S(1)} custom-call(s32[8]{0:T(128)S(1)} %stack.51.s, bf16[512,1152]{1,0:T(8,128)(2,1)S(1)} %shard_map.42.refs_0_, bf16[512,640]{1,0:T(8,128)(2,1)S(1)} %shard_map.44.refs_1_, bf16[896,512]{1,0:T(8,128)(2,1)} %collective-permute-done.4.refs_1_.refs_2_, bf16[896,512]{1,0:T(8,128)(2,1)} %collective-permute-done.5.refs_2_.refs_3_), custom_call_target="tpu_custom_call" | custom-call | tf_op jit(solution)/shard_map/pallas_call | solution.py:42
  62.4 0.0 collective-permute-done.7.refs_2_
  62.4 0.0 all-to-all-done.1.refs_3_
  62.4 2.8 %shard_map.47 = (bf16[256,512]{1,0:T(8,128)(2,1)S(1)}, bf16[256,512]{1,0:T(8,128)(2,1)S(1)}) custom-call(s32[8]{0:T(128)S(1)} %stack.51.s, f32[512,640]{1,0:T(8,128)S(1)} %shard_map.46.refs_0_, bf16[128,640]{1,0:T(8,128)(2,1)S(1)} %get-tuple-element.30.refs_1_, bf16[128,640]{1,0:T(8,128)(2,1)S(1)} %collective-permute-done.7.refs_2_, ...), custom_call_target="tpu_custom_call" | custom-call | tf_op jit(solution)/shard_map/pallas_call | solution.py:42
  65.2 3.3 %collective-permute-start.8 = (bf16[256,512]{1,0:T(8,128)(2,1)S(1)}, bf16[256,512]{1,0:T(8,128)(2,1)S(1)}, u32[]{:S(2)}, u32[]{:S(2)}) collective-permute-start(bf16[256,512]{1,0:T(8,128)(2,1)S(1)} %get-tuple-element.32), channel_id=1, source_target_pairs={{0,1},{1,0},{2,3},{3,2},{4,5},{5,4},{6,7},{7,6},{8,9},{9,8},{10,11... | collective-permute-start | bytes 786440 | tf_op jit(solution)/shard_map/ppermute | solution.py:460
  68.5 1.2 %collective-permute-done.8.theirs = bf16[256,512]{1,0:T(8,128)(2,1)S(1)} collective-permute-done((bf16[256,512]{1,0:T(8,128)(2,1)S(1)}, bf16[256,512]{1,0:T(8,128)(2,1)S(1)}, u32[]{:S(2)}, u32[]{:S(2)}) %collective-permute-start.8) | collective-permute-done | bytes 262176 | tf_op jit(solution)/shard_map/ppermute | solution.py:460
  69.6 1.3 %shard_map.48 = bf16[256,1024]{1,0:T(8,128)(2,1)} custom-call(s32[8]{0:T(128)S(1)} %stack.51.s, bf16[256,512]{1,0:T(8,128)(2,1)S(1)} %get-tuple-element.31.mine, bf16[256,512]{1,0:T(8,128)(2,1)S(1)} %collective-permute-done.8.theirs), custom_call_target="tpu_custom_call" | custom-call | tf_op jit(solution)/shard_map/pallas_call | solution.py:426
Async XLA Ops:
  0.0 3.0 %collective-permute-start = (bf16[256,1024]{1,0:T(8,128)(2,1)}, bf16[256,1024]{1,0:T(8,128)(2,1)S(1)}, u32[]{:S(2)}, u32[]{:S(2)}) collective-permute-start(bf16[256,1024]{1,0:T(8,128)(2,1)} %q.1), channel_id=1, source_target_pairs={{0,1},{1,0},{2,3},{3,2},{4,5},{5,4},{6,7},{7,6},{8,9},{9,8},{10,11... | collective-permute-start | bytes 1572872 | tf_op jit(solution)/shard_map/ppermute | solution.py:460
  0.7 2.5 %collective-permute-start.1 = (bf16[256,1024]{1,0:T(8,128)(2,1)}, bf16[256,1024]{1,0:T(8,128)(2,1)S(1)}, u32[]{:S(2)}, u32[]{:S(2)}) collective-permute-start(bf16[256,1024]{1,0:T(8,128)(2,1)} %k.1), channel_id=1, source_target_pairs={{0,1},{1,0},{2,3},{3,2},{4,5},{5,4},{6,7},{7,6},{8,9},{9,8},{10,11... | collective-permute-start | bytes 1572872 | tf_op jit(solution)/shard_map/ppermute | solution.py:460
  0.7 3.2 %collective-permute-start.2 = (bf16[256,1024]{1,0:T(8,128)(2,1)}, bf16[256,1024]{1,0:T(8,128)(2,1)S(1)}, u32[]{:S(2)}, u32[]{:S(2)}) collective-permute-start(bf16[256,1024]{1,0:T(8,128)(2,1)} %v.1), channel_id=1, source_target_pairs={{0,1},{1,0},{2,3},{3,2},{4,5},{5,4},{6,7},{7,6},{8,9},{9,8},{10,11... | collective-permute-start | bytes 1572872 | tf_op jit(solution)/shard_map/ppermute | solution.py:460
  5.6 24.6 %all-to-all-start = ((bf16[8,224,128]{2,1,0:T(8,128)(2,1)}), bf16[8,224,128]{2,1,0:T(8,128)(2,1)S(1)}, u32[]{:S(2)}, u32[]{:S(2)}) async-start(bf16[8,224,128]{2,1,0:T(8,128)(2,1)} %shard_map.38), calls=%async_computation | async-start | bytes 917504 | tf_op jit(solution)/shard_map/all_to_all | solution.py:468
  16.0 32.9 %collective-permute-start.4 = (bf16[896,512]{1,0:T(8,128)(2,1)}, bf16[896,512]{1,0:T(8,128)(2,1)}, u32[]{:S(2)}, u32[]{:S(2)}) collective-permute-start(bf16[896,512]{1,0:T(8,128)(2,1)} %get-tuple-element.20), channel_id=1, source_target_pairs={{0,2},{1,3},{2,4},{3,5},{4,6},{5,7},{6,8},{7,9},{8,10},{9,11},{10,... | collective-permute-start | bytes 2752520 | tf_op jit(solution)/shard_map/ppermute | solution.py:460
  19.4 29.5 %collective-permute-start.5 = (bf16[896,512]{1,0:T(8,128)(2,1)}, bf16[896,512]{1,0:T(8,128)(2,1)}, u32[]{:S(2)}, u32[]{:S(2)}) collective-permute-start(bf16[896,512]{1,0:T(8,128)(2,1)} %get-tuple-element.21), channel_id=1, source_target_pairs={{2,0},{3,1},{4,2},{5,3},{6,4},{7,5},{8,6},{9,7},{10,8},{11,9},{12,... | collective-permute-start | bytes 2752520 | tf_op jit(solution)/shard_map/ppermute | solution.py:460
  30.2 6.6 %copy-start = (bf16[8,224,128]{2,1,0:T(8,128)(2,1)}, bf16[8,224,128]{2,1,0:T(8,128)(2,1)S(1)}, u32[]{:S(2)}) copy-start(bf16[8,224,128]{2,1,0:T(8,128)(2,1)S(1)} %all-to-all-done.refs_0_) | copy-start | bytes 1376260
  30.8 10.4 %collective-permute-start.3 = (bf16[1024,128]{1,0:T(8,128)(2,1)S(1)}, bf16[1024,128]{1,0:T(8,128)(2,1)S(1)}, u32[]{:S(2)}, u32[]{:S(2)}) collective-permute-start(bf16[1024,128]{1,0:T(8,128)(2,1)S(1)} %shard_map.40), channel_id=1, source_target_pairs={{8,24},{9,25},{10,26},{11,27},{12,28},{13,29},{14,30},{15,31},{16,... | collective-permute-start | bytes 786440 | tf_op jit(solution)/shard_map/ppermute | solution.py:460
  36.8 18.7 %collective-permute-start.6 = (bf16[256,512]{1,0:T(8,128)(2,1)}, bf16[256,512]{1,0:T(8,128)(2,1)}, u32[]{:S(2)}, u32[]{:S(2)}) collective-permute-start(bf16[256,512]{1,0:T(8,128)(2,1)} %shard_map.41), channel_id=1, source_target_pairs={{0,4},{1,5},{4,8},{5,9},{6,2},{7,3},{8,12},{9,13},{10,6},{11,7},{1... | collective-permute-start | bytes 786440 | tf_op jit(solution)/shard_map/ppermute | solution.py:460
  38.7 2.5 %copy-start.1 = (bf16[8,224,128]{2,1,0:T(8,128)(2,1)S(1)}, bf16[8,224,128]{2,1,0:T(8,128)(2,1)}, u32[]{:S(2)}) copy-start(bf16[8,224,128]{2,1,0:T(8,128)(2,1)} %copy-done) | copy-start | bytes 1376260
  43.3 19.1 %all-to-all-start.1 = ((bf16[8,112,128]{2,1,0:T(8,128)(2,1)}), bf16[8,112,128]{2,1,0:T(8,128)(2,1)S(1)}, u32[]{:S(2)}, u32[]{:S(2)}) async-start(bf16[8,112,128]{2,1,0:T(8,128)(2,1)} %shard_map.43), calls=%async_computation.1 | async-start | bytes 458752 | tf_op jit(solution)/shard_map/all_to_all | solution.py:468
  57.9 4.5 %collective-permute-start.7 = (bf16[128,640]{1,0:T(8,128)(2,1)S(1)}, bf16[128,640]{1,0:T(8,128)(2,1)S(1)}, u32[]{:S(2)}, u32[]{:S(2)}) collective-permute-start(bf16[128,640]{1,0:T(8,128)(2,1)S(1)} %get-tuple-element.28), channel_id=1, source_target_pairs={{0,2},{1,3},{2,0},{3,1},{4,6},{5,7},{6,4},{7,5},{8,10},{9,11},{10,... | collective-permute-start | bytes 491528 | tf_op jit(solution)/shard_map/ppermute | solution.py:460
  65.2 4.4 %collective-permute-start.8 = (bf16[256,512]{1,0:T(8,128)(2,1)S(1)}, bf16[256,512]{1,0:T(8,128)(2,1)S(1)}, u32[]{:S(2)}, u32[]{:S(2)}) collective-permute-start(bf16[256,512]{1,0:T(8,128)(2,1)S(1)} %get-tuple-element.32), channel_id=1, source_target_pairs={{0,1},{1,0},{2,3},{3,2},{4,5},{5,4},{6,7},{7,6},{8,9},{9,8},{10,11... | collective-permute-start | bytes 786440 | tf_op jit(solution)/shard_map/ppermute | solution.py:460

commit v5 on v4

--- a/solution.py
+++ b/solution.py
@@ -260,7 +260,7 @@
     return left, right
 
 
-def far_body(s, near, rin, lin, out):
+def far_body(s, near, rin, lin, out, two_in, one_in):
     first = s[0] == 0
     bias_left, bias_right = sides(s)
     for at in (0, 1):
@@ -283,16 +283,26 @@
         )
 
 
-def one_body(s, near, far, rin, lin, out, one):
+    odd = s[7] == 1
+    for at in (0, 1):
+        two_in[at * 64 : (at + 1) * 64] = pooled(near[at * B : (at + 1) * B, PACK:], 2, True)
+    two_in[128:B] = jnp.where(odd, rin[EDGE:], lin[EDGE:])
+    beside = jnp.where(odd, lin[:EDGE], rin[:EDGE])
+    for n in (0, 1):
+        two_in[B + n * 128 : B + (n + 1) * 128] = level_two(beside, n)
+    for i, ref in enumerate((rin, lin)):
+        for n in (0, 1):
+            rows = (2 * i + n) * B
+            one_in[rows : rows + 128] = pooled(ref[n * B : (n + 1) * B], 1, n == 0)
+            one_in[rows + 128 : rows + B] = ref[2 * B + n * 128 : 2 * B + (n + 1) * 128]
+
+
+def one_body(s, near, far, one_in, out, one):
     def coarse(cols):
-        parts = []
-        for ref, bias in zip((rin, lin), sides(s)):
-            keys = pooled(ref[:B, cols], 1, True)
-            values = pooled(ref[B : 2 * B, cols], 1, False)
-            keys = jnp.concatenate([keys, ref[2 * B : 2 * B + 128, cols]], axis=0)
-            values = jnp.concatenate([values, ref[2 * B + 128 : EDGE, cols]], axis=0)
-            parts.append((keys, values, bias))
-        return parts
+        return [
+            (one_in[2 * i * B : (2 * i + 1) * B, cols], one_in[(2 * i + 1) * B : (2 * i + 2) * B, cols], bias)
+            for i, bias in enumerate(sides(s))
+        ]
 
     q_one = jnp.concatenate([pooled(near[at * B : (at + 1) * B, PACK:], 1, True) for at in (0, 1)])
     attend_to(one, 0, lambda cols: q_one[:, cols], coarse, B, 2.0)
@@ -305,19 +315,16 @@
         out[rows, COLS:] = weights
 
 
-def pair_body(s, near, rin, lin, bin_, mine, theirs):
+def pair_body(s, two_in, bin_, mine, theirs):
     bias = jnp.where(s[4] == 1, 0.0, ABSENT).astype(F32)
-    odd = s[7] == 1
-    beside = jnp.where(odd, lin[:EDGE], rin[:EDGE])
     kept = [
-        jnp.concatenate([level_two(beside, n), bin_[n * 128 : (n + 1) * 128]], axis=0)
+        jnp.concatenate(
+            [two_in[B + n * 128 : B + (n + 1) * 128], bin_[n * 128 : (n + 1) * 128]], axis=0
+        )
         for n in (0, 1)
     ]
-    queries = [pooled(near[at * B : (at + 1) * B, PACK:], 2, True) for at in (0, 1)]
-    queries.append(jnp.where(odd, rin[EDGE:], lin[EDGE:]))
-    queries = jnp.concatenate(queries, axis=0)
     spans = [slice(h * DH, (h + 1) * DH) for h in range(HEADS)]
-    jobs = [(queries[:, cols], [(kept[0][:, cols], kept[1][:, cols], bias)]) for cols in spans]
+    jobs = [(two_in[:B, cols], [(kept[0][:, cols], kept[1][:, cols], bias)]) for cols in spans]
     values = []
     for cols, (o, value) in zip(spans, attend(jobs, 4.0)):
         mine[:, cols] = o[:128]
@@ -519,18 +526,21 @@
     (back,) = call(row_body, (shaped(RING, BACK, DH),), s, (ain, xin))
     row_back = line_swap(back)
     s, _ = after(s, back)
-    (far,) = call(far_body, (shaped(2 * B, PACK),), s, (near, rin, lin))
+    far, two_in, one_in = call(
+        far_body,
+        (shaped(2 * B, PACK), shaped(2 * B, COLS), shaped(4 * B, COLS)),
+        s,
+        (near, rin, lin),
+    )
     s, _ = after(s, far)
-    two, theirs = call(
-        pair_body, (shaped(128, PACK), shaped(128, PACK)), s, (near, rin, lin, bin_)
-    )
+    two, theirs = call(pair_body, (shaped(128, PACK), shaped(128, PACK)), s, (two_in, bin_))
     two_back = send_to(theirs, PAIR)
     s, _ = after(s, theirs)
     (fine,) = call(
         one_body,
         (jax.ShapeDtypeStruct((2 * B, PACK), F32),),
         s,
-        (near, far, rin, lin),
+        (near, far, one_in),
         extra=[pltpu.VMEM((B, PACK), BF16)],
     )
     mine, send = call(

time: 71.6 us -> 71.2 us (level)
  Pallas kernels: 25.9 us -> 24.7 us
    pallas_call x10, Pallas kernels: 22.9 us -> 21.7 us  [call(): pl.pallas_call(outer, out_shape=[pltpu.HBM(o.shape, o.dtype) for o in out...]
  transfers between devices with their start and end apart: 11 -> 11, of which waited for: 6 -> 7; matrix products, arithmetic and copies ran while one was open for 0% -> 0% of each run, Pallas kernels for 28% -> 27%
where the time goes in v5:
time: 71.2 us; the launch traced here: 70.8 us
  starting transfers between devices  32.8 us (46%)
  Pallas kernels  24.7 us (35%)
  waiting for transfers between devices  12.9 us (18%)
    pallas_call x10, Pallas kernels, call(): pl.pallas_call(outer, out_shape=[pltpu.HBM(o.shape, o.dtype) for o in out...  21.7 us
    ppermute x9, starting transfers between devices, send_to(): return lax.ppermute(x, 'seq', pairs)  21.2 us
    all_to_all x2, starting transfers between devices, line_swap(): return lax.all_to_all(x, 'seq', 0, 0, axis_index_groups=LINES)  11.7 us
    ppermute x9, waiting for transfers between devices, send_to(): return lax.ppermute(x, 'seq', pairs)  8.21 us
    all_to_all x2, waiting for transfers between devices, line_swap(): return lax.all_to_all(x, 'seq', 0, 0, axis_index_groups=LINES)  4.66 us
    pallas_call x1, Pallas kernels, half_columns(): pl.pallas_call(half_body, out_shape=shaped(3, B, COLS), in_specs=[pl.Bloc...  1.68 us
  transfers between devices with their start and end apart: 11, of which 7 were waited for; matrix products, arithmetic and copies ran while one was open for 0% of the time, Pallas kernels for 27%

profile of v5, /device:TPU:25, one launch (start us, length us, event | category | flops | bytes accessed | tf_op | source)
XLA Modules:
  0.0 70.8 jit_solution(16803921728750315962)
XLA Ops:
  0.0 0.7 collective-permute-start
  0.7 0.0 collective-permute-start.1
  0.7 0.5 collective-permute-start.2
  1.2 0.1 stack.51.s
  1.3 1.7 %shard_map.37.refs_0_ = bf16[3,256,512]{2,1,0:T(8,128)(2,1)S(1)} custom-call(s32[8]{0:T(128)S(1)} %stack.51.s, bf16[256,1024]{1,0:T(8,128)(2,1)} %q.1, bf16[256,1024]{1,0:T(8,128)(2,1)} %k.1, bf16[256,1024]{1,0:T(8,128)(2,1)} %v.1), custom_call_target="tpu_custom_call" | custom-call | tf_op jit(solution)/shard_map/pallas_call | solution.py:67
  3.0 0.0 collective-permute-done.refs_1_
  3.0 0.2 collective-permute-done.1.refs_2_.refs_1_
  3.2 0.7 %collective-permute-done.2.refs_3_.refs_2_ = bf16[256,1024]{1,0:T(8,128)(2,1)S(1)} collective-permute-done((bf16[256,1024]{1,0:T(8,128)(2,1)}, bf16[256,1024]{1,0:T(8,128)(2,1)S(1)}, u32[]{:S(2)}, u32[]{:S(2)}) %collective-permute-start.2) | collective-permute-done | bytes 524320 | tf_op jit(solution)/shard_map/ppermute | solution.py:467
  3.9 1.7 %shard_map.38 = bf16[8,224,128]{2,1,0:T(8,128)(2,1)} custom-call(s32[8]{0:T(128)S(1)} %stack.51.s, bf16[3,256,512]{2,1,0:T(8,128)(2,1)S(1)} %shard_map.37.refs_0_, bf16[256,1024]{1,0:T(8,128)(2,1)S(1)} %collective-permute-done.refs_1_, bf16[256,1024]{1,0:T(8,128)(2,1)S(1)} %collective-permute-done.1.refs_2_.refs_1_, ...), custom_call_target="tpu_custom_call" | custom-call | tf_op jit(solution)/shard_map/pallas_call | solution.py:42
  5.6 8.2 %all-to-all-start = ((bf16[8,224,128]{2,1,0:T(8,128)(2,1)}), bf16[8,224,128]{2,1,0:T(8,128)(2,1)S(1)}, u32[]{:S(2)}, u32[]{:S(2)}) async-start(bf16[8,224,128]{2,1,0:T(8,128)(2,1)} %shard_map.38), calls=%async_computation | async-start | bytes 917504 | tf_op jit(solution)/shard_map/all_to_all | solution.py:475
  13.8 2.2 %shard_map.39 = (bf16[896,512]{1,0:T(8,128)(2,1)}, bf16[896,512]{1,0:T(8,128)(2,1)}) custom-call(s32[8]{0:T(128)S(1)} %stack.51.s, bf16[3,256,512]{2,1,0:T(8,128)(2,1)S(1)} %shard_map.37.refs_0_, bf16[256,1024]{1,0:T(8,128)(2,1)S(1)} %collective-permute-done.refs_1_, bf16[256,1024]{1,0:T(8,128)(2,1)S(1)} %collective-permute-done.1.refs_2_.refs_1_, ...), custom_call_target="tpu_custom_call" | custom-call | tf_op jit(solution)/shard_map/pallas_call | solution.py:42
  16.0 3.4 %collective-permute-start.4 = (bf16[896,512]{1,0:T(8,128)(2,1)}, bf16[896,512]{1,0:T(8,128)(2,1)}, u32[]{:S(2)}, u32[]{:S(2)}) collective-permute-start(bf16[896,512]{1,0:T(8,128)(2,1)} %get-tuple-element.23), channel_id=1, source_target_pairs={{0,2},{1,3},{2,4},{3,5},{4,6},{5,7},{6,8},{7,9},{8,10},{9,11},{10,... | collective-permute-start | bytes 2752520 | tf_op jit(solution)/shard_map/ppermute | solution.py:467
  19.4 6.1 %collective-permute-start.5 = (bf16[896,512]{1,0:T(8,128)(2,1)}, bf16[896,512]{1,0:T(8,128)(2,1)}, u32[]{:S(2)}, u32[]{:S(2)}) collective-permute-start(bf16[896,512]{1,0:T(8,128)(2,1)} %get-tuple-element.24), channel_id=1, source_target_pairs={{2,0},{3,1},{4,2},{5,3},{6,4},{7,5},{8,6},{9,7},{10,8},{11,9},{12,... | collective-permute-start | bytes 2752520 | tf_op jit(solution)/shard_map/ppermute | solution.py:467
  25.5 4.7 %all-to-all-done.refs_0_ = bf16[8,224,128]{2,1,0:T(8,128)(2,1)S(1)} async-done(((bf16[8,224,128]{2,1,0:T(8,128)(2,1)}), bf16[8,224,128]{2,1,0:T(8,128)(2,1)S(1)}, u32[]{:S(2)}, u32[]{:S(2)}) %all-to-all-start) | async-done | bytes 458784 | tf_op jit(solution)/shard_map/all_to_all | solution.py:475
  30.2 0.0 copy-start
  30.2 0.6 shard_map.40
  30.8 4.5 %collective-permute-start.3 = (bf16[1024,128]{1,0:T(8,128)(2,1)S(1)}, bf16[1024,128]{1,0:T(8,128)(2,1)S(1)}, u32[]{:S(2)}, u32[]{:S(2)}) collective-permute-start(bf16[1024,128]{1,0:T(8,128)(2,1)S(1)} %shard_map.40), channel_id=1, source_target_pairs={{8,24},{9,25},{10,26},{11,27},{12,28},{13,29},{14,30},{15,31},{16,... | collective-permute-start | bytes 786440 | tf_op jit(solution)/shard_map/ppermute | solution.py:467
  35.2 1.6 %shard_map.41 = bf16[256,512]{1,0:T(8,128)(2,1)} custom-call(s32[8]{0:T(128)S(1)} %stack.51.s, bf16[3,256,512]{2,1,0:T(8,128)(2,1)S(1)} %shard_map.37.refs_0_, bf16[256,1024]{1,0:T(8,128)(2,1)S(1)} %collective-permute-done.1.refs_2_.refs_1_, bf16[256,1024]{1,0:T(8,128)(2,1)S(1)} %collective-permute-done.2.refs_3_.refs_2_), custom_call_target="tpu_custom_call" | custom-call | tf_op jit(solution)/shard_map/pallas_call | solution.py:42
  36.8 0.0 copy-done
  36.8 1.9 %collective-permute-start.6 = (bf16[256,512]{1,0:T(8,128)(2,1)}, bf16[256,512]{1,0:T(8,128)(2,1)}, u32[]{:S(2)}, u32[]{:S(2)}) collective-permute-start(bf16[256,512]{1,0:T(8,128)(2,1)} %shard_map.41), channel_id=1, source_target_pairs={{0,4},{1,5},{4,8},{5,9},{6,2},{7,3},{8,12},{9,13},{10,6},{11,7},{1... | collective-permute-start | bytes 786440 | tf_op jit(solution)/shard_map/ppermute | solution.py:467
  38.7 0.0 copy-start.1
  38.7 2.5 %shard_map.42.refs_0_ = bf16[512,1152]{1,0:T(8,128)(2,1)S(1)} custom-call(s32[8]{0:T(128)S(1)} %stack.51.s, bf16[3,256,512]{2,1,0:T(8,128)(2,1)S(1)} %shard_map.37.refs_0_, bf16[256,1024]{1,0:T(8,128)(2,1)S(1)} %collective-permute-done.refs_1_, bf16[256,1024]{1,0:T(8,128)(2,1)S(1)} %collective-permute-done.1.refs_2_.refs_1_, ...), custom_call_target="tpu_custom_call" | custom-call | tf_op jit(solution)/shard_map/pallas_call | solution.py:42
  41.2 0.0 collective-permute-done.3.refs_1_
  41.2 0.0 copy-done.1
  41.2 2.1 %shard_map.43 = bf16[8,112,128]{2,1,0:T(8,128)(2,1)} custom-call(s32[8]{0:T(128)S(1)} %stack.51.s, bf16[8,224,128]{2,1,0:T(8,128)(2,1)S(1)} %copy-done.1, bf16[1024,128]{1,0:T(8,128)(2,1)S(1)} %collective-permute-done.3.refs_1_), custom_call_target="tpu_custom_call" | custom-call | tf_op jit(solution)/shard_map/pallas_call | solution.py:42
  43.3 3.5 %all-to-all-start.1 = ((bf16[8,112,128]{2,1,0:T(8,128)(2,1)}), bf16[8,112,128]{2,1,0:T(8,128)(2,1)S(1)}, u32[]{:S(2)}, u32[]{:S(2)}) async-start(bf16[8,112,128]{2,1,0:T(8,128)(2,1)} %shard_map.43), calls=%async_computation.1 | async-start | bytes 458752 | tf_op jit(solution)/shard_map/all_to_all | solution.py:475
  46.8 2.1 %collective-permute-done.4.refs_1_ = bf16[896,512]{1,0:T(8,128)(2,1)} collective-permute-done((bf16[896,512]{1,0:T(8,128)(2,1)}, bf16[896,512]{1,0:T(8,128)(2,1)}, u32[]{:S(2)}, u32[]{:S(2)}) %collective-permute-start.4) | collective-permute-done | bytes 917536 | tf_op jit(solution)/shard_map/ppermute | solution.py:467
  48.9 0.0 collective-permute-done.5.refs_2_
  48.9 3.4 %shard_map.44 = (bf16[512,640]{1,0:T(8,128)(2,1)S(1)}, bf16[512,512]{1,0:T(8,128)(2,1)S(1)}, bf16[1024,512]{1,0:T(8,128)(2,1)S(1)}) custom-call(s32[8]{0:T(128)S(1)} %stack.51.s, bf16[512,1152]{1,0:T(8,128)(2,1)S(1)} %shard_map.42.refs_0_, bf16[896,512]{1,0:T(8,128)(2,1)} %collective-permute-done.4.refs_1_, bf16[896,512]{1,0:T(8,128)(2,1)} %collective-permute-done.5.refs_2_), custom_call_target="tpu_custom_call" | custom-call | tf_op jit(solution)/shard_map/pallas_call | solution.py:42
  52.3 3.2 %collective-permute-done.6.refs_1_ = bf16[256,512]{1,0:T(8,128)(2,1)} collective-permute-done((bf16[256,512]{1,0:T(8,128)(2,1)}, bf16[256,512]{1,0:T(8,128)(2,1)}, u32[]{:S(2)}, u32[]{:S(2)}) %collective-permute-start.6) | collective-permute-done | bytes 262176 | tf_op jit(solution)/shard_map/ppermute | solution.py:467
  55.5 1.6 %shard_map.45 = (bf16[128,640]{1,0:T(8,128)(2,1)S(1)}, bf16[128,640]{1,0:T(8,128)(2,1)S(1)}) custom-call(s32[8]{0:T(128)S(1)} %stack.51.s, bf16[512,512]{1,0:T(8,128)(2,1)S(1)} %get-tuple-element.32.refs_0_, bf16[256,512]{1,0:T(8,128)(2,1)} %collective-permute-done.6.refs_1_), custom_call_target="tpu_custom_call" | custom-call | tf_op jit(solution)/shard_map/pallas_call | solution.py:42
  57.0 0.3 collective-permute-start.7
  57.3 3.4 %shard_map.46.refs_0_ = f32[512,640]{1,0:T(8,128)S(1)} custom-call(s32[8]{0:T(128)S(1)} %stack.51.s, bf16[512,1152]{1,0:T(8,128)(2,1)S(1)} %shard_map.42.refs_0_, bf16[512,640]{1,0:T(8,128)(2,1)S(1)} %get-tuple-element.30.refs_1_, bf16[1024,512]{1,0:T(8,128)(2,1)S(1)} %get-tuple-element.35.refs_2_), custom_call_target="tpu_custom_call" | custom-call | tf_op jit(solution)/shard_map/pallas_call | solution.py:42
  60.7 0.8 %collective-permute-done.7.refs_2_ = bf16[128,640]{1,0:T(8,128)(2,1)S(1)} collective-permute-done((bf16[128,640]{1,0:T(8,128)(2,1)S(1)}, bf16[128,640]{1,0:T(8,128)(2,1)S(1)}, u32[]{:S(2)}, u32[]{:S(2)}) %collective-permute-start.7) | collective-permute-done | bytes 163872 | tf_op jit(solution)/shard_map/ppermute | solution.py:467
  61.5 0.0 all-to-all-done.1.refs_3_
  61.5 2.8 %shard_map.47 = (bf16[256,512]{1,0:T(8,128)(2,1)S(1)}, bf16[256,512]{1,0:T(8,128)(2,1)S(1)}) custom-call(s32[8]{0:T(128)S(1)} %stack.51.s, f32[512,640]{1,0:T(8,128)S(1)} %shard_map.46.refs_0_, bf16[128,640]{1,0:T(8,128)(2,1)S(1)} %get-tuple-element.36.refs_1_, bf16[128,640]{1,0:T(8,128)(2,1)S(1)} %collective-permute-done.7.refs_2_, ...), custom_call_target="tpu_custom_call" | custom-call | tf_op jit(solution)/shard_map/pallas_call | solution.py:42
  64.3 3.8 %collective-permute-start.8 = (bf16[256,512]{1,0:T(8,128)(2,1)S(1)}, bf16[256,512]{1,0:T(8,128)(2,1)S(1)}, u32[]{:S(2)}, u32[]{:S(2)}) collective-permute-start(bf16[256,512]{1,0:T(8,128)(2,1)S(1)} %get-tuple-element.38), channel_id=1, source_target_pairs={{0,1},{1,0},{2,3},{3,2},{4,5},{5,4},{6,7},{7,6},{8,9},{9,8},{10,11... | collective-permute-start | bytes 786440 | tf_op jit(solution)/shard_map/ppermute | solution.py:467
  68.1 1.2 %collective-permute-done.8.theirs = bf16[256,512]{1,0:T(8,128)(2,1)S(1)} collective-permute-done((bf16[256,512]{1,0:T(8,128)(2,1)S(1)}, bf16[256,512]{1,0:T(8,128)(2,1)S(1)}, u32[]{:S(2)}, u32[]{:S(2)}) %collective-permute-start.8) | collective-permute-done | bytes 262176 | tf_op jit(solution)/shard_map/ppermute | solution.py:467
  69.3 1.3 %shard_map.48 = bf16[256,1024]{1,0:T(8,128)(2,1)} custom-call(s32[8]{0:T(128)S(1)} %stack.51.s, bf16[256,512]{1,0:T(8,128)(2,1)S(1)} %get-tuple-element.37.mine, bf16[256,512]{1,0:T(8,128)(2,1)S(1)} %collective-permute-done.8.theirs), custom_call_target="tpu_custom_call" | custom-call | tf_op jit(solution)/shard_map/pallas_call | solution.py:433
Async XLA Ops:
  0.0 3.0 %collective-permute-start = (bf16[256,1024]{1,0:T(8,128)(2,1)}, bf16[256,1024]{1,0:T(8,128)(2,1)S(1)}, u32[]{:S(2)}, u32[]{:S(2)}) collective-permute-start(bf16[256,1024]{1,0:T(8,128)(2,1)} %q.1), channel_id=1, source_target_pairs={{0,1},{1,0},{2,3},{3,2},{4,5},{5,4},{6,7},{7,6},{8,9},{9,8},{10,11... | collective-permute-start | bytes 1572872 | tf_op jit(solution)/shard_map/ppermute | solution.py:467
  0.7 2.5 %collective-permute-start.1 = (bf16[256,1024]{1,0:T(8,128)(2,1)}, bf16[256,1024]{1,0:T(8,128)(2,1)S(1)}, u32[]{:S(2)}, u32[]{:S(2)}) collective-permute-start(bf16[256,1024]{1,0:T(8,128)(2,1)} %k.1), channel_id=1, source_target_pairs={{0,1},{1,0},{2,3},{3,2},{4,5},{5,4},{6,7},{7,6},{8,9},{9,8},{10,11... | collective-permute-start | bytes 1572872 | tf_op jit(solution)/shard_map/ppermute | solution.py:467
  0.7 3.2 %collective-permute-start.2 = (bf16[256,1024]{1,0:T(8,128)(2,1)}, bf16[256,1024]{1,0:T(8,128)(2,1)S(1)}, u32[]{:S(2)}, u32[]{:S(2)}) collective-permute-start(bf16[256,1024]{1,0:T(8,128)(2,1)} %v.1), channel_id=1, source_target_pairs={{0,1},{1,0},{2,3},{3,2},{4,5},{5,4},{6,7},{7,6},{8,9},{9,8},{10,11... | collective-permute-start | bytes 1572872 | tf_op jit(solution)/shard_map/ppermute | solution.py:467
  5.6 24.6 %all-to-all-start = ((bf16[8,224,128]{2,1,0:T(8,128)(2,1)}), bf16[8,224,128]{2,1,0:T(8,128)(2,1)S(1)}, u32[]{:S(2)}, u32[]{:S(2)}) async-start(bf16[8,224,128]{2,1,0:T(8,128)(2,1)} %shard_map.38), calls=%async_computation | async-start | bytes 917504 | tf_op jit(solution)/shard_map/all_to_all | solution.py:475
  16.0 32.9 %collective-permute-start.4 = (bf16[896,512]{1,0:T(8,128)(2,1)}, bf16[896,512]{1,0:T(8,128)(2,1)}, u32[]{:S(2)}, u32[]{:S(2)}) collective-permute-start(bf16[896,512]{1,0:T(8,128)(2,1)} %get-tuple-element.23), channel_id=1, source_target_pairs={{0,2},{1,3},{2,4},{3,5},{4,6},{5,7},{6,8},{7,9},{8,10},{9,11},{10,... | collective-permute-start | bytes 2752520 | tf_op jit(solution)/shard_map/ppermute | solution.py:467
  19.4 29.5 %collective-permute-start.5 = (bf16[896,512]{1,0:T(8,128)(2,1)}, bf16[896,512]{1,0:T(8,128)(2,1)}, u32[]{:S(2)}, u32[]{:S(2)}) collective-permute-start(bf16[896,512]{1,0:T(8,128)(2,1)} %get-tuple-element.24), channel_id=1, source_target_pairs={{2,0},{3,1},{4,2},{5,3},{6,4},{7,5},{8,6},{9,7},{10,8},{11,9},{12,... | collective-permute-start | bytes 2752520 | tf_op jit(solution)/shard_map/ppermute | solution.py:467
  30.2 6.6 %copy-start = (bf16[8,224,128]{2,1,0:T(8,128)(2,1)}, bf16[8,224,128]{2,1,0:T(8,128)(2,1)S(1)}, u32[]{:S(2)}) copy-start(bf16[8,224,128]{2,1,0:T(8,128)(2,1)S(1)} %all-to-all-done.refs_0_) | copy-start | bytes 1376260
  30.8 10.4 %collective-permute-start.3 = (bf16[1024,128]{1,0:T(8,128)(2,1)S(1)}, bf16[1024,128]{1,0:T(8,128)(2,1)S(1)}, u32[]{:S(2)}, u32[]{:S(2)}) collective-permute-start(bf16[1024,128]{1,0:T(8,128)(2,1)S(1)} %shard_map.40), channel_id=1, source_target_pairs={{8,24},{9,25},{10,26},{11,27},{12,28},{13,29},{14,30},{15,31},{16,... | collective-permute-start | bytes 786440 | tf_op jit(solution)/shard_map/ppermute | solution.py:467
  36.8 18.7 %collective-permute-start.6 = (bf16[256,512]{1,0:T(8,128)(2,1)}, bf16[256,512]{1,0:T(8,128)(2,1)}, u32[]{:S(2)}, u32[]{:S(2)}) collective-permute-start(bf16[256,512]{1,0:T(8,128)(2,1)} %shard_map.41), channel_id=1, source_target_pairs={{0,4},{1,5},{4,8},{5,9},{6,2},{7,3},{8,12},{9,13},{10,6},{11,7},{1... | collective-permute-start | bytes 786440 | tf_op jit(solution)/shard_map/ppermute | solution.py:467
  38.7 2.5 %copy-start.1 = (bf16[8,224,128]{2,1,0:T(8,128)(2,1)S(1)}, bf16[8,224,128]{2,1,0:T(8,128)(2,1)}, u32[]{:S(2)}) copy-start(bf16[8,224,128]{2,1,0:T(8,128)(2,1)} %copy-done) | copy-start | bytes 1376260
  43.3 18.2 %all-to-all-start.1 = ((bf16[8,112,128]{2,1,0:T(8,128)(2,1)}), bf16[8,112,128]{2,1,0:T(8,128)(2,1)S(1)}, u32[]{:S(2)}, u32[]{:S(2)}) async-start(bf16[8,112,128]{2,1,0:T(8,128)(2,1)} %shard_map.43), calls=%async_computation.1 | async-start | bytes 458752 | tf_op jit(solution)/shard_map/all_to_all | solution.py:475
  57.0 4.4 %collective-permute-start.7 = (bf16[128,640]{1,0:T(8,128)(2,1)S(1)}, bf16[128,640]{1,0:T(8,128)(2,1)S(1)}, u32[]{:S(2)}, u32[]{:S(2)}) collective-permute-start(bf16[128,640]{1,0:T(8,128)(2,1)S(1)} %get-tuple-element.33), channel_id=1, source_target_pairs={{0,2},{1,3},{2,0},{3,1},{4,6},{5,7},{6,4},{7,5},{8,10},{9,11},{10,... | collective-permute-start | bytes 491528 | tf_op jit(solution)/shard_map/ppermute | solution.py:467
  64.3 5.0 %collective-permute-start.8 = (bf16[256,512]{1,0:T(8,128)(2,1)S(1)}, bf16[256,512]{1,0:T(8,128)(2,1)S(1)}, u32[]{:S(2)}, u32[]{:S(2)}) collective-permute-start(bf16[256,512]{1,0:T(8,128)(2,1)S(1)} %get-tuple-element.38), channel_id=1, source_target_pairs={{0,1},{1,0},{2,3},{3,2},{4,5},{5,4},{6,7},{7,6},{8,9},{9,8},{10,11... | collective-permute-start | bytes 786440 | tf_op jit(solution)/shard_map/ppermute | solution.py:467

commit v6 on v5

--- a/solution.py
+++ b/solution.py
@@ -381,7 +381,7 @@
         back[j, ROWS4 + ROWS3 :] = three.astype(BF16)
 
 
-def merge_body(s, fine, two, two_back, row_back, mine, send):
+def merge_body(s, fine, two, two_back, row_back, send, kept):
     low = (1 - s[1]) * HEADS
     row = lax.broadcasted_iota(jnp.int32, (ROWS4 + ROWS3, 128), 0)
     lane = lax.broadcasted_iota(jnp.int32, (ROWS4 + ROWS3, 128), 1)
@@ -407,38 +407,60 @@
     ]
     outs, weights = merged(terms)
     coarse = jnp.concatenate([o.astype(BF16) for o in outs] + [packed_tile(weights)], axis=1)
-    for at, out in enumerate((mine, send)):
-        rows = slice(at * B, (at + 1) * B)
-        outs, _ = merged(
-            [(fine[rows, :COLS], fine[rows, COLS:]), spread(coarse[at * 64 : (at + 1) * 64], B, 2)]
-        )
-        for h in range(HEADS):
-            out[:, h * DH : (h + 1) * DH] = outs[h].astype(BF16)
-
-
-def join_body(s, mine, theirs, out, sems):
+    kept[...] = coarse[:64]
+    finish(fine, B, coarse[64:], send)
+
+
+def finish(fine, start, coarse, out):
+    rows = slice(start, start + B)
+    outs, _ = merged([(fine[rows, :COLS], fine[rows, COLS:]), spread(coarse, B, 2)])
+    for h in range(HEADS):
+        out[:, h * DH : (h + 1) * DH] = outs[h].astype(BF16)
+
+
+def own_body(s, fine, kept, out, mine, sem):
+    finish(fine, 0, kept[...], mine)
     low = pl.multiple_of(s[0] * COLS, COLS)
-    high = pl.multiple_of((1 - s[0]) * COLS, COLS)
-    copies = [
-        pltpu.make_async_copy(mine, out.at[:, pl.ds(low, COLS)], sems.at[0]),
-        pltpu.make_async_copy(theirs, out.at[:, pl.ds(high, COLS)], sems.at[1]),
-    ]
-    for copy in copies:
-        copy.start()
-    for copy in copies:
-        copy.wait()
-
-
-def join(s, mine, theirs):
+    copy = pltpu.make_async_copy(mine, out.at[:, pl.ds(low, COLS)], sem)
+    copy.start()
+    copy.wait()
+
+
+def own_columns(s, fine, kept):
     return pl.pallas_call(
-        join_body,
+        own_body,
         out_shape=shaped(B, 2 * COLS),
         in_specs=[pl.BlockSpec(memory_space=pltpu.SMEM)]
         + [pl.BlockSpec(memory_space=pltpu.VMEM)] * 2,
         out_specs=pl.BlockSpec(memory_space=pl.ANY),
-        scratch_shapes=[pltpu.SemaphoreType.DMA((2,))],
+        scratch_shapes=[pltpu.VMEM((B, COLS), BF16), pltpu.SemaphoreType.DMA],
         compiler_params=pltpu.CompilerParams(vmem_limit_bytes=VMEM_LIMIT),
-    )(s, mine, theirs)
+        cost_estimate=pl.CostEstimate(flops=0, bytes_accessed=0, transcendentals=0),
+    )(s, fine, kept)
+
+
+def join_body(s, part, theirs, out, sem):
+    high = pl.multiple_of((1 - s[0]) * COLS, COLS)
+    copy = pltpu.make_async_copy(theirs, out.at[:, pl.ds(high, COLS)], sem)
+    copy.start()
+    copy.wait()
+
+
+def join(s, part, theirs):
+    return pl.pallas_call(
+        join_body,
+        out_shape=shaped(B, 2 * COLS),
+        in_specs=[
+            pl.BlockSpec(memory_space=pltpu.SMEM),
+            pl.BlockSpec(memory_space=pl.ANY),
+            pl.BlockSpec(memory_space=pltpu.VMEM),
+        ],
+        out_specs=pl.BlockSpec(memory_space=pl.ANY),
+        scratch_shapes=[pltpu.SemaphoreType.DMA],
+        input_output_aliases={1: 0},
+        compiler_params=pltpu.CompilerParams(vmem_limit_bytes=VMEM_LIMIT),
+        cost_estimate=pl.CostEstimate(flops=0, bytes_accessed=0, transcendentals=0),
+    )(s, part, theirs)
 
 
 def pairs_of(target):
@@ -509,20 +531,20 @@
     rin = send_to(rpay, RIGHT)
     lin = send_to(lpay, LEFT)
     s, _ = after(s, (rpay, lpay))
+    (near,) = call(
+        near_body,
+        (shaped(2 * B, PACK + COLS),),
+        s,
+        (own, q1, k1, v1),
+        wide=(1, 2, 3),
+    )
+    s, _ = after(s, near)
     (xpay,) = call(row_pay_body, (shaped(4 * B, DH),), s, (ain,))
     xin = send_to(xpay, ROW)
     s, _ = after(s, xpay)
     (bpay,) = call(block_body, (shaped(B, COLS),), s, (own, k1, v1), wide=(1, 2))
     bin_ = send_to(bpay, BOUND)
     s, _ = after(s, bpay)
-    (near,) = call(
-        near_body,
-        (shaped(2 * B, PACK + COLS),),
-        s,
-        (own, q1, k1, v1),
-        wide=(1, 2, 3),
-    )
-    s, _ = after(s, near)
     (back,) = call(row_body, (shaped(RING, BACK, DH),), s, (ain, xin))
     row_back = line_swap(back)
     s, _ = after(s, back)
@@ -543,10 +565,12 @@
         (near, far, one_in),
         extra=[pltpu.VMEM((B, PACK), BF16)],
     )
-    mine, send = call(
-        merge_body, (shaped(B, COLS), shaped(B, COLS)), s, (fine, two, two_back, row_back)
-    )
-    return join(s, mine, send_to(send, SWAP))
+    send, kept = call(
+        merge_body, (shaped(B, COLS), shaped(64, PACK)), s, (fine, two, two_back, row_back)
+    )
+    theirs = send_to(send, SWAP)
+    s, _ = after(s, send)
+    return join(s, own_columns(s, fine, kept), theirs)
 
 
 def solution(mesh):

time: 71.2 us -> 71 us (level)
  waiting for transfers between devices: 12.9 us -> 11.3 us
  Pallas kernels: 24.7 us -> 25.8 us
    all_to_all x2, waiting for transfers between devices: 4.66 us -> 2.18 us  [line_swap(): return lax.all_to_all(x, 'seq', 0, 0, axis_index_groups=LINES)]
    pallas_call x0 -> x1, Pallas kernels: none -> 1.9 us  [own_columns(): pl.pallas_call(own_body, out_shape=shaped(B, 2 * COLS), in_specs=[pl.Bloc...]
    ppermute x9, waiting for transfers between devices: 8.21 us -> 9.12 us  [send_to(): return lax.ppermute(x, 'seq', pairs)]
    pallas_call x10, Pallas kernels: 21.7 us -> 21 us  [call(): pl.pallas_call(outer, out_shape=[pltpu.HBM(o.shape, o.dtype) for o in out...]
  transfers between devices with their start and end apart: 11 -> 11, of which waited for: 7 -> 7; matrix products, arithmetic and copies ran while one was open for 0% -> 0% of each run, Pallas kernels for 27% -> 29%
where the time goes in v6:
time: 71 us; the launch traced here: 70.5 us
  starting transfers between devices  33 us (46%)
  Pallas kernels  25.8 us (36%)
  waiting for transfers between devices  11.3 us (16%)
    ppermute x9, starting transfers between devices, send_to(): return lax.ppermute(x, 'seq', pairs)  21.4 us
    pallas_call x10, Pallas kernels, call(): pl.pallas_call(outer, out_shape=[pltpu.HBM(o.shape, o.dtype) for o in out...  21 us
    all_to_all x2, starting transfers between devices, line_swap(): return lax.all_to_all(x, 'seq', 0, 0, axis_index_groups=LINES)  11.6 us
    ppermute x9, waiting for transfers between devices, send_to(): return lax.ppermute(x, 'seq', pairs)  9.12 us
    all_to_all x2, waiting for transfers between devices, line_swap(): return lax.all_to_all(x, 'seq', 0, 0, axis_index_groups=LINES)  2.18 us
    pallas_call x1, Pallas kernels, own_columns(): pl.pallas_call(own_body, out_shape=shaped(B, 2 * COLS), in_specs=[pl.Bloc...  1.9 us
    pallas_call x1, Pallas kernels, half_columns(): pl.pallas_call(half_body, out_shape=shaped(3, B, COLS), in_specs=[pl.Bloc...  1.68 us
  transfers between devices with their start and end apart: 11, of which 7 were waited for; matrix products, arithmetic and copies ran while one was open for 0% of the time, Pallas kernels for 29%

profile of v6, /device:TPU:25, one launch (start us, length us, event | category | flops | bytes accessed | tf_op | source)
XLA Modules:
  0.0 70.5 jit_solution(5307572638056392911)
XLA Ops:
  0.0 0.7 collective-permute-start
  0.7 0.0 collective-permute-start.1
  0.7 0.5 collective-permute-start.2
  1.2 0.1 stack.51.s
  1.3 1.7 %shard_map.37.refs_0_ = bf16[3,256,512]{2,1,0:T(8,128)(2,1)S(1)} custom-call(s32[8]{0:T(128)S(1)} %stack.51.s, bf16[256,1024]{1,0:T(8,128)(2,1)} %q.1, bf16[256,1024]{1,0:T(8,128)(2,1)} %k.1, bf16[256,1024]{1,0:T(8,128)(2,1)} %v.1), custom_call_target="tpu_custom_call" | custom-call | tf_op jit(solution)/shard_map/pallas_call | solution.py:67
  3.0 0.0 collective-permute-done.refs_1_
  3.0 0.2 collective-permute-done.1.refs_2_.refs_1_
  3.2 0.7 %collective-permute-done.2.refs_3_.refs_2_ = bf16[256,1024]{1,0:T(8,128)(2,1)S(1)} collective-permute-done((bf16[256,1024]{1,0:T(8,128)(2,1)}, bf16[256,1024]{1,0:T(8,128)(2,1)S(1)}, u32[]{:S(2)}, u32[]{:S(2)}) %collective-permute-start.2) | collective-permute-done | bytes 524320 | tf_op jit(solution)/shard_map/ppermute | solution.py:489
  3.9 1.7 %shard_map.38 = bf16[8,224,128]{2,1,0:T(8,128)(2,1)} custom-call(s32[8]{0:T(128)S(1)} %stack.51.s, bf16[3,256,512]{2,1,0:T(8,128)(2,1)S(1)} %shard_map.37.refs_0_, bf16[256,1024]{1,0:T(8,128)(2,1)S(1)} %collective-permute-done.refs_1_, bf16[256,1024]{1,0:T(8,128)(2,1)S(1)} %collective-permute-done.1.refs_2_.refs_1_, ...), custom_call_target="tpu_custom_call" | custom-call | tf_op jit(solution)/shard_map/pallas_call | solution.py:42
  5.6 8.2 %all-to-all-start = ((bf16[8,224,128]{2,1,0:T(8,128)(2,1)}), bf16[8,224,128]{2,1,0:T(8,128)(2,1)}, u32[]{:S(2)}, u32[]{:S(2)}) async-start(bf16[8,224,128]{2,1,0:T(8,128)(2,1)} %shard_map.38), calls=%async_computation | async-start | bytes 917504 | tf_op jit(solution)/shard_map/all_to_all | solution.py:497
  13.8 2.2 %shard_map.39 = (bf16[896,512]{1,0:T(8,128)(2,1)}, bf16[896,512]{1,0:T(8,128)(2,1)}) custom-call(s32[8]{0:T(128)S(1)} %stack.51.s, bf16[3,256,512]{2,1,0:T(8,128)(2,1)S(1)} %shard_map.37.refs_0_, bf16[256,1024]{1,0:T(8,128)(2,1)S(1)} %collective-permute-done.refs_1_, bf16[256,1024]{1,0:T(8,128)(2,1)S(1)} %collective-permute-done.1.refs_2_.refs_1_, ...), custom_call_target="tpu_custom_call" | custom-call | tf_op jit(solution)/shard_map/pallas_call | solution.py:42
  16.0 3.4 %collective-permute-start.4 = (bf16[896,512]{1,0:T(8,128)(2,1)}, bf16[896,512]{1,0:T(8,128)(2,1)}, u32[]{:S(2)}, u32[]{:S(2)}) collective-permute-start(bf16[896,512]{1,0:T(8,128)(2,1)} %get-tuple-element.24), channel_id=1, source_target_pairs={{0,2},{1,3},{2,4},{3,5},{4,6},{5,7},{6,8},{7,9},{8,10},{9,11},{10,... | collective-permute-start | bytes 2752520 | tf_op jit(solution)/shard_map/ppermute | solution.py:489
  19.4 6.1 %collective-permute-start.5 = (bf16[896,512]{1,0:T(8,128)(2,1)}, bf16[896,512]{1,0:T(8,128)(2,1)}, u32[]{:S(2)}, u32[]{:S(2)}) collective-permute-start(bf16[896,512]{1,0:T(8,128)(2,1)} %get-tuple-element.25), channel_id=1, source_target_pairs={{2,0},{3,1},{4,2},{5,3},{6,4},{7,5},{8,6},{9,7},{10,8},{11,9},{12,... | collective-permute-start | bytes 2752520 | tf_op jit(solution)/shard_map/ppermute | solution.py:489
  25.5 2.5 %shard_map.40.refs_0_ = bf16[512,1152]{1,0:T(8,128)(2,1)S(1)} custom-call(s32[8]{0:T(128)S(1)} %stack.51.s, bf16[3,256,512]{2,1,0:T(8,128)(2,1)S(1)} %shard_map.37.refs_0_, bf16[256,1024]{1,0:T(8,128)(2,1)S(1)} %collective-permute-done.refs_1_, bf16[256,1024]{1,0:T(8,128)(2,1)S(1)} %collective-permute-done.1.refs_2_.refs_1_, ...), custom_call_target="tpu_custom_call" | custom-call | tf_op jit(solution)/shard_map/pallas_call | solution.py:42
  28.0 2.2 %all-to-all-done.refs_0_ = bf16[8,224,128]{2,1,0:T(8,128)(2,1)} async-done(((bf16[8,224,128]{2,1,0:T(8,128)(2,1)}), bf16[8,224,128]{2,1,0:T(8,128)(2,1)}, u32[]{:S(2)}, u32[]{:S(2)}) %all-to-all-start) | async-done | bytes 458784 | tf_op jit(solution)/shard_map/all_to_all | solution.py:497
  30.2 1.0 %shard_map.41 = bf16[1024,128]{1,0:T(8,128)(2,1)S(1)} custom-call(s32[8]{0:T(128)S(1)} %stack.51.s, bf16[8,224,128]{2,1,0:T(8,128)(2,1)} %all-to-all-done.refs_0_), custom_call_target="tpu_custom_call" | custom-call | tf_op jit(solution)/shard_map/pallas_call | solution.py:42
  31.2 4.6 %collective-permute-start.3 = (bf16[1024,128]{1,0:T(8,128)(2,1)S(1)}, bf16[1024,128]{1,0:T(8,128)(2,1)S(1)}, u32[]{:S(2)}, u32[]{:S(2)}) collective-permute-start(bf16[1024,128]{1,0:T(8,128)(2,1)S(1)} %shard_map.41), channel_id=1, source_target_pairs={{8,24},{9,25},{10,26},{11,27},{12,28},{13,29},{14,30},{15,31},{16,... | collective-permute-start | bytes 786440 | tf_op jit(solution)/shard_map/ppermute | solution.py:489
  35.8 0.8 %shard_map.42 = bf16[256,512]{1,0:T(8,128)(2,1)S(1)} custom-call(s32[8]{0:T(128)S(1)} %stack.51.s, bf16[3,256,512]{2,1,0:T(8,128)(2,1)S(1)} %shard_map.37.refs_0_, bf16[256,1024]{1,0:T(8,128)(2,1)S(1)} %collective-permute-done.1.refs_2_.refs_1_, bf16[256,1024]{1,0:T(8,128)(2,1)S(1)} %collective-permute-done.2.refs_3_.refs_2_), custom_call_target="tpu_custom_call" | custom-call | tf_op jit(solution)/shard_map/pallas_call | solution.py:42
  36.7 1.9 %collective-permute-start.6 = (bf16[256,512]{1,0:T(8,128)(2,1)S(1)}, bf16[256,512]{1,0:T(8,128)(2,1)S(1)}, u32[]{:S(2)}, u32[]{:S(2)}) collective-permute-start(bf16[256,512]{1,0:T(8,128)(2,1)S(1)} %shard_map.42), channel_id=1, source_target_pairs={{0,4},{1,5},{4,8},{5,9},{6,2},{7,3},{8,12},{9,13},{10,6},{11,7},{1... | collective-permute-start | bytes 786440 | tf_op jit(solution)/shard_map/ppermute | solution.py:489
  38.6 2.1 %collective-permute-done.3.refs_1_ = bf16[1024,128]{1,0:T(8,128)(2,1)S(1)} collective-permute-done((bf16[1024,128]{1,0:T(8,128)(2,1)S(1)}, bf16[1024,128]{1,0:T(8,128)(2,1)S(1)}, u32[]{:S(2)}, u32[]{:S(2)}) %collective-permute-start.3) | collective-permute-done | bytes 262176 | tf_op jit(solution)/shard_map/ppermute | solution.py:489
  40.6 2.6 %shard_map.43 = bf16[8,112,128]{2,1,0:T(8,128)(2,1)} custom-call(s32[8]{0:T(128)S(1)} %stack.51.s, bf16[8,224,128]{2,1,0:T(8,128)(2,1)} %all-to-all-done.refs_0_, bf16[1024,128]{1,0:T(8,128)(2,1)S(1)} %collective-permute-done.3.refs_1_), custom_call_target="tpu_custom_call" | custom-call | tf_op jit(solution)/shard_map/pallas_call | solution.py:42
  43.2 3.4 %all-to-all-start.1 = ((bf16[8,112,128]{2,1,0:T(8,128)(2,1)}), bf16[8,112,128]{2,1,0:T(8,128)(2,1)S(1)}, u32[]{:S(2)}, u32[]{:S(2)}) async-start(bf16[8,112,128]{2,1,0:T(8,128)(2,1)} %shard_map.43), calls=%async_computation.1 | async-start | bytes 458752 | tf_op jit(solution)/shard_map/all_to_all | solution.py:497
  46.6 2.3 %collective-permute-done.4.refs_1_ = bf16[896,512]{1,0:T(8,128)(2,1)} collective-permute-done((bf16[896,512]{1,0:T(8,128)(2,1)}, bf16[896,512]{1,0:T(8,128)(2,1)}, u32[]{:S(2)}, u32[]{:S(2)}) %collective-permute-start.4) | collective-permute-done | bytes 917536 | tf_op jit(solution)/shard_map/ppermute | solution.py:489
  48.9 0.0 collective-permute-done.5.refs_2_
  48.9 3.4 %shard_map.44 = (bf16[512,640]{1,0:T(8,128)(2,1)S(1)}, bf16[512,512]{1,0:T(8,128)(2,1)S(1)}, bf16[1024,512]{1,0:T(8,128)(2,1)S(1)}) custom-call(s32[8]{0:T(128)S(1)} %stack.51.s, bf16[512,1152]{1,0:T(8,128)(2,1)S(1)} %shard_map.40.refs_0_, bf16[896,512]{1,0:T(8,128)(2,1)} %collective-permute-done.4.refs_1_, bf16[896,512]{1,0:T(8,128)(2,1)} %collective-permute-done.5.refs_2_), custom_call_target="tpu_custom_call" | custom-call | tf_op jit(solution)/shard_map/pallas_call | solution.py:42
  52.3 3.1 %collective-permute-done.6.refs_1_ = bf16[256,512]{1,0:T(8,128)(2,1)S(1)} collective-permute-done((bf16[256,512]{1,0:T(8,128)(2,1)S(1)}, bf16[256,512]{1,0:T(8,128)(2,1)S(1)}, u32[]{:S(2)}, u32[]{:S(2)}) %collective-permute-start.6) | collective-permute-done | bytes 262176 | tf_op jit(solution)/shard_map/ppermute | solution.py:489
  55.3 1.2 %shard_map.45 = (bf16[128,640]{1,0:T(8,128)(2,1)S(1)}, bf16[128,640]{1,0:T(8,128)(2,1)S(1)}) custom-call(s32[8]{0:T(128)S(1)} %stack.51.s, bf16[512,512]{1,0:T(8,128)(2,1)S(1)} %get-tuple-element.33.refs_0_, bf16[256,512]{1,0:T(8,128)(2,1)S(1)} %collective-permute-done.6.refs_1_), custom_call_target="tpu_custom_call" | custom-call | tf_op jit(solution)/shard_map/pallas_call | solution.py:42
  56.5 0.3 collective-permute-start.7
  56.8 3.4 %shard_map.46.refs_0_.fine = f32[512,640]{1,0:T(8,128)S(1)} custom-call(s32[8]{0:T(128)S(1)} %stack.51.s, bf16[512,1152]{1,0:T(8,128)(2,1)S(1)} %shard_map.40.refs_0_, bf16[512,640]{1,0:T(8,128)(2,1)S(1)} %get-tuple-element.31.refs_1_, bf16[1024,512]{1,0:T(8,128)(2,1)S(1)} %get-tuple-element.36.refs_2_), custom_call_target="tpu_custom_call" | custom-call | tf_op jit(solution)/shard_map/pallas_call | solution.py:42
  60.2 0.8 %collective-permute-done.7.refs_2_ = bf16[128,640]{1,0:T(8,128)(2,1)S(1)} collective-permute-done((bf16[128,640]{1,0:T(8,128)(2,1)S(1)}, bf16[128,640]{1,0:T(8,128)(2,1)S(1)}, u32[]{:S(2)}, u32[]{:S(2)}) %collective-permute-start.7) | collective-permute-done | bytes 163872 | tf_op jit(solution)/shard_map/ppermute | solution.py:489
  60.9 0.0 all-to-all-done.1.refs_3_
  60.9 2.2 %shard_map.47 = (bf16[256,512]{1,0:T(8,128)(2,1)S(1)}, bf16[64,640]{1,0:T(8,128)(2,1)S(1)}) custom-call(s32[8]{0:T(128)S(1)} %stack.51.s, f32[512,640]{1,0:T(8,128)S(1)} %shard_map.46.refs_0_.fine, bf16[128,640]{1,0:T(8,128)(2,1)S(1)} %get-tuple-element.37.refs_1_, bf16[128,640]{1,0:T(8,128)(2,1)S(1)} %collective-permute-done.7.refs_2_, ...), custom_call_target="tpu_custom_call" | custom-call | tf_op jit(solution)/shard_map/pallas_call | solution.py:42
  63.2 3.9 %collective-permute-start.8 = (bf16[256,512]{1,0:T(8,128)(2,1)S(1)}, bf16[256,512]{1,0:T(8,128)(2,1)S(1)}, u32[]{:S(2)}, u32[]{:S(2)}) collective-permute-start(bf16[256,512]{1,0:T(8,128)(2,1)S(1)} %get-tuple-element.38), channel_id=1, source_target_pairs={{0,1},{1,0},{2,3},{3,2},{4,5},{5,4},{6,7},{7,6},{8,9},{9,8},{10,11... | collective-permute-start | bytes 786440 | tf_op jit(solution)/shard_map/ppermute | solution.py:489
  67.1 1.9 %shard_map.48.part = bf16[256,1024]{1,0:T(8,128)(2,1)} custom-call(s32[8]{0:T(128)S(1)} %stack.51.s, f32[512,640]{1,0:T(8,128)S(1)} %shard_map.46.refs_0_.fine, bf16[64,640]{1,0:T(8,128)(2,1)S(1)} %get-tuple-element.40.kept), custom_call_target="tpu_custom_call" | custom-call | tf_op jit(solution)/shard_map/pallas_call | solution.py:430
  69.0 0.0 collective-permute-done.8.theirs
  69.1 1.3 %shard_map.49 = bf16[256,1024]{1,0:T(8,128)(2,1)} custom-call(s32[8]{0:T(128)S(1)} %stack.51.s, bf16[256,1024]{1,0:T(8,128)(2,1)} %shard_map.48.part, bf16[256,512]{1,0:T(8,128)(2,1)S(1)} %collective-permute-done.8.theirs), custom_call_target="tpu_custom_call", output_to_operand_aliasing={{}: (1, {})} | custom-call | tf_op jit(solution)/shard_map/pallas_call | solution.py:450
Async XLA Ops:
  0.0 3.0 %collective-permute-start = (bf16[256,1024]{1,0:T(8,128)(2,1)}, bf16[256,1024]{1,0:T(8,128)(2,1)S(1)}, u32[]{:S(2)}, u32[]{:S(2)}) collective-permute-start(bf16[256,1024]{1,0:T(8,128)(2,1)} %q.1), channel_id=1, source_target_pairs={{0,1},{1,0},{2,3},{3,2},{4,5},{5,4},{6,7},{7,6},{8,9},{9,8},{10,11... | collective-permute-start | bytes 1572872 | tf_op jit(solution)/shard_map/ppermute | solution.py:489
  0.7 2.5 %collective-permute-start.1 = (bf16[256,1024]{1,0:T(8,128)(2,1)}, bf16[256,1024]{1,0:T(8,128)(2,1)S(1)}, u32[]{:S(2)}, u32[]{:S(2)}) collective-permute-start(bf16[256,1024]{1,0:T(8,128)(2,1)} %k.1), channel_id=1, source_target_pairs={{0,1},{1,0},{2,3},{3,2},{4,5},{5,4},{6,7},{7,6},{8,9},{9,8},{10,11... | collective-permute-start | bytes 1572872 | tf_op jit(solution)/shard_map/ppermute | solution.py:489
  0.7 3.2 %collective-permute-start.2 = (bf16[256,1024]{1,0:T(8,128)(2,1)}, bf16[256,1024]{1,0:T(8,128)(2,1)S(1)}, u32[]{:S(2)}, u32[]{:S(2)}) collective-permute-start(bf16[256,1024]{1,0:T(8,128)(2,1)} %v.1), channel_id=1, source_target_pairs={{0,1},{1,0},{2,3},{3,2},{4,5},{5,4},{6,7},{7,6},{8,9},{9,8},{10,11... | collective-permute-start | bytes 1572872 | tf_op jit(solution)/shard_map/ppermute | solution.py:489
  5.6 24.6 %all-to-all-start = ((bf16[8,224,128]{2,1,0:T(8,128)(2,1)}), bf16[8,224,128]{2,1,0:T(8,128)(2,1)}, u32[]{:S(2)}, u32[]{:S(2)}) async-start(bf16[8,224,128]{2,1,0:T(8,128)(2,1)} %shard_map.38), calls=%async_computation | async-start | bytes 917504 | tf_op jit(solution)/shard_map/all_to_all | solution.py:497
  16.0 32.9 %collective-permute-start.4 = (bf16[896,512]{1,0:T(8,128)(2,1)}, bf16[896,512]{1,0:T(8,128)(2,1)}, u32[]{:S(2)}, u32[]{:S(2)}) collective-permute-start(bf16[896,512]{1,0:T(8,128)(2,1)} %get-tuple-element.24), channel_id=1, source_target_pairs={{0,2},{1,3},{2,4},{3,5},{4,6},{5,7},{6,8},{7,9},{8,10},{9,11},{10,... | collective-permute-start | bytes 2752520 | tf_op jit(solution)/shard_map/ppermute | solution.py:489
  19.4 29.5 %collective-permute-start.5 = (bf16[896,512]{1,0:T(8,128)(2,1)}, bf16[896,512]{1,0:T(8,128)(2,1)}, u32[]{:S(2)}, u32[]{:S(2)}) collective-permute-start(bf16[896,512]{1,0:T(8,128)(2,1)} %get-tuple-element.25), channel_id=1, source_target_pairs={{2,0},{3,1},{4,2},{5,3},{6,4},{7,5},{8,6},{9,7},{10,8},{11,9},{12,... | collective-permute-start | bytes 2752520 | tf_op jit(solution)/shard_map/ppermute | solution.py:489
  31.2 9.4 %collective-permute-start.3 = (bf16[1024,128]{1,0:T(8,128)(2,1)S(1)}, bf16[1024,128]{1,0:T(8,128)(2,1)S(1)}, u32[]{:S(2)}, u32[]{:S(2)}) collective-permute-start(bf16[1024,128]{1,0:T(8,128)(2,1)S(1)} %shard_map.41), channel_id=1, source_target_pairs={{8,24},{9,25},{10,26},{11,27},{12,28},{13,29},{14,30},{15,31},{16,... | collective-permute-start | bytes 786440 | tf_op jit(solution)/shard_map/ppermute | solution.py:489
  36.7 18.7 %collective-permute-start.6 = (bf16[256,512]{1,0:T(8,128)(2,1)S(1)}, bf16[256,512]{1,0:T(8,128)(2,1)S(1)}, u32[]{:S(2)}, u32[]{:S(2)}) collective-permute-start(bf16[256,512]{1,0:T(8,128)(2,1)S(1)} %shard_map.42), channel_id=1, source_target_pairs={{0,4},{1,5},{4,8},{5,9},{6,2},{7,3},{8,12},{9,13},{10,6},{11,7},{1... | collective-permute-start | bytes 786440 | tf_op jit(solution)/shard_map/ppermute | solution.py:489
  43.2 17.7 %all-to-all-start.1 = ((bf16[8,112,128]{2,1,0:T(8,128)(2,1)}), bf16[8,112,128]{2,1,0:T(8,128)(2,1)S(1)}, u32[]{:S(2)}, u32[]{:S(2)}) async-start(bf16[8,112,128]{2,1,0:T(8,128)(2,1)} %shard_map.43), calls=%async_computation.1 | async-start | bytes 458752 | tf_op jit(solution)/shard_map/all_to_all | solution.py:497
  56.5 4.4 %collective-permute-start.7 = (bf16[128,640]{1,0:T(8,128)(2,1)S(1)}, bf16[128,640]{1,0:T(8,128)(2,1)S(1)}, u32[]{:S(2)}, u32[]{:S(2)}) collective-permute-start(bf16[128,640]{1,0:T(8,128)(2,1)S(1)} %get-tuple-element.34), channel_id=1, source_target_pairs={{0,2},{1,3},{2,0},{3,1},{4,6},{5,7},{6,4},{7,5},{8,10},{9,11},{10,... | collective-permute-start | bytes 491528 | tf_op jit(solution)/shard_map/ppermute | solution.py:489
  63.2 5.9 %collective-permute-start.8 = (bf16[256,512]{1,0:T(8,128)(2,1)S(1)}, bf16[256,512]{1,0:T(8,128)(2,1)S(1)}, u32[]{:S(2)}, u32[]{:S(2)}) collective-permute-start(bf16[256,512]{1,0:T(8,128)(2,1)S(1)} %get-tuple-element.38), channel_id=1, source_target_pairs={{0,1},{1,0},{2,3},{3,2},{4,5},{5,4},{6,7},{7,6},{8,9},{9,8},{10,11... | collective-permute-start | bytes 786440 | tf_op jit(solution)/shard_map/ppermute | solution.py:489

commit v7 on v6

--- a/solution.py
+++ b/solution.py
@@ -110,8 +110,8 @@
     ]
     weights = [[jnp.exp2(s - m) for s in row] for row, m in zip(scores, tops)]
     totals = [
-        functools.reduce(jnp.add, [jnp.sum(w, axis=1, keepdims=True) for w in row]) * factor
-        for row in weights
+        functools.reduce(jnp.add, [jnp.sum(w, axis=1, keepdims=True) for w in row]) * f
+        for row, f in zip(weights, factor if isinstance(factor, tuple) else (factor,) * len(jobs))
     ]
     for (_, parts), row, m, total in zip(jobs, weights, tops, totals):
         out = None
@@ -356,12 +356,12 @@
         [ain[at + j, low : low + ROWS3] for j in range(HEADS)], axis=0
     )
     q4 = jnp.concatenate([ain[j, :ROWS4] for j in range(RING)], axis=0)
-    ((o4, value4),) = attend([(q4, [(xin[:B], xin[B : 2 * B], bias)])], 16.0)
+    job4 = (q4, [(xin[:B], xin[B : 2 * B], bias)])
     parts = [
         (rows3(mine, base), rows3(mine, base + ROWS3), None),
         (xin[2 * B : 3 * B], xin[3 * B :], bias),
     ]
-    ((o3, value3),) = attend([(rows3(other, base), parts)], 8.0)
+    (o4, value4), (o3, value3) = attend([job4, (rows3(other, base), parts)], (16.0, 8.0))
     row = lax.broadcasted_iota(jnp.int32, (ROWS4 + ROWS3, 128), 0)
     col = lax.broadcasted_iota(jnp.int32, (ROWS4 + ROWS3, 128), 1)
     term = lax.broadcasted_iota(jnp.int32, (16, 128), 0)

time: 71 us -> 71 us (level)
  no operation moved by 1% of the time
where the time goes in v7:
time: 71 us; the launch traced here: 70.5 us
  starting transfers between devices  33 us (46%)
  Pallas kernels  25.9 us (36%)
  waiting for transfers between devices  11.2 us (16%)
    ppermute x9, starting transfers between devices, send_to(): return lax.ppermute(x, 'seq', pairs)  21.4 us
    pallas_call x10, Pallas kernels, call(): pl.pallas_call(outer, out_shape=[pltpu.HBM(o.shape, o.dtype) for o in out...  21 us
    all_to_all x2, starting transfers between devices, line_swap(): return lax.all_to_all(x, 'seq', 0, 0, axis_index_groups=LINES)  11.6 us
    ppermute x9, waiting for transfers between devices, send_to(): return lax.ppermute(x, 'seq', pairs)  9.04 us
    all_to_all x2, waiting for transfers between devices, line_swap(): return lax.all_to_all(x, 'seq', 0, 0, axis_index_groups=LINES)  2.18 us
    pallas_call x1, Pallas kernels, own_columns(): pl.pallas_call(own_body, out_shape=shaped(B, 2 * COLS), in_specs=[pl.Bloc...  1.9 us
    pallas_call x1, Pallas kernels, half_columns(): pl.pallas_call(half_body, out_shape=shaped(3, B, COLS), in_specs=[pl.Bloc...  1.68 us
  transfers between devices with their start and end apart: 11, of which 7 were waited for; matrix products, arithmetic and copies ran while one was open for 0% of the time, Pallas kernels for 29%

profile of v7, /device:TPU:25, one launch (start us, length us, event | category | flops | bytes accessed | tf_op | source)
XLA Modules:
  0.0 70.5 jit_solution(1839571334223860623)
XLA Ops:
  0.0 0.7 collective-permute-start
  0.7 0.0 collective-permute-start.1
  0.7 0.5 collective-permute-start.2
  1.2 0.1 stack.51.s
  1.3 1.7 %shard_map.37.refs_0_ = bf16[3,256,512]{2,1,0:T(8,128)(2,1)S(1)} custom-call(s32[8]{0:T(128)S(1)} %stack.51.s, bf16[256,1024]{1,0:T(8,128)(2,1)} %q.1, bf16[256,1024]{1,0:T(8,128)(2,1)} %k.1, bf16[256,1024]{1,0:T(8,128)(2,1)} %v.1), custom_call_target="tpu_custom_call" | custom-call | tf_op jit(solution)/shard_map/pallas_call | solution.py:67
  3.0 0.0 collective-permute-done.refs_1_
  3.0 0.2 collective-permute-done.1.refs_2_.refs_1_
  3.2 0.7 %collective-permute-done.2.refs_3_.refs_2_ = bf16[256,1024]{1,0:T(8,128)(2,1)S(1)} collective-permute-done((bf16[256,1024]{1,0:T(8,128)(2,1)}, bf16[256,1024]{1,0:T(8,128)(2,1)S(1)}, u32[]{:S(2)}, u32[]{:S(2)}) %collective-permute-start.2) | collective-permute-done | bytes 524320 | tf_op jit(solution)/shard_map/ppermute | solution.py:489
  3.9 1.7 %shard_map.38 = bf16[8,224,128]{2,1,0:T(8,128)(2,1)} custom-call(s32[8]{0:T(128)S(1)} %stack.51.s, bf16[3,256,512]{2,1,0:T(8,128)(2,1)S(1)} %shard_map.37.refs_0_, bf16[256,1024]{1,0:T(8,128)(2,1)S(1)} %collective-permute-done.refs_1_, bf16[256,1024]{1,0:T(8,128)(2,1)S(1)} %collective-permute-done.1.refs_2_.refs_1_, ...), custom_call_target="tpu_custom_call" | custom-call | tf_op jit(solution)/shard_map/pallas_call | solution.py:42
  5.6 8.2 %all-to-all-start = ((bf16[8,224,128]{2,1,0:T(8,128)(2,1)}), bf16[8,224,128]{2,1,0:T(8,128)(2,1)}, u32[]{:S(2)}, u32[]{:S(2)}) async-start(bf16[8,224,128]{2,1,0:T(8,128)(2,1)} %shard_map.38), calls=%async_computation | async-start | bytes 917504 | tf_op jit(solution)/shard_map/all_to_all | solution.py:497
  13.8 2.2 %shard_map.39 = (bf16[896,512]{1,0:T(8,128)(2,1)}, bf16[896,512]{1,0:T(8,128)(2,1)}) custom-call(s32[8]{0:T(128)S(1)} %stack.51.s, bf16[3,256,512]{2,1,0:T(8,128)(2,1)S(1)} %shard_map.37.refs_0_, bf16[256,1024]{1,0:T(8,128)(2,1)S(1)} %collective-permute-done.refs_1_, bf16[256,1024]{1,0:T(8,128)(2,1)S(1)} %collective-permute-done.1.refs_2_.refs_1_, ...), custom_call_target="tpu_custom_call" | custom-call | tf_op jit(solution)/shard_map/pallas_call | solution.py:42
  16.0 3.4 %collective-permute-start.4 = (bf16[896,512]{1,0:T(8,128)(2,1)}, bf16[896,512]{1,0:T(8,128)(2,1)}, u32[]{:S(2)}, u32[]{:S(2)}) collective-permute-start(bf16[896,512]{1,0:T(8,128)(2,1)} %get-tuple-element.24), channel_id=1, source_target_pairs={{0,2},{1,3},{2,4},{3,5},{4,6},{5,7},{6,8},{7,9},{8,10},{9,11},{10,... | collective-permute-start | bytes 2752520 | tf_op jit(solution)/shard_map/ppermute | solution.py:489
  19.4 6.1 %collective-permute-start.5 = (bf16[896,512]{1,0:T(8,128)(2,1)}, bf16[896,512]{1,0:T(8,128)(2,1)}, u32[]{:S(2)}, u32[]{:S(2)}) collective-permute-start(bf16[896,512]{1,0:T(8,128)(2,1)} %get-tuple-element.25), channel_id=1, source_target_pairs={{2,0},{3,1},{4,2},{5,3},{6,4},{7,5},{8,6},{9,7},{10,8},{11,9},{12,... | collective-permute-start | bytes 2752520 | tf_op jit(solution)/shard_map/ppermute | solution.py:489
  25.5 2.5 %shard_map.40.refs_0_ = bf16[512,1152]{1,0:T(8,128)(2,1)S(1)} custom-call(s32[8]{0:T(128)S(1)} %stack.51.s, bf16[3,256,512]{2,1,0:T(8,128)(2,1)S(1)} %shard_map.37.refs_0_, bf16[256,1024]{1,0:T(8,128)(2,1)S(1)} %collective-permute-done.refs_1_, bf16[256,1024]{1,0:T(8,128)(2,1)S(1)} %collective-permute-done.1.refs_2_.refs_1_, ...), custom_call_target="tpu_custom_call" | custom-call | tf_op jit(solution)/shard_map/pallas_call | solution.py:42
  28.0 2.2 %all-to-all-done.refs_0_ = bf16[8,224,128]{2,1,0:T(8,128)(2,1)} async-done(((bf16[8,224,128]{2,1,0:T(8,128)(2,1)}), bf16[8,224,128]{2,1,0:T(8,128)(2,1)}, u32[]{:S(2)}, u32[]{:S(2)}) %all-to-all-start) | async-done | bytes 458784 | tf_op jit(solution)/shard_map/all_to_all | solution.py:497
  30.2 1.0 %shard_map.41 = bf16[1024,128]{1,0:T(8,128)(2,1)S(1)} custom-call(s32[8]{0:T(128)S(1)} %stack.51.s, bf16[8,224,128]{2,1,0:T(8,128)(2,1)} %all-to-all-done.refs_0_), custom_call_target="tpu_custom_call" | custom-call | tf_op jit(solution)/shard_map/pallas_call | solution.py:42
  31.2 4.6 %collective-permute-start.3 = (bf16[1024,128]{1,0:T(8,128)(2,1)S(1)}, bf16[1024,128]{1,0:T(8,128)(2,1)S(1)}, u32[]{:S(2)}, u32[]{:S(2)}) collective-permute-start(bf16[1024,128]{1,0:T(8,128)(2,1)S(1)} %shard_map.41), channel_id=1, source_target_pairs={{8,24},{9,25},{10,26},{11,27},{12,28},{13,29},{14,30},{15,31},{16,... | collective-permute-start | bytes 786440 | tf_op jit(solution)/shard_map/ppermute | solution.py:489
  35.8 0.8 %shard_map.42 = bf16[256,512]{1,0:T(8,128)(2,1)S(1)} custom-call(s32[8]{0:T(128)S(1)} %stack.51.s, bf16[3,256,512]{2,1,0:T(8,128)(2,1)S(1)} %shard_map.37.refs_0_, bf16[256,1024]{1,0:T(8,128)(2,1)S(1)} %collective-permute-done.1.refs_2_.refs_1_, bf16[256,1024]{1,0:T(8,128)(2,1)S(1)} %collective-permute-done.2.refs_3_.refs_2_), custom_call_target="tpu_custom_call" | custom-call | tf_op jit(solution)/shard_map/pallas_call | solution.py:42
  36.7 1.9 %collective-permute-start.6 = (bf16[256,512]{1,0:T(8,128)(2,1)S(1)}, bf16[256,512]{1,0:T(8,128)(2,1)S(1)}, u32[]{:S(2)}, u32[]{:S(2)}) collective-permute-start(bf16[256,512]{1,0:T(8,128)(2,1)S(1)} %shard_map.42), channel_id=1, source_target_pairs={{0,4},{1,5},{4,8},{5,9},{6,2},{7,3},{8,12},{9,13},{10,6},{11,7},{1... | collective-permute-start | bytes 786440 | tf_op jit(solution)/shard_map/ppermute | solution.py:489
  38.6 2.1 %collective-permute-done.3.refs_1_ = bf16[1024,128]{1,0:T(8,128)(2,1)S(1)} collective-permute-done((bf16[1024,128]{1,0:T(8,128)(2,1)S(1)}, bf16[1024,128]{1,0:T(8,128)(2,1)S(1)}, u32[]{:S(2)}, u32[]{:S(2)}) %collective-permute-start.3) | collective-permute-done | bytes 262176 | tf_op jit(solution)/shard_map/ppermute | solution.py:489
  40.6 2.7 %shard_map.43 = bf16[8,112,128]{2,1,0:T(8,128)(2,1)} custom-call(s32[8]{0:T(128)S(1)} %stack.51.s, bf16[8,224,128]{2,1,0:T(8,128)(2,1)} %all-to-all-done.refs_0_, bf16[1024,128]{1,0:T(8,128)(2,1)S(1)} %collective-permute-done.3.refs_1_), custom_call_target="tpu_custom_call" | custom-call | tf_op jit(solution)/shard_map/pallas_call | solution.py:42
  43.3 3.4 %all-to-all-start.1 = ((bf16[8,112,128]{2,1,0:T(8,128)(2,1)}), bf16[8,112,128]{2,1,0:T(8,128)(2,1)S(1)}, u32[]{:S(2)}, u32[]{:S(2)}) async-start(bf16[8,112,128]{2,1,0:T(8,128)(2,1)} %shard_map.43), calls=%async_computation.1 | async-start | bytes 458752 | tf_op jit(solution)/shard_map/all_to_all | solution.py:497
  46.7 2.2 %collective-permute-done.4.refs_1_ = bf16[896,512]{1,0:T(8,128)(2,1)} collective-permute-done((bf16[896,512]{1,0:T(8,128)(2,1)}, bf16[896,512]{1,0:T(8,128)(2,1)}, u32[]{:S(2)}, u32[]{:S(2)}) %collective-permute-start.4) | collective-permute-done | bytes 917536 | tf_op jit(solution)/shard_map/ppermute | solution.py:489
  48.9 0.0 collective-permute-done.5.refs_2_
  48.9 3.4 %shard_map.44 = (bf16[512,640]{1,0:T(8,128)(2,1)S(1)}, bf16[512,512]{1,0:T(8,128)(2,1)S(1)}, bf16[1024,512]{1,0:T(8,128)(2,1)S(1)}) custom-call(s32[8]{0:T(128)S(1)} %stack.51.s, bf16[512,1152]{1,0:T(8,128)(2,1)S(1)} %shard_map.40.refs_0_, bf16[896,512]{1,0:T(8,128)(2,1)} %collective-permute-done.4.refs_1_, bf16[896,512]{1,0:T(8,128)(2,1)} %collective-permute-done.5.refs_2_), custom_call_target="tpu_custom_call" | custom-call | tf_op jit(solution)/shard_map/pallas_call | solution.py:42
  52.3 3.1 %collective-permute-done.6.refs_1_ = bf16[256,512]{1,0:T(8,128)(2,1)S(1)} collective-permute-done((bf16[256,512]{1,0:T(8,128)(2,1)S(1)}, bf16[256,512]{1,0:T(8,128)(2,1)S(1)}, u32[]{:S(2)}, u32[]{:S(2)}) %collective-permute-start.6) | collective-permute-done | bytes 262176 | tf_op jit(solution)/shard_map/ppermute | solution.py:489
  55.3 1.2 %shard_map.45 = (bf16[128,640]{1,0:T(8,128)(2,1)S(1)}, bf16[128,640]{1,0:T(8,128)(2,1)S(1)}) custom-call(s32[8]{0:T(128)S(1)} %stack.51.s, bf16[512,512]{1,0:T(8,128)(2,1)S(1)} %get-tuple-element.33.refs_0_, bf16[256,512]{1,0:T(8,128)(2,1)S(1)} %collective-permute-done.6.refs_1_), custom_call_target="tpu_custom_call" | custom-call | tf_op jit(solution)/shard_map/pallas_call | solution.py:42
  56.5 0.3 collective-permute-start.7
  56.8 3.4 %shard_map.46.refs_0_.fine = f32[512,640]{1,0:T(8,128)S(1)} custom-call(s32[8]{0:T(128)S(1)} %stack.51.s, bf16[512,1152]{1,0:T(8,128)(2,1)S(1)} %shard_map.40.refs_0_, bf16[512,640]{1,0:T(8,128)(2,1)S(1)} %get-tuple-element.31.refs_1_, bf16[1024,512]{1,0:T(8,128)(2,1)S(1)} %get-tuple-element.36.refs_2_), custom_call_target="tpu_custom_call" | custom-call | tf_op jit(solution)/shard_map/pallas_call | solution.py:42
  60.2 0.8 %collective-permute-done.7.refs_2_ = bf16[128,640]{1,0:T(8,128)(2,1)S(1)} collective-permute-done((bf16[128,640]{1,0:T(8,128)(2,1)S(1)}, bf16[128,640]{1,0:T(8,128)(2,1)S(1)}, u32[]{:S(2)}, u32[]{:S(2)}) %collective-permute-start.7) | collective-permute-done | bytes 163872 | tf_op jit(solution)/shard_map/ppermute | solution.py:489
  60.9 0.0 all-to-all-done.1.refs_3_
  60.9 2.2 %shard_map.47 = (bf16[256,512]{1,0:T(8,128)(2,1)S(1)}, bf16[64,640]{1,0:T(8,128)(2,1)S(1)}) custom-call(s32[8]{0:T(128)S(1)} %stack.51.s, f32[512,640]{1,0:T(8,128)S(1)} %shard_map.46.refs_0_.fine, bf16[128,640]{1,0:T(8,128)(2,1)S(1)} %get-tuple-element.37.refs_1_, bf16[128,640]{1,0:T(8,128)(2,1)S(1)} %collective-permute-done.7.refs_2_, ...), custom_call_target="tpu_custom_call" | custom-call | tf_op jit(solution)/shard_map/pallas_call | solution.py:42
  63.2 3.9 %collective-permute-start.8 = (bf16[256,512]{1,0:T(8,128)(2,1)S(1)}, bf16[256,512]{1,0:T(8,128)(2,1)S(1)}, u32[]{:S(2)}, u32[]{:S(2)}) collective-permute-start(bf16[256,512]{1,0:T(8,128)(2,1)S(1)} %get-tuple-element.38), channel_id=1, source_target_pairs={{0,1},{1,0},{2,3},{3,2},{4,5},{5,4},{6,7},{7,6},{8,9},{9,8},{10,11... | collective-permute-start | bytes 786440 | tf_op jit(solution)/shard_map/ppermute | solution.py:489
  67.1 1.9 %shard_map.48.part = bf16[256,1024]{1,0:T(8,128)(2,1)} custom-call(s32[8]{0:T(128)S(1)} %stack.51.s, f32[512,640]{1,0:T(8,128)S(1)} %shard_map.46.refs_0_.fine, bf16[64,640]{1,0:T(8,128)(2,1)S(1)} %get-tuple-element.40.kept), custom_call_target="tpu_custom_call" | custom-call | tf_op jit(solution)/shard_map/pallas_call | solution.py:430
  69.0 0.0 collective-permute-done.8.theirs
  69.1 1.3 %shard_map.49 = bf16[256,1024]{1,0:T(8,128)(2,1)} custom-call(s32[8]{0:T(128)S(1)} %stack.51.s, bf16[256,1024]{1,0:T(8,128)(2,1)} %shard_map.48.part, bf16[256,512]{1,0:T(8,128)(2,1)S(1)} %collective-permute-done.8.theirs), custom_call_target="tpu_custom_call", output_to_operand_aliasing={{}: (1, {})} | custom-call | tf_op jit(solution)/shard_map/pallas_call | solution.py:450
Async XLA Ops:
  0.0 3.0 %collective-permute-start = (bf16[256,1024]{1,0:T(8,128)(2,1)}, bf16[256,1024]{1,0:T(8,128)(2,1)S(1)}, u32[]{:S(2)}, u32[]{:S(2)}) collective-permute-start(bf16[256,1024]{1,0:T(8,128)(2,1)} %q.1), channel_id=1, source_target_pairs={{0,1},{1,0},{2,3},{3,2},{4,5},{5,4},{6,7},{7,6},{8,9},{9,8},{10,11... | collective-permute-start | bytes 1572872 | tf_op jit(solution)/shard_map/ppermute | solution.py:489
  0.7 2.5 %collective-permute-start.1 = (bf16[256,1024]{1,0:T(8,128)(2,1)}, bf16[256,1024]{1,0:T(8,128)(2,1)S(1)}, u32[]{:S(2)}, u32[]{:S(2)}) collective-permute-start(bf16[256,1024]{1,0:T(8,128)(2,1)} %k.1), channel_id=1, source_target_pairs={{0,1},{1,0},{2,3},{3,2},{4,5},{5,4},{6,7},{7,6},{8,9},{9,8},{10,11... | collective-permute-start | bytes 1572872 | tf_op jit(solution)/shard_map/ppermute | solution.py:489
  0.7 3.2 %collective-permute-start.2 = (bf16[256,1024]{1,0:T(8,128)(2,1)}, bf16[256,1024]{1,0:T(8,128)(2,1)S(1)}, u32[]{:S(2)}, u32[]{:S(2)}) collective-permute-start(bf16[256,1024]{1,0:T(8,128)(2,1)} %v.1), channel_id=1, source_target_pairs={{0,1},{1,0},{2,3},{3,2},{4,5},{5,4},{6,7},{7,6},{8,9},{9,8},{10,11... | collective-permute-start | bytes 1572872 | tf_op jit(solution)/shard_map/ppermute | solution.py:489
  5.6 24.6 %all-to-all-start = ((bf16[8,224,128]{2,1,0:T(8,128)(2,1)}), bf16[8,224,128]{2,1,0:T(8,128)(2,1)}, u32[]{:S(2)}, u32[]{:S(2)}) async-start(bf16[8,224,128]{2,1,0:T(8,128)(2,1)} %shard_map.38), calls=%async_computation | async-start | bytes 917504 | tf_op jit(solution)/shard_map/all_to_all | solution.py:497
  16.0 32.9 %collective-permute-start.4 = (bf16[896,512]{1,0:T(8,128)(2,1)}, bf16[896,512]{1,0:T(8,128)(2,1)}, u32[]{:S(2)}, u32[]{:S(2)}) collective-permute-start(bf16[896,512]{1,0:T(8,128)(2,1)} %get-tuple-element.24), channel_id=1, source_target_pairs={{0,2},{1,3},{2,4},{3,5},{4,6},{5,7},{6,8},{7,9},{8,10},{9,11},{10,... | collective-permute-start | bytes 2752520 | tf_op jit(solution)/shard_map/ppermute | solution.py:489
  19.4 29.5 %collective-permute-start.5 = (bf16[896,512]{1,0:T(8,128)(2,1)}, bf16[896,512]{1,0:T(8,128)(2,1)}, u32[]{:S(2)}, u32[]{:S(2)}) collective-permute-start(bf16[896,512]{1,0:T(8,128)(2,1)} %get-tuple-element.25), channel_id=1, source_target_pairs={{2,0},{3,1},{4,2},{5,3},{6,4},{7,5},{8,6},{9,7},{10,8},{11,9},{12,... | collective-permute-start | bytes 2752520 | tf_op jit(solution)/shard_map/ppermute | solution.py:489
  31.2 9.4 %collective-permute-start.3 = (bf16[1024,128]{1,0:T(8,128)(2,1)S(1)}, bf16[1024,128]{1,0:T(8,128)(2,1)S(1)}, u32[]{:S(2)}, u32[]{:S(2)}) collective-permute-start(bf16[1024,128]{1,0:T(8,128)(2,1)S(1)} %shard_map.41), channel_id=1, source_target_pairs={{8,24},{9,25},{10,26},{11,27},{12,28},{13,29},{14,30},{15,31},{16,... | collective-permute-start | bytes 786440 | tf_op jit(solution)/shard_map/ppermute | solution.py:489
  36.7 18.7 %collective-permute-start.6 = (bf16[256,512]{1,0:T(8,128)(2,1)S(1)}, bf16[256,512]{1,0:T(8,128)(2,1)S(1)}, u32[]{:S(2)}, u32[]{:S(2)}) collective-permute-start(bf16[256,512]{1,0:T(8,128)(2,1)S(1)} %shard_map.42), channel_id=1, source_target_pairs={{0,4},{1,5},{4,8},{5,9},{6,2},{7,3},{8,12},{9,13},{10,6},{11,7},{1... | collective-permute-start | bytes 786440 | tf_op jit(solution)/shard_map/ppermute | solution.py:489
  43.3 17.6 %all-to-all-start.1 = ((bf16[8,112,128]{2,1,0:T(8,128)(2,1)}), bf16[8,112,128]{2,1,0:T(8,128)(2,1)S(1)}, u32[]{:S(2)}, u32[]{:S(2)}) async-start(bf16[8,112,128]{2,1,0:T(8,128)(2,1)} %shard_map.43), calls=%async_computation.1 | async-start | bytes 458752 | tf_op jit(solution)/shard_map/all_to_all | solution.py:497
  56.5 4.4 %collective-permute-start.7 = (bf16[128,640]{1,0:T(8,128)(2,1)S(1)}, bf16[128,640]{1,0:T(8,128)(2,1)S(1)}, u32[]{:S(2)}, u32[]{:S(2)}) collective-permute-start(bf16[128,640]{1,0:T(8,128)(2,1)S(1)} %get-tuple-element.34), channel_id=1, source_target_pairs={{0,2},{1,3},{2,0},{3,1},{4,6},{5,7},{6,4},{7,5},{8,10},{9,11},{10,... | collective-permute-start | bytes 491528 | tf_op jit(solution)/shard_map/ppermute | solution.py:489
  63.2 5.9 %collective-permute-start.8 = (bf16[256,512]{1,0:T(8,128)(2,1)S(1)}, bf16[256,512]{1,0:T(8,128)(2,1)S(1)}, u32[]{:S(2)}, u32[]{:S(2)}) collective-permute-start(bf16[256,512]{1,0:T(8,128)(2,1)S(1)} %get-tuple-element.38), channel_id=1, source_target_pairs={{0,1},{1,0},{2,3},{3,2},{4,5},{5,4},{6,7},{7,6},{8,9},{9,8},{10,11... | collective-permute-start | bytes 786440 | tf_op jit(solution)/shard_map/ppermute | solution.py:489
